TPU v7x, 128 devices: a whole 4x4x4 slice. The times are simulated.
128 devices in a mesh: section: 2 (over y_hi), dp: 64 (over x, y_lo, z, core).
Axes of the slice: x: 4, y: 4 (y_hi: 2, y_lo: 2; y = y_hi * 2 + y_lo), z: 4, core: 2. Of those that a mesh axis runs over, the one named last changes fastest.
Arguments:
- block_input: bfloat16 [4, 2048, 2048], P(None, 'dp'), may hold values from -16 to 16
- segment_ids: int32 [4, 2048], P(None, 'dp'), may hold values from 0 to 31, as said below
- cotangent: bfloat16 [4, 2048, 2048], P(None, 'dp'), may hold values from -16 to 16
- first_gain: bfloat16 [2, 2048], P('section', 'dp'), may hold values from 0.25 to 1.75
- first_shift: bfloat16 [2, 2048], P('section', 'dp'), may hold values from -3 to 3
- qkv_weight: bfloat16 [2, 2048, 6144], P('section', 'dp'), may hold values from -0.125 to 0.125
- qkv_bias: bfloat16 [2, 6144], P('section', 'dp'), may hold values from -3 to 3
- out_weight: bfloat16 [2, 2048, 2048], P('section', 'dp'), may hold values from -0.25 to 0.25
- second_gain: bfloat16 [2, 2048], P('section', 'dp'), may hold values from 0.25 to 1.75
- second_shift: bfloat16 [2, 2048], P('section', 'dp'), may hold values from -3 to 3
- gate_up: bfloat16 [2, 2048, 11264], P('section', 'dp'), may hold values from -0.125 to 0.125
- down_weight: bfloat16 [2, 5632, 2048], P('section', 'dp'), may hold values from -0.078125 to 0.078125
Outputs:
- activations: bfloat16 [2, 4, 2048, 2048], P('section', None, 'dp')
- input_grads: float32 [2, 4, 2048, 2048], P('section', None, 'dp')
- first_gain_grad: float32 [2, 2048], P('section', 'dp')
- first_shift_grad: float32 [2, 2048], P('section', 'dp')
- qkv_weight_grad: float32 [2, 2048, 6144], P('section', 'dp')
- qkv_bias_grad: float32 [2, 6144], P('section', 'dp')
- out_weight_grad: float32 [2, 2048, 2048], P('section', 'dp')
- second_gain_grad: float32 [2, 2048], P('section', 'dp')
- second_shift_grad: float32 [2, 2048], P('section', 'dp')
- gate_up_grad: float32 [2, 2048, 11264], P('section', 'dp')
- down_weight_grad: float32 [2, 5632, 2048], P('section', 'dp')
Inputs may be any that keep to these rules, and one draw needn't show every extreme that they name: `segment_ids`: within each aligned block of 32 rows (one dp index of one micro-batch) the ids start at 0 and rise by 0 or 1 from row to row, so each sequence is a run of rows; in some block one sequence fills all 32 rows, in another every row is a sequence of its own.
All inputs are finite; a program needn't handle non-finite values.
Results may differ from a plain program's by a relative error of at most 0.017.
Values may be sent and summed in bfloat16 or wider, within the bound.
No kernel may reach another device: no remote copies, remote signals or barrier semaphores. Data moves between devices by JAX's collectives and lax.ppermute only.
A program may use at most 576 MiB of HBM per device.

v0:
```python
import math

import jax
import jax.numpy as jnp
from jax import lax
from jax.sharding import PartitionSpec as P

HEAD_DIM = 64
ROT = 16
FF = 5632


EPSILON = 1e-05
NEG_FILL = -1e30


def sent_together(arrays, axis, dim, along):
    widths = [math.prod(a.shape[along:]) for a in arrays]
    both = jnp.concatenate(
        [a.reshape(*a.shape[:along], w) for a, w in zip(arrays, widths)], axis=along
    )
    out = lax.all_gather(both, axis, axis=dim, tiled=True)
    blocks = jnp.split(out, [sum(widths[:k]) for k in range(1, len(widths))], axis=along)
    return tuple((b.reshape(*out.shape[:along], *a.shape[along:]) for a, b in zip(arrays, blocks)))


def from_behind(block, axis, distance):
    devices = range(lax.axis_size(axis))
    route = [(i - distance, i) for i in devices if i - distance in devices]
    return lax.ppermute(block, axis, route)


def in_one_piece(arrays, axis, dim, along):
    widths = [math.prod(a.shape[along:]) for a in arrays]
    both = jnp.concatenate(
        [a.reshape(*a.shape[:along], w) for a, w in zip(arrays, widths)], axis=along
    )
    out = lax.psum_scatter(both, axis, scatter_dimension=dim, tiled=True)
    blocks = jnp.split(out, [sum(widths[:k]) for k in range(1, len(widths))], axis=along)
    return tuple((b.reshape(*out.shape[:along], *a.shape[along:]) for a, b in zip(arrays, blocks)))


def geometry(segments):
    count = segments.shape[-1]
    index = jnp.arange(count, dtype=jnp.int32)
    same = segments[..., :, None] == segments[..., None, :]
    before = index[None, :] < index[:, None]
    places = jnp.sum(jnp.where(same & before, 1.0, 0.0), axis=-1).astype(jnp.float32)
    inverse = 10000.0 ** (-(jnp.arange(ROT // 2).astype(jnp.float32) * 2.0 / ROT))
    theta = places[..., None] * inverse
    allowed = same & (index[None, :] <= index[:, None])
    return (jnp.cos(theta)[..., None, :], jnp.sin(theta)[..., None, :], allowed)


def turn(values, cosine, sine):
    half = ROT // 2
    first = values[..., :half]
    second = values[..., half:ROT]
    return jnp.concatenate(
        [first * cosine - second * sine, second * cosine + first * sine, values[..., ROT:]], axis=-1
    )


def normalize(values, gain, shift):
    mean = jnp.mean(values, axis=-1, keepdims=True)
    centred = values - mean
    scale = lax.rsqrt(jnp.mean(centred * centred, axis=-1, keepdims=True) + EPSILON)
    unit = centred * scale
    return (unit * gain + shift, unit, scale)


def normalize_back(grad_out, unit, scale, gain):
    grad_unit = grad_out * gain
    return scale * (
        grad_unit
        - jnp.mean(grad_unit, axis=-1, keepdims=True)
        - unit * jnp.mean(grad_unit * unit, axis=-1, keepdims=True)
    )


def attention_scores(queries, key_rows, allowed):
    scores = jnp.einsum(
        "qhd,khd->hqk", queries, key_rows, preferred_element_type=jnp.float32
    ) * HEAD_DIM ** (-0.5)
    return jnp.where(allowed[None], scores, NEG_FILL)


def forward_layer(layer_in, segments, weights):
    (
        first_gain,
        first_shift,
        qkv_weight,
        qkv_bias,
        out_weight,
        second_gain,
        second_shift,
        gate_up,
        down_weight,
    ) = weights
    rows, width = layer_in.shape
    cosine, sine, allowed = geometry(segments)
    inputs = layer_in.astype(jnp.float32)
    normed, unit_one, scale_one = normalize(
        inputs, first_gain.astype(jnp.float32), first_shift.astype(jnp.float32)
    )
    normed_low = normed.astype(jnp.bfloat16)
    projected = jnp.dot(
        normed_low, qkv_weight, preferred_element_type=jnp.float32
    ) + qkv_bias.astype(jnp.float32)
    projected = projected.reshape(rows, 3, width // HEAD_DIM, HEAD_DIM)
    queries = turn(projected[:, 0], cosine, sine).astype(jnp.bfloat16)
    key_rows = turn(projected[:, 1], cosine, sine).astype(jnp.bfloat16)
    value_rows = projected[:, 2].astype(jnp.bfloat16)
    scores = attention_scores(queries, key_rows, allowed)
    top = jnp.max(scores, axis=-1, keepdims=True)
    spread = jnp.exp(scores - top)
    total = jnp.sum(spread, axis=-1, keepdims=True)
    probs = spread / total
    logsum = (top + jnp.log(total))[:, :, 0]
    mixed = jnp.einsum(
        "hqk,khd->qhd", probs.astype(jnp.bfloat16), value_rows, preferred_element_type=jnp.float32
    )
    mixed_low = mixed.reshape(rows, width).astype(jnp.bfloat16)
    hidden = inputs + jnp.dot(mixed_low, out_weight, preferred_element_type=jnp.float32)
    normed_two, unit_two, scale_two = normalize(
        hidden, second_gain.astype(jnp.float32), second_shift.astype(jnp.float32)
    )
    normed_two_low = normed_two.astype(jnp.bfloat16)
    gate_up_out = jnp.dot(normed_two_low, gate_up, preferred_element_type=jnp.float32)
    gate_part = gate_up_out[:, :FF]
    activated = (gate_part * jax.nn.sigmoid(gate_part) * gate_up_out[:, FF:]).astype(jnp.bfloat16)
    result = hidden + jnp.dot(activated, down_weight, preferred_element_type=jnp.float32)
    kept = (
        segments,
        unit_one,
        scale_one,
        normed_low,
        queries,
        key_rows,
        value_rows,
        logsum,
        mixed_low,
        unit_two,
        scale_two,
        normed_two_low,
        gate_up_out,
        activated,
    )
    return (result, kept)


def backward_layer(grad_in, kept, weights):
    (
        first_gain,
        first_shift,
        qkv_weight,
        qkv_bias,
        out_weight,
        second_gain,
        second_shift,
        gate_up,
        down_weight,
    ) = weights
    (
        segments,
        unit_one,
        scale_one,
        normed_low,
        queries,
        key_rows,
        value_rows,
        logsum,
        mixed_low,
        unit_two,
        scale_two,
        normed_two_low,
        gate_up_out,
        activated,
    ) = kept
    rows, width = grad_in.shape
    cosine, sine, allowed = geometry(segments)
    across = (((1,), (1,)), ((), ()))
    grad_mlp_low = grad_in.astype(jnp.bfloat16)
    grad_act = lax.dot_general(
        grad_mlp_low, down_weight, across, preferred_element_type=jnp.float32
    )
    gate_part = gate_up_out[:, :FF]
    up_part = gate_up_out[:, FF:]
    sigma = jax.nn.sigmoid(gate_part)
    grad_gate = grad_act * up_part * sigma * (1.0 + gate_part * (1.0 - sigma))
    grad_up = grad_act * gate_part * sigma
    grad_gu_low = jnp.concatenate([grad_gate, grad_up], axis=1).astype(jnp.bfloat16)
    grad_normed_two = lax.dot_general(
        grad_gu_low, gate_up, across, preferred_element_type=jnp.float32
    )
    grad_hidden = grad_in + normalize_back(
        grad_normed_two, unit_two, scale_two, second_gain.astype(jnp.float32)
    )
    grad_attn_low = grad_hidden.astype(jnp.bfloat16)
    grad_mixed = lax.dot_general(
        grad_attn_low, out_weight, across, preferred_element_type=jnp.float32
    )
    grad_mixed = grad_mixed.astype(jnp.bfloat16).reshape(rows, width // HEAD_DIM, HEAD_DIM)
    scores = attention_scores(queries, key_rows, allowed)
    probs = jnp.exp(scores - logsum[:, :, None])
    grad_values = jnp.einsum(
        "hqk,qhd->khd", probs.astype(jnp.bfloat16), grad_mixed, preferred_element_type=jnp.float32
    )
    grad_probs = jnp.einsum(
        "qhd,khd->hqk", grad_mixed, value_rows, preferred_element_type=jnp.float32
    )
    grad_scores = probs * (grad_probs - jnp.sum(probs * grad_probs, axis=-1, keepdims=True))
    grad_scores = jnp.where(allowed[None], grad_scores, 0.0).astype(jnp.bfloat16)
    factor = HEAD_DIM ** (-0.5)
    grad_queries = (
        jnp.einsum("hqk,khd->qhd", grad_scores, key_rows, preferred_element_type=jnp.float32)
        * factor
    )
    grad_keys = (
        jnp.einsum("hqk,qhd->khd", grad_scores, queries, preferred_element_type=jnp.float32)
        * factor
    )
    grad_projected = jnp.stack(
        [turn(grad_queries, cosine, -sine), turn(grad_keys, cosine, -sine), grad_values], axis=1
    )
    grad_projected = grad_projected.reshape(rows, 3 * width).astype(jnp.bfloat16)
    grad_normed = lax.dot_general(
        grad_projected, qkv_weight, across, preferred_element_type=jnp.float32
    )
    grad_rows = grad_hidden + normalize_back(
        grad_normed, unit_one, scale_one, first_gain.astype(jnp.float32)
    )
    parts = (
        normed_low,
        grad_projected,
        mixed_low,
        grad_attn_low,
        normed_two_low,
        grad_gu_low,
        activated,
        grad_mlp_low,
        jnp.sum(grad_normed * unit_one, axis=0),
        jnp.sum(grad_normed, axis=0),
        jnp.sum(grad_normed_two * unit_two, axis=0),
        jnp.sum(grad_normed_two, axis=0),
    )
    return (grad_rows, parts)


def outer(left, right):
    return lax.dot_general(
        left.reshape(-1, left.shape[-1]),
        right.reshape(-1, right.shape[-1]),
        (((0,), (0,)), ((), ())),
        preferred_element_type=jnp.float32,
    )


def on_device(
    block_input,
    segment_ids,
    cotangent,
    first_gain,
    first_shift,
    qkv_weight,
    qkv_bias,
    out_weight,
    second_gain,
    second_shift,
    gate_up,
    down_weight,
):
    section = lax.axis_index("section")
    micro = block_input.shape[0]
    shards = (
        first_gain,
        first_shift,
        qkv_weight,
        qkv_bias,
        out_weight,
        second_gain,
        second_shift,
        gate_up,
        down_weight,
    )
    gathered = (
        *sent_together((shards[0], shards[1], shards[2]), "dp", 1, 2),
        lax.all_gather(shards[3], "dp", axis=1, tiled=True),
        *sent_together((shards[4], shards[5], shards[6], shards[7]), "dp", 1, 2),
        lax.all_gather(shards[8], "dp", axis=1, tiled=True),
    )
    forward_weights = tuple((piece[0] for piece in gathered))
    received = jnp.zeros(block_input.shape[1:], jnp.bfloat16)
    results = []
    stored = []
    for tick_index in range(micro + 1):
        own_rows = block_input[min(tick_index, micro - 1)]
        layer_in = jnp.where(section == 0, own_rows, received)
        batch_index = jnp.clip(tick_index - section, 0, micro - 1)
        segments = lax.dynamic_index_in_dim(segment_ids, batch_index, 0, keepdims=False)
        result, kept = forward_layer(layer_in, segments, forward_weights)
        results.append(result.astype(jnp.bfloat16))
        stored.append(kept)
        if tick_index < micro:
            received = from_behind(results[-1], "section", 1)
    activations = lax.dynamic_slice_in_dim(jnp.stack(results), section, micro, 0)
    stacked = jax.tree.map(lambda *items: jnp.stack(items), *stored)
    regathered = (
        *sent_together((shards[0], shards[1], shards[2]), "dp", 1, 2),
        lax.all_gather(shards[3], "dp", axis=1, tiled=True),
        *sent_together((shards[4], shards[5], shards[6], shards[7]), "dp", 1, 2),
        lax.all_gather(shards[8], "dp", axis=1, tiled=True),
    )
    backward_weights = tuple((piece[0] for piece in regathered))
    upstream = jnp.zeros(cotangent.shape[1:], jnp.bfloat16)
    sent_grads = []
    pieces = []
    for tick_index in range(micro + 1):
        own_grad = cotangent[min(tick_index, micro - 1)]
        grad_in = jnp.where(section == 1, own_grad, upstream).astype(jnp.float32)
        source = jnp.clip(tick_index - 1 + 2 * section, 0, micro)
        kept = jax.tree.map(
            lambda item: lax.dynamic_index_in_dim(item, source, 0, keepdims=False), stacked
        )
        grad_rows, parts = backward_layer(grad_in, kept, backward_weights)
        grad_low = grad_rows.astype(jnp.bfloat16)
        sent_grads.append(jnp.where(section == 1, grad_low.astype(jnp.float32), grad_rows))
        pieces.append(parts)
        if tick_index < micro:
            upstream = from_behind(grad_low, "section", -1)
    input_grads = lax.dynamic_slice_in_dim(jnp.stack(sent_grads), 1 - section, micro, 0)
    chosen = jax.tree.map(
        lambda *items: lax.dynamic_slice_in_dim(jnp.stack(items), 1 - section, micro, 0), *pieces
    )
    (
        normed_low,
        grad_projected,
        mixed_low,
        grad_attn_low,
        normed_two_low,
        grad_gu_low,
        activated,
        grad_mlp_low,
        gain_one,
        shift_one,
        gain_two,
        shift_two,
    ) = chosen
    attention_totals = (
        jnp.sum(gain_one, axis=0)[None],
        jnp.sum(shift_one, axis=0)[None],
        outer(normed_low, grad_projected)[None],
        jnp.sum(grad_projected.astype(jnp.float32), axis=(0, 1))[None],
        outer(mixed_low, grad_attn_low)[None],
    )
    attention_owned = (
        *in_one_piece((attention_totals[0], attention_totals[1], attention_totals[2]), "dp", 1, 2),
        lax.psum_scatter(attention_totals[3], "dp", scatter_dimension=1, tiled=True),
        lax.psum_scatter(attention_totals[4], "dp", scatter_dimension=1, tiled=True),
    )
    feed_totals = (
        jnp.sum(gain_two, axis=0)[None],
        jnp.sum(shift_two, axis=0)[None],
        outer(normed_two_low, grad_gu_low)[None],
        outer(activated, grad_mlp_low)[None],
    )
    feed_owned = (
        *in_one_piece((feed_totals[0], feed_totals[1], feed_totals[2]), "dp", 1, 2),
        lax.psum_scatter(feed_totals[3], "dp", scatter_dimension=1, tiled=True),
    )
    return (activations[None], input_grads[None]) + tuple(attention_owned) + tuple(feed_owned)


def solution(mesh):
    return jax.shard_map(
        on_device,
        mesh=mesh,
        in_specs=(
            P(None, "dp", None),
            P(None, "dp"),
            P(None, "dp", None),
            P("section", "dp"),
            P("section", "dp"),
            P("section", "dp", None),
            P("section", "dp"),
            P("section", "dp", None),
            P("section", "dp"),
            P("section", "dp"),
            P("section", "dp", None),
            P("section", "dp", None),
        ),
        out_specs=(
            P("section", None, "dp", None),
            P("section", None, "dp", None),
            P("section", "dp"),
            P("section", "dp"),
            P("section", "dp", None),
            P("section", "dp"),
            P("section", "dp", None),
            P("section", "dp"),
            P("section", "dp"),
            P("section", "dp", None),
            P("section", "dp", None),
        ),
        check_vma=False,
    )
```

profile of v0, /device:TPU:1, one launch (start us, length us, event | category | flops | bytes accessed | tf_op | source)
XLA Modules:
  0.0 3117.4 jit_solution(843046039580945331)
XLA Ops:
  17.3 279.6 %all-reduce = bf16[6144]{0:T(1024)(128)(2,1)S(1)} all-reduce(bf16[6144]{0:T(1024)(128)(2,1)S(1)} %dynamic-update-slice), channel_id=1, replica_groups=mesh['section'=2,'dp'=64] {'dp'}, use_global_device_ids=true, to_apply=%add | all-reduce | flops 6144 | bytes 24576
  318.3 13.1 convolution_add_fusion.4
  339.4 126.1 %all-gather.6.cloned.1.call-done = bf16[1,2048,13314]{2,1,0:T(8,128)(2,1)} async-done(((bf16[1,32,13314]{2,1,0:T(8,128)(2,1)}), bf16[1,2048,13314]{2,1,0:T(8,128)(2,1)}) %all-gather.6.cloned.1.call-update) | async-done | bytes 54534160 | tf_op jit(solution)/shard_map/all_gather | solution.py:22
  474.1 21.3 bitcast_dynamic-update-slice_fusion.4
  495.6 106.7 %all-gather.8.cloned.1.call-done = bf16[1,5632,2048]{2,1,0:T(8,128)(2,1)} async-done(((bf16[1,88,2048]{2,1,0:T(8,128)(2,1)}), bf16[1,5632,2048]{2,1,0:T(8,128)(2,1)}) %all-gather.8.cloned.1.call-update) | async-done | bytes 23068688 | tf_op jit(solution)/shard_map/all_gather | solution.py:290
  621.3 13.3 convolution_add_fusion.3
  652.0 21.2 bitcast_dynamic-update-slice_fusion.3
  692.9 13.5 convolution_add_fusion.2
  724.0 21.0 bitcast_dynamic-update-slice_fusion.2
  764.3 13.6 convolution_add_fusion.1
  795.3 21.3 bitcast_dynamic-update-slice_fusion.1
  836.5 12.7 convolution_add_fusion
  861.8 21.4 bitcast_dynamic-update-slice_fusion
  900.1 22.2 fusion.358
  954.5 15.3 fusion.347
  992.2 22.0 fusion.342
  1035.1 15.2 fusion.331
  1072.9 22.0 fusion.326
  1112.5 15.1 fusion.315
  1149.0 22.1 fusion.310
  1189.1 15.1 fusion.299
  1225.6 21.8 fusion.294
  1266.8 15.4 fusion.283
  1282.3 20.6 convolution_bitcast_fusion.2
  1303.9 60.1 %concatenate.401 = f32[1,2048,6146]{2,1,0:T(8,128)} concatenate(f32[1,2048,1]{2,1,0:T(8,128)S(1)} %copy.325, f32[1,2048,1]{2,1,0:T(8,128)S(1)} %copy.326, f32[1,2048,6144]{2,1,0:T(8,128)} %convolution_bitcast_fusion.2), dimensions={2} | concatenate | bytes 100696064 | tf_op jit(solution)/shard_map/concatenate | solution.py:35
  1370.5 33.9 %convolution_bitcast_fusion = f32[1,2048,11264]{2,1,0:T(8,128)} fusion(bf16[5,32,11264]{2,1,0:T(8,128)(2,1)} %maximum_dynamic-update-slice_fusion, s32[]{:T(128)S(6)} %select_n.303, bf16[5,32,2048]{2,1,0:T(8,128)(2,1)S(1)} %copy-done.95), kind=kOutput, calls=%fused_computation.5 | convolution fusion | flops 5905580032 | bytes 95683584 | tf_op jit(solution)/shard_map/dot_general | solution.py:251
  1404.4 110.3 %concatenate.417 = f32[1,2048,11266]{2,1,0:T(8,128)} concatenate(f32[1,2048,1]{2,1,0:T(8,128)S(1)} %copy.332, f32[1,2048,1]{2,1,0:T(8,128)S(1)} %copy.333, f32[1,2048,11264]{2,1,0:T(8,128)} %convolution_bitcast_fusion), dimensions={2} | concatenate | bytes 184582144 | tf_op jit(solution)/shard_map/concatenate | solution.py:35
  1529.6 18.2 convolution_bitcast_fusion.1
  1563.3 365.5 %reduce-scatter.8.cloned.1.call-done = f32[1,32,6146]{2,1,0:T(8,128)} async-done(((f32[1,2048,6146]{2,1,0:T(8,128)}), f32[1,32,6146]{2,1,0:T(8,128)}) %reduce-scatter.8.cloned.1.call-update) | async-done | bytes 786704 | tf_op jit(solution)/shard_map/reduce_scatter | solution.py:38
  1932.5 504.0 %reduce-scatter.12.cloned.1.call-done = f32[1,32,11266]{2,1,0:T(8,128)} async-done(((f32[1,2048,11266]{2,1,0:T(8,128)}), f32[1,32,11266]{2,1,0:T(8,128)}) %reduce-scatter.12.cloned.1.call-update) | async-done | bytes 1442064 | tf_op jit(solution)/shard_map/reduce_scatter | solution.py:38
  2440.9 305.4 %reduce-scatter.10.cloned.1.call-done = f32[1,32,2048]{2,1,0:T(8,128)} async-done(((f32[1,2048,2048]{2,1,0:T(8,128)}), f32[1,32,2048]{2,1,0:T(8,128)}) %reduce-scatter.10.cloned.1.call-update) | async-done | bytes 262160 | tf_op jit(solution)/shard_map/reduce_scatter | solution.py:359
  2746.3 363.7 %reduce-scatter.14.cloned.1.call-done = f32[1,88,2048]{2,1,0:T(8,128)} async-done(((f32[1,5632,2048]{2,1,0:T(8,128)}), f32[1,88,2048]{2,1,0:T(8,128)}) %reduce-scatter.14.cloned.1.call-update) | async-done | bytes 720912 | tf_op jit(solution)/shard_map/reduce_scatter | solution.py:369
  (780 shorter events, 446.7 us)
Async XLA Ops:
  7.2 309.2 %all-gather.4.cloned.1.call-start = ((), (), s32[]{:S(2)}) async-start(), calls=%async_computation.5 | async-start | bytes 26091520 | tf_op jit(solution)/shard_map/all_gather | solution.py:22
  10.8 286.1 %copy-start.139 = (s32[4,32]{1,0:T(4,128)S(1)}, s32[4,32]{1,0:T(4,128)}, u32[]{:S(2)}) copy-start(s32[4,32]{1,0:T(4,128)} %param.13) | copy-start | bytes 1540
  10.9 454.6 %all-gather.6.cloned.1.call-start = ((), (), s32[]{:S(2)}) async-start(), calls=%async_computation.6 | async-start | bytes 55910400 | tf_op jit(solution)/shard_map/all_gather | solution.py:22
  12.4 297.5 %copy-start.17 = (bf16[4,32,2048]{2,1,0:T(8,128)(2,1)S(1)}, bf16[4,32,2048]{2,1,0:T(8,128)(2,1)}, u32[]{:S(2)}) copy-start(bf16[4,32,2048]{2,1,0:T(8,128)(2,1)} %param.12) | copy-start | bytes 1572868
  14.9 587.3 %all-gather.8.cloned.1.call-start = ((), (), s32[]{:S(2)}) async-start(), calls=%async_computation.7 | async-start | bytes 23429120 | tf_op jit(solution)/shard_map/all_gather | solution.py:290
  15.7 1546.3 %reduce-scatter.16.cloned.1.call-start = ((), (), s32[]{:S(2)}) async-start(), calls=%async_computation.12 | async-start | bytes 3194880
  296.9 34.5 %copy-start.96 = (f32[6144]{0:T(1024)}, f32[6144]{0:T(1024)S(1)}, u32[]{:S(2)}) copy-start(f32[6144]{0:T(1024)S(1)} %add.731) | copy-start | bytes 73732
  318.2 947.7 %copy-start.62 = (f32[2048]{0:T(1024)}, f32[2048]{0:T(1024)S(1)}, u32[]{:S(2)}) copy-start(f32[2048]{0:T(1024)S(1)} %get-tuple-element.13) | copy-start | bytes 24580
  612.7 7.3 collective-permute-start
  683.9 7.7 collective-permute-start.1
  755.6 7.3 collective-permute-start.2
  827.8 7.3 collective-permute-start.3
  860.2 62.1 %copy-start = (f32[32,2048]{1,0:T(8,128)}, f32[32,2048]{1,0:T(8,128)S(1)}, u32[]{:S(2)}) copy-start(f32[32,2048]{1,0:T(8,128)S(1)} %get-tuple-element.280) | copy-start | bytes 786436
  900.1 22.2 copy-start.25
  900.1 22.2 copy-start.27
  971.8 7.2 collective-permute-start.4
  976.8 49.1 %copy-start.19 = (f32[32,32,32]{1,2,0:T(8,128)}, f32[32,32,32]{1,2,0:T(8,128)S(1)}, u32[]{:S(2)}) copy-start(f32[32,32,32]{1,2,0:T(8,128)S(1)} %fusion.99) | copy-start | bytes 393220
  992.2 22.0 copy-start.29
  992.2 22.0 copy-start.31
  992.2 22.0 copy-start.156
  1052.1 7.2 collective-permute-start.5
  1072.8 22.0 copy-start.33
  1072.9 22.0 copy-start.35
  1072.9 22.0 copy-start.154
  1128.4 7.2 collective-permute-start.6
  1149.0 22.1 copy-start.37
  1149.0 22.1 copy-start.152
  1205.0 7.2 collective-permute-start.7
  1265.9 662.9 %reduce-scatter.8.cloned.1.call-start = ((), (), s32[]{:S(2)}) async-start(), calls=%async_computation.8 | async-start | bytes 52183040 | tf_op jit(solution)/shard_map/reduce_scatter | solution.py:38
  1364.0 1072.5 %reduce-scatter.12.cloned.1.call-start = ((), (), s32[]{:S(2)}) async-start(), calls=%async_computation.10 | async-start | bytes 94781440 | tf_op jit(solution)/shard_map/reduce_scatter | solution.py:38
  1514.8 1231.6 %reduce-scatter.10.cloned.1.call-start = ((), (), s32[]{:S(2)}) async-start(), calls=%async_computation.9 | async-start | bytes 17039360 | tf_op jit(solution)/shard_map/reduce_scatter | solution.py:359
  1525.5 1584.5 %reduce-scatter.14.cloned.1.call-start = ((), (), s32[]{:S(2)}) async-start(), calls=%async_computation.11 | async-start | bytes 46858240 | tf_op jit(solution)/shard_map/reduce_scatter | solution.py:369
  (153 other events, 1029.7 us)
Sparse Core Ops, SparseCore 0:
  11.0 151.4 all-gather.3
  164.7 300.6 all-gather.5
  467.2 135.0 all-gather.7
  1266.0 288.0 reduce-scatter.15
  1556.5 372.2 reduce-scatter.7
  1931.0 505.4 reduce-scatter.11
  2439.6 306.6 reduce-scatter.9
  2749.5 360.5 reduce-scatter.13
where the time goes:
time: 3130 us; the launch traced here: 3120 us
  waiting for transfers between devices  1790 us (57%)
  matrix products  640 us (20%)
  local copies, waits for them, and re-layouts  281 us (9%)
  blocking collectives  280 us (9%)
  other arithmetic  81.7 us (3%)
    reduce_scatter x2, waiting for transfers between devices, in_one_piece(): out = lax.psum_scatter(both, axis, scatter_dimension=dim, tiled=True)  869 us
    reduce_scatter x1, waiting for transfers between devices, on_device(): lax.psum_scatter(feed_totals[3], 'dp', scatter_dimension=1, tiled=True)  364 us
    reduce_scatter x1, waiting for transfers between devices, on_device(): lax.psum_scatter(attention_totals[4], 'dp', scatter_dimension=1, tiled=True)  305 us
    unnamed x1, blocking collectives  280 us
    concatenate x2, local copies, waits for them, and re-layouts, in_one_piece(): jnp.concatenate([a.reshape(*a.shape[:along], w) for a, w in zip(arrays, w...  170 us
    all_gather x2, waiting for transfers between devices, sent_together(): out = lax.all_gather(both, axis, axis=dim, tiled=True)  126 us
    dot_general x5, matrix products, backward_layer(): lax.dot_general(grad_gu_low, gate_up, across, preferred_element_type=jnp....  110 us
    all_gather x1, waiting for transfers between devices, on_device(): lax.all_gather(shards[8], 'dp', axis=1, tiled=True)  107 us
  transfers between devices with their start and end apart: 16, of which 11 were waited for; matrix products, arithmetic and copies ran while one was open for 12% of the time, Pallas kernels for 0%

commit v1 on v0

v1 whole, which is shorter than its diff:
```python
import functools
import math

import jax
import jax.numpy as jnp
from jax import lax
from jax.experimental import pallas as pl
from jax.experimental.pallas import tpu as pltpu
from jax.sharding import Mesh
from jax.sharding import PartitionSpec as P

D = 2048
HEAD_DIM = 64
ROT = 16
FF = 5632
EPSILON = 1e-05
NEG_FILL = -1e30
TILE = 256
BLOCKS = D // TILE
ROWS = 64
GROUP = 8 * ROWS
HALF = GROUP // 2
LOCAL = 704
PIECE = 88
PADDED = 96
WIDE = 8 * PADDED
ATTN = 4 * TILE
MLP = 9 * TILE
VEC = 16
VMEM = 56 * 1024 * 1024
F32 = jnp.float32
BF16 = jnp.bfloat16

GRID = ("section", "x", "y", "z", "core")
DP = ("x", "y", "z", "core")
RING = ("section", "y")
SPREAD = ("section", "y", "z")


def dot(a, b):
    return jnp.dot(a, b, preferred_element_type=F32)


def dot_nt(a, b):
    return lax.dot_general(a, b, (((1,), (1,)), ((), ())), preferred_element_type=F32)


def dot_tn(a, b):
    return lax.dot_general(a, b, (((0,), (0,)), ((), ())), preferred_element_type=F32)


def call(kernel, outs, in_specs, *args, flops):
    moved = sum(math.prod(o.shape) * o.dtype.itemsize for o in outs) + 8 * 1024 * 1024
    return pl.pallas_call(
        kernel,
        grid=(1,),
        in_specs=in_specs,
        out_specs=[whole(o.shape) for o in outs],
        out_shape=outs,
        compiler_params=pltpu.CompilerParams(vmem_limit_bytes=VMEM),
        cost_estimate=pl.CostEstimate(flops=flops, bytes_accessed=moved, transcendentals=0),
    )(*args)


def whole(shape):
    return pl.BlockSpec(shape, lambda i: (0,) * len(shape), pipeline_mode=pl.Buffered(1))


def of_layer(layer, rows):
    return pl.BlockSpec(
        (1, BLOCKS, rows, TILE), lambda i: (layer, 0, 0, 0), pipeline_mode=pl.Buffered(1)
    )


def shape_of(*dims, dtype=BF16):
    return jax.ShapeDtypeStruct(dims, dtype)


def both(a_ref, b_ref):
    return jnp.concatenate([a_ref[...], b_ref[...]], axis=0)


def tile_of(w_ref, row, count=TILE):
    return w_ref[0, :, row : row + count, :].reshape(BLOCKS * count, TILE)


def twisted(u, table_ref, sign):
    def wide(k):
        t = table_ref[k]
        return jnp.concatenate([t, t], axis=1)

    n = u.shape[1]
    half = ROT // 2
    side = pltpu.roll(u, n - half, 1) * wide(1) + pltpu.roll(u, half, 1) * wide(2)
    return u * wide(0) + (side if sign > 0 else -side)


def pair_mask(h):
    lane = lax.broadcasted_iota(jnp.int32, (128, 128), 1)
    return (lane // HEAD_DIM) == h


def value_mask(h):
    lane = lax.broadcasted_iota(jnp.int32, (128, TILE), 1)
    return (lane // 32) % 4 == h


def probabilities(q, k, g, h, mask_ref):
    rows = slice(128 * g, 128 * g + 128)
    lanes = slice(128 * (h // 2), 128 * (h // 2) + 128)
    qh = jnp.where(pair_mask(h % 2), q[rows, lanes], jnp.zeros((), BF16))
    s = dot_nt(qh, k[rows, lanes]) * HEAD_DIM**-0.5
    m = mask_ref[rows, :]
    s = jnp.where(m > 0, s, NEG_FILL)
    e = jnp.exp(s - jnp.max(s, axis=1, keepdims=True))
    return e / jnp.sum(e, axis=1, keepdims=True)


def attention_kernel(na_ref, nb_ref, w_ref, bias_ref, table_ref, mask_ref, pa_ref, pb_ref, q_ref, k_ref, v_ref, o_ref):
    n = both(na_ref, nb_ref)
    for j, ref in enumerate((q_ref, k_ref, v_ref)):
        u = dot(n, tile_of(w_ref, TILE * j)) + bias_ref[j : j + 1, :]
        ref[...] = (twisted(u, table_ref, 1) if j < 2 else u).astype(BF16)
    q, k, v = q_ref[...], k_ref[...], v_ref[...]
    for g in range(GROUP // 128):
        rows = slice(128 * g, 128 * g + 128)
        o = jnp.zeros((128, TILE), F32)
        for h in range(4):
            p = probabilities(q, k, g, h, mask_ref).astype(BF16)
            o = jnp.where(value_mask(h), dot(p, v[rows]), o)
        o_ref[rows, :] = o.astype(BF16)
    o = o_ref[...]
    for j in range(BLOCKS):
        part = dot(o, tile_of(w_ref, 3 * TILE + 32 * j, 32)).astype(BF16)
        pa_ref[:, TILE * j : TILE * (j + 1)] = part[:HALF]
        pb_ref[:, TILE * j : TILE * (j + 1)] = part[HALF:]


def attention(layer, na, nb, weights, bias, table, mask):
    return call(
        attention_kernel,
        [shape_of(HALF, D), shape_of(HALF, D)] + [shape_of(GROUP, TILE)] * 4,
        [whole(na.shape), whole(nb.shape), of_layer(layer, ATTN), whole(bias.shape), whole(table.shape), whole(mask.shape)],
        na, nb, weights, bias, table, mask,
        flops=2 * GROUP * D * ATTN,
    )


def feed_kernel(na_ref, nb_ref, w_ref, pa_ref, pb_ref, g_ref, u_ref, act_ref):
    n = both(na_ref, nb_ref)
    for j in range(3):
        lanes = slice(TILE * j, TILE * (j + 1))
        g = dot(n, tile_of(w_ref, TILE * j))
        u = dot(n, tile_of(w_ref, TILE * (3 + j)))
        g_ref[:, lanes] = g
        u_ref[:, lanes] = u
        act_ref[:, lanes] = (g * jax.nn.sigmoid(g) * u).astype(BF16)
    act = act_ref[...]
    for j in range(BLOCKS):
        part = dot(act, tile_of(w_ref, 6 * TILE + PADDED * j, PADDED)).astype(BF16)
        pa_ref[:, TILE * j : TILE * (j + 1)] = part[:HALF]
        pb_ref[:, TILE * j : TILE * (j + 1)] = part[HALF:]


def feed(layer, na, nb, weights):
    return call(
        feed_kernel,
        [shape_of(HALF, D), shape_of(HALF, D), shape_of(GROUP, WIDE, dtype=F32), shape_of(GROUP, WIDE, dtype=F32), shape_of(GROUP, WIDE)],
        [whole(na.shape), whole(nb.shape), of_layer(layer, MLP)],
        na, nb, weights,
        flops=2 * GROUP * D * MLP,
    )


def feed_back_kernel(ma_ref, mb_ref, w_ref, g_ref, u_ref, ea_ref, eb_ref, dg_ref, du_ref):
    gm = both(ma_ref, mb_ref)
    da = jnp.zeros((GROUP, WIDE), F32)
    for j in range(BLOCKS):
        da += dot_nt(gm[:, TILE * j : TILE * (j + 1)], tile_of(w_ref, 6 * TILE + PADDED * j, PADDED))
    g = g_ref[...]
    u = u_ref[...]
    sigma = jax.nn.sigmoid(g)
    dg_ref[...] = (da * u * sigma * (1.0 + g * (1.0 - sigma))).astype(BF16)
    du_ref[...] = (da * g * sigma).astype(BF16)
    dg = dg_ref[...]
    du = du_ref[...]
    for b in range(BLOCKS):
        e = jnp.zeros((GROUP, TILE), F32)
        for j in range(3):
            lanes = slice(TILE * j, TILE * (j + 1))
            e += dot_nt(dg[:, lanes], w_ref[0, b, TILE * j : TILE * (j + 1), :])
            e += dot_nt(du[:, lanes], w_ref[0, b, TILE * (3 + j) : TILE * (4 + j), :])
        e = e.astype(BF16)
        ea_ref[:, TILE * b : TILE * (b + 1)] = e[:HALF]
        eb_ref[:, TILE * b : TILE * (b + 1)] = e[HALF:]


def feed_back(layer, ma, mb, weights, g, u):
    return call(
        feed_back_kernel,
        [shape_of(HALF, D), shape_of(HALF, D), shape_of(GROUP, WIDE), shape_of(GROUP, WIDE)],
        [whole(ma.shape), whole(mb.shape), of_layer(layer, MLP), whole(g.shape), whole(u.shape)],
        ma, mb, weights, g, u,
        flops=2 * GROUP * D * MLP,
    )


def attention_back_kernel(
    da_ref, db_ref, w_ref, q_ref, k_ref, v_ref, table_ref, mask_ref, ea_ref, eb_ref, dq_ref, dk_ref, dv_ref, db_sum_ref
):
    dattn = both(da_ref, db_ref)
    do = jnp.zeros((GROUP, TILE), F32)
    for j in range(BLOCKS):
        do += dot_nt(dattn[:, TILE * j : TILE * (j + 1)], tile_of(w_ref, 3 * TILE + 32 * j, 32))
    do = do.astype(BF16)
    q, k, v = q_ref[...], k_ref[...], v_ref[...]
    dqs, dks = [], []
    for g in range(GROUP // 128):
        rows = slice(128 * g, 128 * g + 128)
        dv = jnp.zeros((128, TILE), F32)
        dq_pairs, dk_pairs = [], []
        for pair in range(2):
            lanes = slice(128 * pair, 128 * pair + 128)
            dq = jnp.zeros((128, 128), F32)
            dk = jnp.zeros((128, 128), F32)
            for h in (2 * pair, 2 * pair + 1):
                p = probabilities(q, k, g, h, mask_ref)
                doh = jnp.where(value_mask(h), do[rows], jnp.zeros((), BF16))
                dp = dot_nt(doh, v[rows])
                ds = p * (dp - jnp.sum(p * dp, axis=1, keepdims=True))
                ds = ds.astype(BF16)
                dv = jnp.where(value_mask(h), dot_tn(p.astype(BF16), do[rows]), dv)
                dq = jnp.where(pair_mask(h % 2), dot(ds, k[rows, lanes]), dq)
                dk = jnp.where(pair_mask(h % 2), dot_tn(ds, q[rows, lanes]), dk)
            dq_pairs.append(dq)
            dk_pairs.append(dk)
        dv_ref[rows, :] = dv.astype(BF16)
        dqs.append(jnp.concatenate(dq_pairs, axis=1))
        dks.append(jnp.concatenate(dk_pairs, axis=1))
    factor = HEAD_DIM**-0.5
    dq_ref[...] = twisted(jnp.concatenate(dqs, axis=0) * factor, table_ref, -1).astype(BF16)
    dk_ref[...] = twisted(jnp.concatenate(dks, axis=0) * factor, table_ref, -1).astype(BF16)
    parts = (dq_ref[...], dk_ref[...], dv_ref[...])
    db_sum_ref[...] = jnp.concatenate(
        [jnp.sum(part.astype(F32), axis=0, keepdims=True) for part in parts] + [jnp.zeros((5, TILE), F32)], axis=0
    )
    for b in range(BLOCKS):
        e = jnp.zeros((GROUP, TILE), F32)
        for j in range(3):
            e += dot_nt(parts[j], w_ref[0, b, TILE * j : TILE * (j + 1), :])
        e = e.astype(BF16)
        ea_ref[:, TILE * b : TILE * (b + 1)] = e[:HALF]
        eb_ref[:, TILE * b : TILE * (b + 1)] = e[HALF:]


def attention_back(layer, da, db, weights, q, k, v, table, mask):
    return call(
        attention_back_kernel,
        [shape_of(HALF, D), shape_of(HALF, D)] + [shape_of(GROUP, TILE)] * 3 + [shape_of(8, TILE, dtype=F32)],
        [whole(da.shape), whole(db.shape), of_layer(layer, ATTN)] + [whole(q.shape)] * 3 + [whole(table.shape), whole(mask.shape)],
        da, db, weights, q, k, v, table, mask,
        flops=2 * GROUP * D * ATTN,
    )


def attention_grads_kernel(na_ref, nb_ref, o_ref, da_ref, db_ref, dq_ref, dk_ref, dv_ref, vec_ref, out_ref):
    n = both(na_ref, nb_ref)
    dattn = both(da_ref, db_ref)
    o = o_ref[...]
    parts = (dq_ref[...], dk_ref[...], dv_ref[...])
    for b in range(BLOCKS):
        left = n[:, TILE * b : TILE * (b + 1)]
        for j in range(3):
            half, row = divmod(TILE * j, 2 * TILE)
            out_ref[half, b, row : row + TILE, :] = dot_tn(left, parts[j]).astype(BF16)
    for j in range(BLOCKS):
        part = dot_tn(o, dattn[:, TILE * j : TILE * (j + 1)]).astype(BF16)
        out_ref[1, :, TILE + 32 * j : TILE + 32 * (j + 1), :] = part.reshape(BLOCKS, 32, TILE)
    out_ref[0, :, 2 * TILE :, :] = vec_ref[...]
    out_ref[1, :, 2 * TILE :, :] = jnp.zeros_like(vec_ref)


def attention_grads(na, nb, o, da, db, dq, dk, dv, vec):
    args = (na, nb, o, da, db, dq, dk, dv, vec)
    return call(
        attention_grads_kernel,
        [shape_of(2, BLOCKS, ATTN // 2 + VEC, TILE)],
        [whole(a.shape) for a in args],
        *args,
        flops=2 * GROUP * D * ATTN,
    )[0]


def feed_grads_kernel(na_ref, nb_ref, dg_ref, du_ref, act_ref, ma_ref, mb_ref, vec_ref, out_ref):
    n = both(na_ref, nb_ref)
    gm = both(ma_ref, mb_ref)
    act = act_ref[...]
    for b in range(BLOCKS):
        left = n[:, TILE * b : TILE * (b + 1)]
        for half, ref in enumerate((dg_ref, du_ref)):
            for j in range(3):
                lanes = slice(TILE * j, TILE * (j + 1))
                out_ref[half, b, lanes, :] = dot_tn(left, ref[:, lanes]).astype(BF16)
    for j in range(BLOCKS):
        half, k = divmod(j, 4)
        part = dot_tn(act, gm[:, TILE * j : TILE * (j + 1)]).astype(BF16)
        row = 3 * TILE + PADDED * k
        out_ref[half, :, row : row + PADDED, :] = part.reshape(BLOCKS, PADDED, TILE)
    out_ref[0, :, MLP // 2 :, :] = vec_ref[...]
    out_ref[1, :, MLP // 2 :, :] = jnp.zeros_like(vec_ref)


def feed_grads(na, nb, dg, du, act, ma, mb, vec):
    args = (na, nb, dg, du, act, ma, mb, vec)
    return call(
        feed_grads_kernel,
        [shape_of(2, BLOCKS, MLP // 2 + VEC, TILE)],
        [whole(a.shape) for a in args],
        *args,
        flops=2 * GROUP * D * MLP,
    )[0]


def turned(block, axis, step):
    n = math.prod(lax.axis_size(a) for a in (axis if isinstance(axis, tuple) else (axis,)))
    return lax.ppermute(block, axis, [(i, (i - step) % n) for i in range(n)])


def in_order(block, axis, n):
    ahead = jnp.stack([block] + [turned(block, axis, k) for k in range(1, n)])
    return jnp.roll(ahead, lax.axis_index(axis), axis=0)


def gathered_rows(block):
    own = jnp.concatenate([block] + [turned(block, "x", k) for k in range(1, 4)], axis=0)
    return own, turned(own, "core", 1)


def summed_rows(part_a, part_b):
    other = turned(part_b, "core", 1)

    def piece(k):
        rows = slice(ROWS * k, ROWS * (k + 1))
        return part_a[rows].astype(F32) + other[rows].astype(F32)

    arrived = [turned(piece(k).astype(BF16), "x", -k) for k in (1, 2, 3)]
    total = piece(0)
    for block in arrived:
        total = total + block.astype(F32)
    return total


def swapped(block):
    return lax.ppermute(block, ("y", "core"), [(2 * y + c, 2 * c + y) for y in range(2) for c in range(2)])


def spread(block):
    return lax.all_to_all(block, ("x", "core"), 0, 0, tiled=True)


def to_stored(rows):
    shape = rows.shape[:-1]
    k = len(shape)
    cut = rows.reshape(*shape, 4, 8, 64)
    return jnp.swapaxes(cut, k, k + 1).reshape(*shape, D)


def from_stored(rows):
    shape = rows.shape[:-1]
    k = len(shape)
    cut = rows.reshape(*shape, 8, 4, 64)
    return jnp.swapaxes(cut, k, k + 1).reshape(*shape, D)


def cut_out(weight):
    rows = weight.shape[0]
    return weight.reshape(rows, 4, 8, 64).transpose(2, 0, 1, 3).reshape(8, rows, TILE)


def join_out(blocks):
    rows = blocks.shape[1]
    return blocks.reshape(8, rows, 4, 64).transpose(1, 2, 0, 3).reshape(rows, D)


def value_columns(cut):
    shape = cut.shape[:-1]
    k = len(shape)
    return jnp.swapaxes(cut.reshape(*shape, 4, 2, 32), k, k + 1).reshape(*shape, TILE)


def value_columns_back(cut):
    shape = cut.shape[:-1]
    k = len(shape)
    return jnp.swapaxes(cut.reshape(*shape, 2, 4, 32), k, k + 1).reshape(*shape, TILE)


def pad_pieces(array, axis):
    pads = [(0, 0)] * array.ndim
    pads[axis] = (0, PADDED - PIECE)
    return jnp.pad(array, pads)


def attention_payload(qkv_weight, out_weight):
    cut = qkv_weight.reshape(32, 3, 8, TILE)
    cut = jnp.concatenate([cut[:, :2], value_columns(cut[:, 2:])], axis=1)
    cut = spread(cut.transpose(2, 1, 0, 3))
    cut = cut.transpose(1, 0, 2, 3).reshape(3 * TILE, TILE)
    return cut, cut_out(out_weight)


def feed_payload(gate_up, down_weight):
    cut = gate_up.reshape(32, 2, 8, 4, 2, PIECE).transpose(2, 1, 0, 4, 3, 5)
    cut = pad_pieces(cut, 5).reshape(8, 2, 32, 3, TILE).transpose(0, 1, 3, 2, 4)
    cut = spread(cut.reshape(8, 6, 32, TILE))
    cut = cut.transpose(1, 0, 2, 3).reshape(6 * TILE, TILE)
    return cut, pad_pieces(cut_out(down_weight), 1)


def attention_owned(full):
    cut = full[: 3 * TILE].reshape(3, 8, 32, TILE).transpose(1, 0, 2, 3)
    cut = spread(cut).transpose(2, 1, 0, 3)
    cut = jnp.concatenate([cut[:, :2], value_columns_back(cut[:, 2:])], axis=1)
    out = swapped(full[3 * TILE :]).reshape(8, 32, TILE)
    return cut.reshape(32, 3 * D).astype(F32), join_out(out).astype(F32)


def feed_owned(gate_up, down):
    cut = gate_up.reshape(6, 8, 32, TILE).transpose(1, 0, 2, 3)
    cut = spread(cut).reshape(8, 2, 3, 32, TILE).transpose(0, 1, 3, 2, 4)
    cut = cut.reshape(8, 2, 32, 2, 4, PADDED)[..., :PIECE]
    cut = cut.transpose(2, 1, 0, 4, 3, 5).reshape(32, 2 * FF)
    down = swapped(down).reshape(8, PADDED, TILE)[:, :PIECE]
    return cut.astype(F32), join_out(down).astype(F32)


def geometry(segments):
    groups = segments.reshape(GROUP // 128, 128)
    index = jnp.arange(128, dtype=jnp.int32)
    block = index // 32
    same = (groups[:, :, None] == groups[:, None, :]) & (block[None, :, None] == block[None, None, :])
    before = index[None, :] < index[:, None]
    places = jnp.sum(jnp.where(same & before, 1.0, 0.0), axis=-1).astype(F32).reshape(GROUP)
    inverse = 10000.0 ** (-(jnp.arange(ROT // 2).astype(F32) * 2.0 / ROT))
    theta = places[:, None] * inverse
    cosine, sine = jnp.cos(theta), jnp.sin(theta)
    rest = HEAD_DIM - ROT
    zero = jnp.zeros((GROUP, ROT // 2), F32)
    straight = jnp.concatenate([cosine, cosine, jnp.ones((GROUP, rest), F32)], axis=1)
    first = jnp.concatenate([-sine, zero, jnp.zeros((GROUP, rest), F32)], axis=1)
    second = jnp.concatenate([zero, sine, jnp.zeros((GROUP, rest), F32)], axis=1)
    table = jnp.stack([jnp.concatenate([t, t], axis=1) for t in (straight, first, second)])
    linked = same & (index[None, :] <= index[:, None])
    return table, jnp.where(linked, 1.0, 0.0).astype(F32).reshape(GROUP, 128)


def normalize(values, gain, shift):
    mean = jnp.mean(values, axis=-1, keepdims=True)
    centred = values - mean
    scale = lax.rsqrt(jnp.mean(centred * centred, axis=-1, keepdims=True) + EPSILON)
    unit = centred * scale
    return (unit * gain + shift).astype(BF16), unit, scale


def normalize_back(grad_out, unit, scale, gain):
    grad_unit = grad_out * gain
    return scale * (
        grad_unit
        - jnp.mean(grad_unit, axis=-1, keepdims=True)
        - unit * jnp.mean(grad_unit * unit, axis=-1, keepdims=True)
    )


def vector_rows(*parts):
    cut = jnp.concatenate(parts, axis=2).astype(BF16)
    return jnp.pad(cut, ((0, 0), (0, VEC - 8), (0, TILE - cut.shape[2])))


def by_owner(vector):
    return vector.reshape(8, 8, 32)


def on_device(
    block_input,
    segment_ids,
    cotangent,
    first_gain,
    first_shift,
    qkv_weight,
    qkv_bias,
    out_weight,
    second_gain,
    second_shift,
    gate_up,
    down_weight,
):
    section = lax.axis_index("section")
    shard = 2 * lax.axis_index("x") + lax.axis_index("core")

    qkv_part, out_part = attention_payload(qkv_weight[0], out_weight[0])
    gate_part, down_part = feed_payload(gate_up[0], down_weight[0])
    out_part = swapped(out_part).reshape(TILE, TILE)
    down_part = swapped(down_part).reshape(3 * TILE, TILE)
    attn_weights = lax.all_gather(jnp.concatenate([qkv_part, out_part], axis=0), SPREAD, axis=0, tiled=True)
    attn_weights = attn_weights.reshape(2, BLOCKS, ATTN, TILE)
    feed_weights = lax.all_gather(jnp.concatenate([gate_part, down_part], axis=0), SPREAD, axis=0, tiled=True)
    feed_weights = feed_weights.reshape(2, BLOCKS, MLP, TILE)

    vectors = jnp.concatenate([first_gain[0], first_shift[0], second_gain[0], second_shift[0], qkv_bias[0]])
    vectors = jnp.pad(vectors, (0, 32)).reshape(1, TILE)
    vectors = in_order(vectors, "core", 2)
    vectors = in_order(vectors, "x", 4)
    vectors = in_order(vectors, "z", 4)
    vectors = in_order(vectors, RING, 4)
    vectors = vectors.reshape(2, 64, TILE).astype(F32)
    gains = [vectors[:, :, 32 * k : 32 * (k + 1)].reshape(2, D) for k in range(4)]
    bias = vectors[:, :, 128:224].reshape(2, 2, 4, 4, 2, 96).transpose(0, 3, 1, 2, 4, 5).reshape(2, 3, 8, TILE)
    bias = lax.dynamic_index_in_dim(bias, shard, 2, keepdims=False)
    bias = jnp.concatenate([bias[:, :2], value_columns(bias[:, 2:])], axis=1)
    bias = jnp.pad(bias, ((0, 0), (0, 5), (0, 0)))

    def own_rows(array):
        return lax.dynamic_slice_in_dim(array, 2 * section, 2, 0)

    rows_in = to_stored(own_rows(block_input).reshape(ROWS, D))
    top_grad = to_stored(own_rows(cotangent).reshape(ROWS, D))
    segments = own_rows(segment_ids).reshape(1, ROWS)
    seg_a, seg_b = gathered_rows(segments)
    table, mask = geometry(jnp.concatenate([seg_a, seg_b], axis=0))
    top_a, top_b = gathered_rows(top_grad)

    kept = []
    outputs = []
    layer_in = rows_in
    for layer in range(2):
        inputs = layer_in.astype(F32)
        n1, unit1, scale1 = normalize(inputs, gains[0][layer], gains[1][layer])
        n1a, n1b = gathered_rows(n1)
        part_a, part_b, q, k, v, mixed = attention(layer, n1a, n1b, attn_weights, bias[layer], table, mask)
        hidden = inputs + summed_rows(part_a, part_b)
        n2, unit2, scale2 = normalize(hidden, gains[2][layer], gains[3][layer])
        n2a, n2b = gathered_rows(n2)
        part_a, part_b, g, u, act = feed(layer, n2a, n2b, feed_weights)
        result = (hidden + summed_rows(part_a, part_b)).astype(BF16)
        outputs.append(result)
        layer_in = result
        kept.append((unit1, scale1, n1a, n1b, q, k, v, mixed, unit2, scale2, n2a, n2b, g, u, act))

    grads_in = [None, None]
    attn_sums = [None, None]
    feed_sums = [None, None]
    upstream = top_grad
    ma, mb = top_a, top_b
    for layer in (1, 0):
        unit1, scale1, n1a, n1b, q, k, v, mixed, unit2, scale2, n2a, n2b, g, u, act = kept[layer]
        if layer == 0:
            ma, mb = gathered_rows(upstream)
        ea, eb, dg, du = feed_back(layer, ma, mb, feed_weights, g, u)
        e2 = summed_rows(ea, eb)
        grad_hidden = upstream.astype(F32) + normalize_back(e2, unit2, scale2, gains[2][layer])
        dattn = grad_hidden.astype(BF16)
        da, db = gathered_rows(dattn)
        feed_sums[layer] = feed_grads(
            n2a, n2b, dg, du, act, ma, mb,
            vector_rows(by_owner(jnp.sum(e2 * unit2, axis=0)), by_owner(jnp.sum(e2, axis=0))),
        )
        ea, eb, dq, dk, dv, bias_sum = attention_back(layer, da, db, attn_weights, q, k, v, table, mask)
        e1 = summed_rows(ea, eb)
        grad_rows = grad_hidden + normalize_back(e1, unit1, scale1, gains[0][layer])
        bias_sum = jnp.concatenate([bias_sum[:2], value_columns_back(bias_sum[2:3])], axis=0)
        bias_sum = lax.dynamic_update_slice_in_dim(jnp.zeros((3, 8, TILE), F32), bias_sum[:, None], shard, 1)
        bias_sum = bias_sum.reshape(4, 2, 4, 2, 96).transpose(1, 2, 0, 3, 4).reshape(8, 8, 96)
        attn_sums[layer] = attention_grads(
            n1a, n1b, mixed, da, db, dq, dk, dv,
            vector_rows(by_owner(jnp.sum(e1 * unit1, axis=0)), by_owner(jnp.sum(e1, axis=0)), bias_sum),
        )
        grads_in[layer] = grad_rows
        upstream = grad_rows.astype(BF16)

    def scattered(parts):
        joined = jnp.concatenate(parts, axis=2) if len(parts) > 1 else parts[0]
        joined = joined.reshape(16, -1, TILE)
        return lax.psum_scatter(joined, SPREAD, scatter_dimension=0, tiled=False)

    attn_rows = ATTN // 2 + VEC
    feed_1 = scattered([feed_sums[1]])
    middle = scattered([attn_sums[1], feed_sums[0]])
    attn_1, feed_0 = middle[:attn_rows], middle[attn_rows:]
    attn_0 = scattered([attn_sums[0]])

    def whole_layer(low, high):
        mine = jnp.where(section == 0, low, high)
        other = turned(jnp.where(section == 0, high, low), "section", 1)
        first = jnp.where(section == 0, mine, other)
        second = jnp.where(section == 0, other, mine)
        return first, second

    feed_first, feed_second = whole_layer(feed_0, feed_1)
    attn_first, attn_second = whole_layer(attn_0, attn_1)
    gate_up_grad, down_grad = feed_owned(
        jnp.concatenate([feed_first[: 3 * TILE], feed_second[: 3 * TILE]], axis=0),
        jnp.concatenate([feed_first[3 * TILE : MLP // 2], feed_second[3 * TILE : MLP // 2]], axis=0),
    )
    qkv_grad, out_grad = attention_owned(
        jnp.concatenate([attn_first[: 2 * TILE], attn_second[: 2 * TILE]], axis=0)
    )
    small = jnp.concatenate([attn_first[2 * TILE : 2 * TILE + 8], feed_first[MLP // 2 : MLP // 2 + 8]], axis=1)
    small = jnp.sum(spread(small).astype(F32), axis=0)

    def layer_rows(first, second):
        mine = jnp.where(section == 0, first, second)
        other = turned(jnp.where(section == 0, second, first).astype(BF16), "section", 1).astype(first.dtype)
        rows = jnp.where(section == 0, jnp.concatenate([mine, other]), jnp.concatenate([other, mine]))
        return from_stored(rows).reshape(1, 4, 32, D)

    activations = layer_rows(outputs[0], outputs[1])
    input_grads = layer_rows(grads_in[0], upstream_of(grads_in[1]))
    return (
        activations,
        input_grads,
        small[None, 0:32],
        small[None, 32:64],
        qkv_grad[None],
        small[None, 64:160],
        out_grad[None],
        small[None, TILE : TILE + 32],
        small[None, TILE + 32 : TILE + 64],
        gate_up_grad[None],
        down_grad[None],
    )


def upstream_of(grad_rows):
    return grad_rows.astype(BF16).astype(F32)


def solution(mesh):
    grid = Mesh(mesh.devices.reshape(2, 4, 2, 4, 2), GRID)
    return jax.shard_map(
        on_device,
        mesh=grid,
        in_specs=(
            P(None, DP, None),
            P(None, DP),
            P(None, DP, None),
            P("section", DP),
            P("section", DP),
            P("section", DP, None),
            P("section", DP),
            P("section", DP, None),
            P("section", DP),
            P("section", DP),
            P("section", DP, None),
            P("section", DP, None),
        ),
        out_specs=(
            P("section", None, DP, None),
            P("section", None, DP, None),
            P("section", DP),
            P("section", DP),
            P("section", DP, None),
            P("section", DP),
            P("section", DP, None),
            P("section", DP),
            P("section", DP),
            P("section", DP, None),
            P("section", DP, None),
        ),
        check_vma=False,
    )
```

time: 3130 us -> 971 us (0.31)
  waiting for transfers between devices: 1790 us -> 544 us
  matrix products: 640 us -> 0 us
  blocking collectives: 280 us -> 0 us
  local copies, waits for them, and re-layouts: 281 us -> 54.2 us
  Pallas kernels: 0 us -> 141 us
  starting transfers between devices: 26.6 us -> 142 us
    reduce_scatter x4 -> x0, waiting for transfers between devices: 1540 us -> none  [the longest x2 869 us: in_one_piece(): out = lax.psum_scatter(both, axis, scatter_dimension=dim, tiled=True)]
    dot_general x79 -> x0, matrix products: 640 us -> none  [the longest x5 110 us: backward_layer(): lax.dot_general(grad_gu_low, gate_up, across, preferred_element_type=jnp....]
    unnamed x1 -> x0, blocking collectives: 280 us -> none
    unnamed x9 -> x8, waiting for transfers between devices: 0.8 us -> 244 us
    ppermute x8 -> x86, waiting for transfers between devices: 17.9 us -> 219 us  [the longest x82 206 us: turned(): return lax.ppermute(block, axis, [(i, (i - step) % n) for i in range(n)])]
    concatenate x14 -> x17, local copies, waits for them, and re-layouts: 179 us -> 5.15 us  [the longest x8 3.67 us: layer_rows(): jnp.concatenate([mine, other])]
    all_gather x3 -> x2, waiting for transfers between devices: 233 us -> 62.5 us  [the longest x1 62.5 us: on_device(): lax.all_gather(jnp.concatenate([gate_part, down_part], axis=0), SPREAD, a...]
    pallas_call x0 -> x12, Pallas kernels: none -> 141 us  [call(): pl.pallas_call(kernel, grid=(1,), in_specs=in_specs, out_specs=[whole(o.s...]
  transfers between devices with their start and end apart: 16 -> 96, of which waited for: 11 -> 65; matrix products, arithmetic and copies ran while one was open for 12% -> 7% of each run, Pallas kernels for 0% -> 7%
where the time goes in v1:
time: 971 us; the launch traced here: 961 us
  waiting for transfers between devices  544 us (56%)
  starting transfers between devices  142 us (15%)
  Pallas kernels  141 us (15%)
  other arithmetic  64.1 us (7%)
  local copies, waits for them, and re-layouts  54.2 us (6%)
  between operations  15.7 us (2%)
    unnamed x8, waiting for transfers between devices  244 us
    ppermute x82, waiting for transfers between devices, turned(): return lax.ppermute(block, axis, [(i, (i - step) % n) for i in range(n)])  206 us
    pallas_call x12, Pallas kernels, call(): pl.pallas_call(kernel, grid=(1,), in_specs=in_specs, out_specs=[whole(o.s...  141 us
    ppermute x82, starting transfers between devices, turned(): return lax.ppermute(block, axis, [(i, (i - step) % n) for i in range(n)])  105 us
    all_gather x1, waiting for transfers between devices, on_device(): lax.all_gather(jnp.concatenate([gate_part, down_part], axis=0), SPREAD, a...  62.5 us
    all_to_all x5, starting transfers between devices, spread(): return lax.all_to_all(block, ('x', 'core'), 0, 0, tiled=True)  23.3 us
  transfers between devices with their start and end apart: 96, of which 65 were waited for; matrix products, arithmetic and copies ran while one was open for 7% of the time, Pallas kernels for 7%

profile of v1, /device:TPU:1, one launch (start us, length us, event | category | flops | bytes accessed | tf_op | source)
XLA Modules:
  0.0 961.4 jit_solution(6542243382895269219)
XLA Ops:
  39.1 13.7 %collective-permute-done.27 = bf16[8,96,256]{1,2,0:T(8,128)(2,1)S(1)} collective-permute-done((bf16[8,96,256]{1,2,0:T(8,128)(2,1)S(1)}, bf16[8,96,256]{1,2,0:T(8,128)(2,1)S(1)}, u32[]{:S(2)}, u32[]{:S(2)}) %collective-permute-start.27) | collective-permute-done | bytes 393248 | tf_op jit(solution)/shard_map/ppermute | solution.py:354
  88.8 7.0 collective-permute-done.15
  107.6 12.6 %shard_map.203 = (bf16[256,2048]{1,0:T(8,128)(2,1)}, bf16[256,2048]{1,0:T(8,128)(2,1)}, bf16[512,256]{1,0:T(8,128)(2,1)}, bf16[512,256]{1,0:T(8,128)(2,1)}, bf16...) custom-call(bf16[256,2048]{1,0:T(8,128)(2,1)} %copy-done.3, bf16[256,2048]{1,0:T(8,128)(2,1)} %collective-permute-done.13.nb_ref, ...), custom_call_target="tpu_custom_call" | custom-call | flops 2147483648 | bytes 11534336 | tf_op jit(solution)/shard_map/pallas_call | solution.py:54
  133.9 6.1 collective-permute-done.21
  144.8 6.2 collective-permute-done.25
  160.4 62.5 %all-gather.5.cloned.1.call-done = bf16[36864,256]{1,0:T(8,128)(2,1)} async-done(((bf16[2304,256]{1,0:T(8,128)(2,1)}), bf16[36864,256]{1,0:T(8,128)(2,1)}) %all-gather.5.cloned.1.call-update) | async-done | bytes 18874384 | tf_op jit(solution)/shard_map/all_gather | solution.py:505
  222.9 11.2 %shard_map.204 = (bf16[256,2048]{1,0:T(8,128)(2,1)}, bf16[256,2048]{1,0:T(8,128)(2,1)}, f32[512,768]{1,0:T(8,128)}, f32[512,768]{1,0:T(8,128)}, bf16[512,768]{1,0:T(8,128)(2,1)}) custom-call(bf16[256,2048]{1,0:T(8,128)(2,1)} %copy-done.10, bf16[256,2048]{1,0:T(8,128)(2,1)} %copy-done.17, bf16[2,8,2304,256]{3,2,1,0:T(8,128)(2,1)} %bitcast.191), custom_call_target="tpu_custom_call" | custom-call | flops 4831838208 | bytes 14417920 | tf_op jit(solution)/shard_map/pallas_call | solution.py:54
  248.3 6.5 collective-permute-done.30
  259.4 6.1 collective-permute-done.34
  276.5 12.3 %shard_map.205 = (bf16[256,2048]{1,0:T(8,128)(2,1)}, bf16[256,2048]{1,0:T(8,128)(2,1)}, bf16[512,256]{1,0:T(8,128)(2,1)}, bf16[512,256]{1,0:T(8,128)(2,1)}, bf16...) custom-call(bf16[256,2048]{1,0:T(8,128)(2,1)} %copy-done.4, bf16[256,2048]{1,0:T(8,128)(2,1)} %copy-done.7, ...), custom_call_target="tpu_custom_call" | custom-call | flops 2147483648 | bytes 11534336 | tf_op jit(solution)/shard_map/pallas_call | solution.py:54
  303.3 6.5 collective-permute-done.38
  334.9 11.1 %shard_map.206 = (bf16[256,2048]{1,0:T(8,128)(2,1)}, bf16[256,2048]{1,0:T(8,128)(2,1)}, f32[512,768]{1,0:T(8,128)}, f32[512,768]{1,0:T(8,128)}, bf16[512,768]{1,0:T(8,128)(2,1)}) custom-call(bf16[256,2048]{1,0:T(8,128)(2,1)} %copy-done.11, bf16[256,2048]{1,0:T(8,128)(2,1)} %copy-done.18, bf16[2,8,2304,256]{3,2,1,0:T(8,128)(2,1)} %bitcast.192), custom_call_target="tpu_custom_call" | custom-call | flops 4831838208 | bytes 14417920 | tf_op jit(solution)/shard_map/pallas_call | solution.py:54
  347.1 13.4 %shard_map.207 = (bf16[256,2048]{1,0:T(8,128)(2,1)}, bf16[256,2048]{1,0:T(8,128)(2,1)}, bf16[512,768]{1,0:T(8,128)(2,1)}, bf16[512,768]{1,0:T(8,128)(2,1)}) custom-call(bf16[256,2048]{1,0:T(8,128)(2,1)} %copy-done.15, bf16[256,2048]{1,0:T(8,128)(2,1)} %copy-done.19, bf16[2,8,2304,256]{3,2,1,0:T(8,128)(2,1)} %bitcast.193, ...), custom_call_target="tpu_custom_call" | custom-call | flops 4831838208 | bytes 12058624 | tf_op jit(solution)/shard_map/pallas_call | solution.py:54
  373.8 6.6 collective-permute-done.55
  385.3 6.6 collective-permute-done.59
  402.2 14.6 %shard_map.208 = (bf16[256,2048]{1,0:T(8,128)(2,1)}, bf16[256,2048]{1,0:T(8,128)(2,1)}, bf16[512,256]{1,0:T(8,128)(2,1)}, bf16[512,256]{1,0:T(8,128)(2,1)}, bf16[512,256]{1,0:T(8,128)(2,1)}, /*index=5*/f32[8,256]{1,0:T(8,128)}) custom-call(bf16[256,2048]{1,0:T(8,128)(2,1)} %copy-done.5, bf16[256,2048]{1,0:T(8,128)(2,1)} %copy-done.8, ...), custom_call_target="tpu_custom_call" | custom-call | flops 2147483648 | bytes 11280384 | tf_op jit(solution)/shard_map/pallas_call | solution.py:54
  429.8 6.5 collective-permute-done.63
  441.1 7.4 collective-permute-done.67
  457.8 13.5 %shard_map.209 = (bf16[256,2048]{1,0:T(8,128)(2,1)}, bf16[256,2048]{1,0:T(8,128)(2,1)}, bf16[512,768]{1,0:T(8,128)(2,1)}, bf16[512,768]{1,0:T(8,128)(2,1)}) custom-call(bf16[256,2048]{1,0:T(8,128)(2,1)} %copy-done.12, bf16[256,2048]{1,0:T(8,128)(2,1)} %copy-done.20, bf16[2,8,2304,256]{3,2,1,0:T(8,128)(2,1)} %bitcast.194, ...), custom_call_target="tpu_custom_call" | custom-call | flops 4831838208 | bytes 12058624 | tf_op jit(solution)/shard_map/pallas_call | solution.py:54
  480.7 6.9 shard_map.212
  493.6 11.9 %shard_map.213 = bf16[2,8,1168,256]{3,2,1,0:T(8,128)(2,1)} custom-call(bf16[256,2048]{1,0:T(8,128)(2,1)} %copy-done.10, bf16[256,2048]{1,0:T(8,128)(2,1)} %copy-done.17, bf16[512,768]{1,0:T(8,128)(2,1)} %get-tuple-element.89.dg_ref, bf16[512,768]{1,0:T(8,128)(2,1)} %get-tuple-element.90.du_ref, bf16[512,768]{1,0:T(8,128)(2,1)} %get-tuple-element.91.act_ref, ...), custom_call_target="tpu_custom_call" | custom-call | flops 4831838208 | bytes 17956864 | tf_op jit(solution)/shard_map/pallas_call | solution.py:54
  505.5 13.1 %pad_maximum_fusion = bf16[2,8,1696,256]{3,2,1,0:T(8,128)(2,1)} fusion(bf16[2,8,1168,256]{3,2,1,0:T(8,128)(2,1)} %shard_map.213, bf16[2,8,528,256]{3,2,1,0:T(8,128)(2,1)S(1)} %copy-done.2), kind=kLoop, calls=%fused_computation | loop fusion | flops 27787264 | bytes 27787264 | tf_op jit(solution)/shard_map/concatenate | solution.py:580
  519.5 11.7 %shard_map.214 = bf16[2,8,1168,256]{3,2,1,0:T(8,128)(2,1)} custom-call(bf16[256,2048]{1,0:T(8,128)(2,1)} %copy-done.11, bf16[256,2048]{1,0:T(8,128)(2,1)} %copy-done.18, bf16[512,768]{1,0:T(8,128)(2,1)} %get-tuple-element.92.dg_ref, bf16[512,768]{1,0:T(8,128)(2,1)} %get-tuple-element.93.du_ref, bf16[512,768]{1,0:T(8,128)(2,1)} %get-tuple-element.94.act_ref, ...), custom_call_target="tpu_custom_call" | custom-call | flops 4831838208 | bytes 17956864 | tf_op jit(solution)/shard_map/pallas_call | solution.py:54
  535.6 6.0 collective-permute-done.75
  552.2 15.1 %shard_map.210 = (bf16[256,2048]{1,0:T(8,128)(2,1)}, bf16[256,2048]{1,0:T(8,128)(2,1)}, bf16[512,256]{1,0:T(8,128)(2,1)}, bf16[512,256]{1,0:T(8,128)(2,1)}, bf16[512,256]{1,0:T(8,128)(2,1)}, /*index=5*/f32[8,256]{1,0:T(8,128)}) custom-call(bf16[256,2048]{1,0:T(8,128)(2,1)} %copy-done.6, bf16[256,2048]{1,0:T(8,128)(2,1)} %copy-done.9, ...), custom_call_target="tpu_custom_call" | custom-call | flops 2147483648 | bytes 11280384 | tf_op jit(solution)/shard_map/pallas_call | solution.py:54
  580.5 6.5 collective-permute-done.79
  590.3 6.9 shard_map.211
  622.7 9.1 collective-permute-done.48
  638.5 77.5 %all-reduce.13.cloned.1.call-done = bf16[16,1696,256]{2,1,0:T(8,128)(2,1)} async-done(((bf16[16,1696,256]{2,1,0:T(8,128)(2,1)}), bf16[16,1696,256]{2,1,0:T(8,128)(2,1)}) %all-reduce.13.cloned.1.call-update) | async-done | bytes 13893648
  716.0 90.4 %reduce-scatter.9.cloned.1.call-done = bf16[1,1168,256]{2,1,0:T(8,128)(2,1)} async-done(((bf16[16,1168,256]{2,1,0:T(8,128)(2,1)}), bf16[1,1168,256]{2,1,0:T(8,128)(2,1)}) %reduce-scatter.9.cloned.1.call-update) | async-done | bytes 598032
  811.4 75.8 %reduce-scatter.7.cloned.1.call-done = bf16[1,528,256]{2,1,0:T(8,128)(2,1)} async-done(((bf16[16,528,256]{2,1,0:T(8,128)(2,1)}), bf16[1,528,256]{2,1,0:T(8,128)(2,1)}) %reduce-scatter.7.cloned.1.call-update) | async-done | bytes 270352
  940.0 6.7 all-to-all-done.4
  (511 shorter events, 377.7 us)
Async XLA Ops:
  10.0 14.0 %all-to-all-start = ((bf16[8,3,32,256]{3,2,1,0:T(8,128)(2,1)}), bf16[8,3,32,256]{3,2,1,0:T(8,128)(2,1)S(1)}, u32[]{:S(2)}, u32[]{:S(2)}) async-start(bf16[8,3,32,256]{3,2,1,0:T(8,128)(2,1)} %copy.296), calls=%async_computation | async-start | bytes 786432 | tf_op jit(solution)/shard_map/all_to_all | solution.py:358
  16.0 91.6 %all-gather.3.cloned.1.call-start = ((), (), s32[]{:S(2)}) async-start(), calls=%async_computation.7 | async-start | bytes 8912896 | tf_op jit(solution)/shard_map/all_gather | solution.py:503
  31.1 21.9 %all-to-all-start.1 = ((bf16[8,6,32,256]{3,2,1,0:T(8,128)(2,1)}), bf16[8,6,32,256]{3,2,1,0:T(8,128)(2,1)S(1)}, u32[]{:S(2)}, u32[]{:S(2)}) async-start(bf16[8,6,32,256]{3,2,1,0:T(8,128)(2,1)} %bitcast.43), calls=%async_computation.1 | async-start | bytes 1572864 | tf_op jit(solution)/shard_map/all_to_all | solution.py:358
  35.4 187.5 %all-gather.5.cloned.1.call-start = ((), (), s32[]{:S(2)}) async-start(), calls=%async_computation.8 | async-start | bytes 20054016 | tf_op jit(solution)/shard_map/all_gather | solution.py:505
  35.9 16.9 %collective-permute-start.27 = (bf16[8,96,256]{1,2,0:T(8,128)(2,1)S(1)}, bf16[8,96,256]{1,2,0:T(8,128)(2,1)S(1)}, u32[]{:S(2)}, u32[]{:S(2)}) collective-permute-start(bf16[8,96,256]{1,2,0:T(8,128)(2,1)S(1)} %pad.33), channel_id=1, source_target_pairs={{0,0},{1,8},{8,1},{9,9},{2,2},{3,10},{10,3},{11,11},{4,4},{5,12},{... | collective-permute-start | bytes 1179656 | tf_op jit(solution)/shard_map/ppermute | solution.py:354
  54.3 661.7 %all-reduce.13.cloned.1.call-start = ((), (), s32[]{:S(2)}) async-start(), calls=%async_computation.9 | async-start | bytes 27787264
  54.4 34.2 %collective-permute-start.17 = (s32[1,64]{1,0:T(1,128)S(1)}, s32[1,64]{1,0:T(1,128)S(1)}, u32[]{:S(2)}, u32[]{:S(2)}) collective-permute-start(s32[1,64]{1,0:T(1,128)S(1)} %reshape.476), channel_id=1, source_target_pairs={{0,16},{16,32},{32,48},{48,0},{1,17},{17,33},{33,49},{49,1},{2,18}... | collective-permute-start | bytes 776 | tf_op jit(solution)/shard_map/ppermute | solution.py:326
  55.6 33.2 %collective-permute-start.16 = (s32[1,64]{1,0:T(1,128)S(1)}, s32[1,64]{1,0:T(1,128)S(1)}, u32[]{:S(2)}, u32[]{:S(2)}) collective-permute-start(s32[1,64]{1,0:T(1,128)S(1)} %reshape.476), channel_id=1, source_target_pairs={{0,32},{16,48},{32,0},{48,16},{1,33},{17,49},{33,1},{49,17},{2,34}... | collective-permute-start | bytes 776 | tf_op jit(solution)/shard_map/ppermute | solution.py:326
  84.7 16.4 %collective-permute-start.12 = (bf16[64,2048]{1,0:T(8,128)(2,1)S(1)}, bf16[64,2048]{1,0:T(8,128)(2,1)S(1)}, u32[]{:S(2)}, u32[]{:S(2)}) collective-permute-start(bf16[64,2048]{1,0:T(8,128)(2,1)S(1)} %add_convert_fusion.28), channel_id=1, source_target_pairs={{0,16},{16,32},{32,48},{48,0},{1,17},{17,33},{33,49},{49,1},{2,18}... | collective-permute-start | bytes 786440 | tf_op jit(solution)/shard_map/ppermute | solution.py:326
  85.4 15.8 %collective-permute-start.11 = (bf16[64,2048]{1,0:T(8,128)(2,1)S(1)}, bf16[64,2048]{1,0:T(8,128)(2,1)S(1)}, u32[]{:S(2)}, u32[]{:S(2)}) collective-permute-start(bf16[64,2048]{1,0:T(8,128)(2,1)S(1)} %add_convert_fusion.28), channel_id=1, source_target_pairs={{0,32},{16,48},{32,0},{48,16},{1,33},{17,49},{33,1},{49,17},{2,34}... | collective-permute-start | bytes 786440 | tf_op jit(solution)/shard_map/ppermute | solution.py:326
  87.4 13.7 %collective-permute-start.10 = (bf16[64,2048]{1,0:T(8,128)(2,1)S(1)}, bf16[64,2048]{1,0:T(8,128)(2,1)S(1)}, u32[]{:S(2)}, u32[]{:S(2)}) collective-permute-start(bf16[64,2048]{1,0:T(8,128)(2,1)S(1)} %add_convert_fusion.28), channel_id=1, source_target_pairs={{0,48},{16,0},{32,16},{48,32},{1,49},{17,1},{33,17},{49,33},{2,50}... | collective-permute-start | bytes 786440 | tf_op jit(solution)/shard_map/ppermute | solution.py:326
  242.0 12.8 %collective-permute-start.30 = (bf16[64,2048]{1,0:T(8,128)(2,1)S(1)}, bf16[64,2048]{1,0:T(8,128)(2,1)S(1)}, u32[]{:S(2)}, u32[]{:S(2)}) collective-permute-start(bf16[64,2048]{1,0:T(8,128)(2,1)S(1)} %get-tuple-element.236), channel_id=1, source_target_pairs={{0,32},{16,48},{32,0},{48,16},{1,33},{17,49},{33,1},{49,17},{2,34}... | collective-permute-start | bytes 786440 | tf_op jit(solution)/shard_map/ppermute | solution.py:326
  297.0 12.7 %collective-permute-start.38 = (bf16[64,2048]{1,0:T(8,128)(2,1)S(1)}, bf16[64,2048]{1,0:T(8,128)(2,1)}, u32[]{:S(2)}, u32[]{:S(2)}) collective-permute-start(bf16[64,2048]{1,0:T(8,128)(2,1)S(1)} %get-tuple-element.233), channel_id=1, source_target_pairs={{0,32},{16,48},{32,0},{48,16},{1,33},{17,49},{33,1},{49,17},{2,34}... | collective-permute-start | bytes 786440 | tf_op jit(solution)/shard_map/ppermute | solution.py:326
  298.9 31.9 %collective-permute-start.51 = (bf16[64,2048]{1,0:T(8,128)(2,1)S(1)}, bf16[64,2048]{1,0:T(8,128)(2,1)S(1)}, u32[]{:S(2)}, u32[]{:S(2)}) collective-permute-start(bf16[64,2048]{1,0:T(8,128)(2,1)S(1)} %reshape.483), channel_id=1, source_target_pairs={{0,16},{16,32},{32,48},{48,0},{1,17},{17,33},{33,49},{49,1},{2,18}... | collective-permute-start | bytes 786440 | tf_op jit(solution)/shard_map/ppermute | solution.py:326
  299.9 14.9 %collective-permute-start.49 = (bf16[64,2048]{1,0:T(8,128)(2,1)S(1)}, bf16[64,2048]{1,0:T(8,128)(2,1)S(1)}, u32[]{:S(2)}, u32[]{:S(2)}) collective-permute-start(bf16[64,2048]{1,0:T(8,128)(2,1)S(1)} %reshape.483), channel_id=1, source_target_pairs={{0,48},{16,0},{32,16},{48,32},{1,49},{17,1},{33,17},{49,33},{2,50}... | collective-permute-start | bytes 786440 | tf_op jit(solution)/shard_map/ppermute | solution.py:326
  313.6 14.4 %collective-permute-start.40 = (bf16[64,2048]{1,0:T(8,128)(2,1)S(1)}, bf16[64,2048]{1,0:T(8,128)(2,1)S(1)}, u32[]{:S(2)}, u32[]{:S(2)}) collective-permute-start(bf16[64,2048]{1,0:T(8,128)(2,1)S(1)} %add_convert_fusion.16), channel_id=1, source_target_pairs={{0,48},{16,0},{32,16},{48,32},{1,49},{17,1},{33,17},{49,33},{2,50}... | collective-permute-start | bytes 786440 | tf_op jit(solution)/shard_map/ppermute | solution.py:326
  314.7 16.1 %collective-permute-start.50 = (bf16[64,2048]{1,0:T(8,128)(2,1)S(1)}, bf16[64,2048]{1,0:T(8,128)(2,1)S(1)}, u32[]{:S(2)}, u32[]{:S(2)}) collective-permute-start(bf16[64,2048]{1,0:T(8,128)(2,1)S(1)} %reshape.483), channel_id=1, source_target_pairs={{0,32},{16,48},{32,0},{48,16},{1,33},{17,49},{33,1},{49,17},{2,34}... | collective-permute-start | bytes 786440 | tf_op jit(solution)/shard_map/ppermute | solution.py:326
  330.9 15.1 %collective-permute-start.52 = (bf16[256,2048]{1,0:T(8,128)(2,1)S(1)}, bf16[256,2048]{1,0:T(8,128)(2,1)S(1)}, u32[]{:S(2)}, u32[]{:S(2)}) collective-permute-start(bf16[256,2048]{1,0:T(8,128)(2,1)S(1)} %constant_dynamic-update-slice_fusion.24.ma_ref), channel_id=1, source_target_pairs={{0,1},{1,0},{2,3},{3,2},{4,5},{5,4},{6,7},{7,6},{8,9},{9,8},{10,11... | collective-permute-start | bytes 3145736 | tf_op jit(solution)/shard_map/ppermute | solution.py:326
  367.5 12.9 %collective-permute-start.55 = (bf16[64,2048]{1,0:T(8,128)(2,1)S(1)}, bf16[64,2048]{1,0:T(8,128)(2,1)S(1)}, u32[]{:S(2)}, u32[]{:S(2)}) collective-permute-start(bf16[64,2048]{1,0:T(8,128)(2,1)S(1)} %get-tuple-element.227), channel_id=1, source_target_pairs={{0,32},{16,48},{32,0},{48,16},{1,33},{17,49},{33,1},{49,17},{2,34}... | collective-permute-start | bytes 786440 | tf_op jit(solution)/shard_map/ppermute | solution.py:326
  384.2 12.6 %collective-permute-start.57 = (bf16[64,2048]{1,0:T(8,128)(2,1)S(1)}, bf16[64,2048]{1,0:T(8,128)(2,1)S(1)}, u32[]{:S(2)}, u32[]{:S(2)}) collective-permute-start(bf16[64,2048]{1,0:T(8,128)(2,1)S(1)} %get-tuple-element.195), channel_id=1, source_target_pairs={{0,48},{16,0},{32,16},{48,32},{1,49},{17,1},{33,17},{49,33},{2,50}... | collective-permute-start | bytes 786440 | tf_op jit(solution)/shard_map/ppermute | solution.py:326
  423.7 12.5 %collective-permute-start.63 = (bf16[64,2048]{1,0:T(8,128)(2,1)S(1)}, bf16[64,2048]{1,0:T(8,128)(2,1)S(1)}, u32[]{:S(2)}, u32[]{:S(2)}) collective-permute-start(bf16[64,2048]{1,0:T(8,128)(2,1)S(1)} %get-tuple-element.224), channel_id=1, source_target_pairs={{0,32},{16,48},{32,0},{48,16},{1,33},{17,49},{33,1},{49,17},{2,34}... | collective-permute-start | bytes 786440 | tf_op jit(solution)/shard_map/ppermute | solution.py:326
  439.7 13.1 %collective-permute-start.65 = (bf16[64,2048]{1,0:T(8,128)(2,1)S(1)}, bf16[64,2048]{1,0:T(8,128)(2,1)S(1)}, u32[]{:S(2)}, u32[]{:S(2)}) collective-permute-start(bf16[64,2048]{1,0:T(8,128)(2,1)S(1)} %fusion.14), channel_id=1, source_target_pairs={{0,48},{16,0},{32,16},{48,32},{1,49},{17,1},{33,17},{49,33},{2,50}... | collective-permute-start | bytes 786440 | tf_op jit(solution)/shard_map/ppermute | solution.py:326
  478.7 12.5 %collective-permute-start.71 = (bf16[64,2048]{1,0:T(8,128)(2,1)S(1)}, bf16[64,2048]{1,0:T(8,128)(2,1)S(1)}, u32[]{:S(2)}, u32[]{:S(2)}) collective-permute-start(bf16[64,2048]{1,0:T(8,128)(2,1)S(1)} %get-tuple-element.221), channel_id=1, source_target_pairs={{0,32},{16,48},{32,0},{48,16},{1,33},{17,49},{33,1},{49,17},{2,34}... | collective-permute-start | bytes 786440 | tf_op jit(solution)/shard_map/ppermute | solution.py:326
  518.6 287.8 %reduce-scatter.9.cloned.1.call-start = ((), (), s32[]{:S(2)}) async-start(), calls=%async_computation.11 | async-start | bytes 10166272
  531.2 356.0 %reduce-scatter.7.cloned.1.call-start = ((), (), s32[]{:S(2)}) async-start(), calls=%async_computation.10 | async-start | bytes 4595712
  574.4 12.7 %collective-permute-start.79 = (bf16[64,2048]{1,0:T(8,128)(2,1)S(1)}, bf16[64,2048]{1,0:T(8,128)(2,1)}, u32[]{:S(2)}, u32[]{:S(2)}) collective-permute-start(bf16[64,2048]{1,0:T(8,128)(2,1)S(1)} %get-tuple-element.218), channel_id=1, source_target_pairs={{0,32},{16,48},{32,0},{48,16},{1,33},{17,49},{33,1},{49,17},{2,34}... | collective-permute-start | bytes 786440 | tf_op jit(solution)/shard_map/ppermute | solution.py:326
  618.7 13.2 %collective-permute-start.48 = (bf16[64,2048]{1,0:T(8,128)(2,1)S(1)}, bf16[64,2048]{1,0:T(8,128)(2,1)S(1)}, u32[]{:S(2)}, u32[]{:S(2)}) collective-permute-start(bf16[64,2048]{1,0:T(8,128)(2,1)S(1)} %broadcast_select_fusion.2), channel_id=1, source_target_pairs={{0,64},{64,0},{1,65},{65,1},{2,66},{66,2},{3,67},{67,3},{4,68},{68... | collective-permute-start | bytes 786440 | tf_op jit(solution)/shard_map/ppermute | solution.py:326
  634.7 259.3 %collective-permute-start.81 = (bf16[64,2048]{1,0:T(8,128)(2,1)}, bf16[64,2048]{1,0:T(8,128)(2,1)}, u32[]{:S(2)}, u32[]{:S(2)}) collective-permute-start(bf16[64,2048]{1,0:T(8,128)(2,1)} %fusion.17), channel_id=1, source_target_pairs={{0,64},{64,0},{1,65},{65,1},{2,66},{66,2},{3,67},{67,3},{4,68},{68... | collective-permute-start | bytes 786440 | tf_op jit(solution)/shard_map/ppermute | solution.py:326
  809.3 95.3 %collective-permute-start.83 = (bf16[1168,256]{1,0:T(8,128)(2,1)}, bf16[1168,256]{1,0:T(8,128)(2,1)}, u32[]{:S(2)}, u32[]{:S(2)}) collective-permute-start(bf16[1168,256]{1,0:T(8,128)(2,1)} %select_bitcast_fusion), channel_id=1, source_target_pairs={{0,64},{64,0},{1,65},{65,1},{2,66},{66,2},{3,67},{67,3},{4,68},{68... | collective-permute-start | bytes 1794056 | tf_op jit(solution)/shard_map/ppermute | solution.py:326
  899.6 14.2 %collective-permute-start.84 = (bf16[256,256]{1,0:T(8,128)(2,1)S(1)}, bf16[256,256]{1,0:T(8,128)(2,1)S(1)}, u32[]{:S(2)}, u32[]{:S(2)}) collective-permute-start(bf16[256,256]{1,0:T(8,128)(2,1)S(1)} %slice.496), channel_id=1, source_target_pairs={{0,0},{1,8},{8,1},{9,9},{2,2},{3,10},{10,3},{11,11},{4,4},{5,12},{... | collective-permute-start | bytes 393224 | tf_op jit(solution)/shard_map/ppermute | solution.py:354
  922.8 15.5 %collective-permute-start.85 = (bf16[768,256]{1,0:T(8,128)(2,1)S(1)}, bf16[768,256]{1,0:T(8,128)(2,1)S(1)}, u32[]{:S(2)}, u32[]{:S(2)}) collective-permute-start(bf16[768,256]{1,0:T(8,128)(2,1)S(1)} %pad_maximum_fusion.13), channel_id=1, source_target_pairs={{0,0},{1,8},{8,1},{9,9},{2,2},{3,10},{10,3},{11,11},{4,4},{5,12},{... | collective-permute-start | bytes 1179656 | tf_op jit(solution)/shard_map/ppermute | solution.py:354
  929.9 16.9 %all-to-all-start.4 = ((bf16[8,6,32,256]{3,2,1,0:T(8,128)(2,1)}), bf16[8,6,32,256]{3,2,1,0:T(8,128)(2,1)S(1)}, u32[]{:S(2)}, u32[]{:S(2)}) async-start(bf16[8,6,32,256]{3,2,1,0:T(8,128)(2,1)} %copy.330), calls=%async_computation.4 | async-start | bytes 1572864 | tf_op jit(solution)/shard_map/all_to_all | solution.py:358
  (103 other events, 957.8 us)
Sparse Core Ops, SparseCore 0:
  25.1 73.0 all-gather.2
  100.9 121.9 all-gather.4
  518.7 197.2 all-reduce.12
  719.7 86.6 reduce-scatter.8
  809.6 77.5 reduce-scatter.6

commit v2 on v1

v2 whole, which is shorter than its diff:
```python
import functools
import math

import jax
import jax.numpy as jnp
import numpy as np
from jax import lax
from jax.experimental import pallas as pl
from jax.experimental.pallas import tpu as pltpu
from jax.sharding import Mesh
from jax.sharding import PartitionSpec as P

D = 2048
HEAD_DIM = 64
ROT = 16
FF = 5632
EPSILON = 1e-05
NEG_FILL = -1e30
TILE = 256
BLOCKS = D // TILE
ROWS = 64
GROUP = 8 * ROWS
HALF = GROUP // 2
PIECE = 88
PADDED = 96
WIDE = 8 * PADDED
DOWN = 4 * PADDED
VEC = 16
ATTN = 2 * TILE
FEED = 3 * TILE + DOWN
LAYER = ATTN + FEED
SUMS = LAYER + 2 * VEC
VMEM = 40 * 1024 * 1024
F32 = jnp.float32
BF16 = jnp.bfloat16

GRID = ("section", "x", "y", "z", "core")
DP = ("x", "y", "z", "core")
RING = ("section", "y")
SPREAD = ("section", "y", "z")


def dot(a, b):
    return jnp.dot(a, b, preferred_element_type=F32)


def dot_nt(a, b):
    return lax.dot_general(a, b, (((1,), (1,)), ((), ())), preferred_element_type=F32)


def dot_tn(a, b):
    return lax.dot_general(a, b, (((0,), (0,)), ((), ())), preferred_element_type=F32)


def shape_of(*dims, dtype=BF16):
    return jax.ShapeDtypeStruct(dims, dtype)


def in_vmem():
    return pl.BlockSpec(memory_space=pltpu.VMEM)


def in_hbm():
    return pl.BlockSpec(memory_space=pltpu.HBM)


def without(kernel, place):
    def run(*refs):
        kernel(*refs[:place], *refs[place + 1 :])

    return run


def call(kernel, args, outs, *, flops, hbm=0, scratch=(), in_place=False, stay=0, to_hbm=False, after=None):
    stay = len(outs) if stay == 0 else stay
    kept = [pltpu.VMEM(o.shape, o.dtype) for o in outs[stay:]]
    scratch = [*scratch, *kept]
    if kept:
        scratch.append(pltpu.SemaphoreType.DMA((len(kept),)))
    moved = sum(math.prod(o.shape) * o.dtype.itemsize for o in outs)
    moved += sum(math.prod(a.shape) * a.dtype.itemsize for a in args)
    in_specs = [in_hbm() if k < hbm else in_vmem() for k in range(len(args))]
    if after is not None:
        kernel = without(kernel, len(args))
        args = (*args, after)
        in_specs.append(in_hbm())
    return pl.pallas_call(
        kernel,
        in_specs=in_specs,
        out_specs=[in_hbm() if to_hbm or k >= stay else in_vmem() for k in range(len(outs))],
        out_shape=outs,
        scratch_shapes=scratch,
        input_output_aliases={0: 0} if in_place else {},
        compiler_params=pltpu.CompilerParams(vmem_limit_bytes=VMEM),
        cost_estimate=pl.CostEstimate(flops=flops, bytes_accessed=min(moved, 16 * 1024 * 1024), transcendentals=0),
    )(*args)


def rows_of(refs):
    return jnp.concatenate([r[...] for r in refs], axis=0)


class Kept:
    def __init__(self, targets, refs):
        self.targets, self.held, self.sems = targets, refs[:-1], refs[-1]
        self.copies = []

    def send(self, k):
        copy = pltpu.make_async_copy(self.held[k], self.targets[k], self.sems.at[k])
        copy.start()
        self.copies.append(copy)

    def wait(self):
        for copy in self.copies:
            copy.wait()


class Weights:
    def __init__(self, source, held, sems, pieces):
        self.held = held
        self.copies = []
        for k, (half, row, count, to) in enumerate(pieces):
            copy = pltpu.make_async_copy(
                source.at[half, :, row : row + count, :], held.at[:, to : to + count, :], sems.at[k]
            )
            copy.start()
            self.copies.append(copy)

    def wait(self, k):
        self.copies[k].wait()

    def tile(self, row, count=TILE):
        return self.held[:, row : row + count, :].reshape(BLOCKS * count, TILE)

    def block(self, b, row):
        return self.held[b, row : row + TILE, :]


def lane_head(width, of):
    lane = lax.broadcasted_iota(jnp.int32, (128, TILE), 1)
    return (lane // width) % 4 == of


def stacked(array, width):
    zero = jnp.zeros((), array.dtype)
    return jnp.concatenate([jnp.where(lane_head(width, h), array, zero) for h in range(4)], axis=0)


def unstacked(array, width):
    out = jnp.where(lane_head(width, 0), array[:128], 0.0)
    for h in range(1, 4):
        out = jnp.where(lane_head(width, h), array[128 * h : 128 * (h + 1)], out)
    return out


def twisted(u, table_ref, sign):
    def wide(k):
        t = table_ref[k]
        return jnp.concatenate([t, t], axis=1)

    n = u.shape[1]
    half = ROT // 2
    side = pltpu.roll(u, n - half, 1) * wide(1) + pltpu.roll(u, half, 1) * wide(2)
    return u * wide(0) + (side if sign > 0 else -side)


def probabilities(qs, k, mask):
    s = dot_nt(qs, k) * HEAD_DIM**-0.5
    s = jnp.where(jnp.concatenate([mask] * 4, axis=0) > 0, s, NEG_FILL)
    e = jnp.exp(s - jnp.max(s, axis=1, keepdims=True))
    return e / jnp.sum(e, axis=1, keepdims=True)


def put_halves(a_ref, b_ref, j, part):
    part = part.astype(BF16)
    a_ref[:, TILE * j : TILE * (j + 1)] = part[:HALF]
    b_ref[:, TILE * j : TILE * (j + 1)] = part[HALF:]


def attention_kernel(w_ref, *refs):
    n_refs, (bias_ref, table_ref, mask_ref, pa_ref, pb_ref), refs = refs[:8], refs[8:13], refs[13:]
    targets, held, sems, kept = refs[:5], refs[5], refs[6], Kept(refs[:5], refs[7:])
    weights = Weights(w_ref, held, sems, [(t // 2, TILE * (t % 2), TILE, TILE * t) for t in range(4)])
    n_ref, q_ref, k_ref, v_ref, o_ref = kept.held
    n = rows_of(n_refs)
    n_ref[...] = n
    kept.send(0)
    for j, ref in enumerate((q_ref, k_ref, v_ref)):
        weights.wait(j)
        u = dot(n, weights.tile(TILE * j)) + bias_ref[j : j + 1, :]
        ref[...] = (twisted(u, table_ref, 1) if j < 2 else u).astype(BF16)
        kept.send(1 + j)
    for g in range(GROUP // 128):
        rows = slice(128 * g, 128 * g + 128)
        p = probabilities(stacked(q_ref[rows, :], HEAD_DIM), k_ref[rows, :], mask_ref[rows, :])
        o_ref[rows, :] = unstacked(dot(p.astype(BF16), v_ref[rows, :]), 32).astype(BF16)
    kept.send(4)
    o = o_ref[...]
    weights.wait(3)
    for j in range(BLOCKS):
        put_halves(pa_ref, pb_ref, j, dot(o, weights.tile(3 * TILE + 32 * j, 32)))
    kept.wait()


def attention(after, weights, blocks, bias, table, mask):
    return call(
        attention_kernel,
        (weights, *blocks, bias, table, mask),
        [shape_of(HALF, D), shape_of(HALF, D), shape_of(GROUP, D)] + [shape_of(GROUP, TILE)] * 4,
        hbm=1,
        stay=2,
        after=after,
        flops=2 * GROUP * D * 4 * TILE,
        scratch=[pltpu.VMEM((BLOCKS, 4 * TILE, TILE), BF16), pltpu.SemaphoreType.DMA((4,))],
    )


def feed_pieces():
    first = []
    for j in range(3):
        first.append((0, ATTN + TILE * j, TILE, TILE * j))
        first.append((1, ATTN + TILE * j, TILE, TILE * (3 + j)))
    last = [(h, ATTN + 3 * TILE, 4 * PADDED, 6 * TILE + 4 * PADDED * h) for h in range(2)]
    return first, last


FEED_SCRATCH = (BLOCKS, 9 * TILE, TILE)


def feed_kernel(w_ref, *refs):
    n_refs, (pa_ref, pb_ref), refs = refs[:8], refs[8:10], refs[10:]
    held, sems, kept = refs[4], refs[5], Kept(refs[:4], refs[6:])
    first, last = feed_pieces()
    weights = Weights(w_ref, held, sems, first + last)
    n_ref, g_ref, u_ref, act_ref = kept.held
    n = rows_of(n_refs)
    n_ref[...] = n
    kept.send(0)
    for j in range(3):
        lanes = slice(TILE * j, TILE * (j + 1))
        weights.wait(2 * j)
        g = dot(n, weights.tile(TILE * j))
        weights.wait(2 * j + 1)
        u = dot(n, weights.tile(TILE * (3 + j)))
        g_ref[:, lanes] = g
        u_ref[:, lanes] = u
        act_ref[:, lanes] = (g * jax.nn.sigmoid(g) * u).astype(BF16)
    for k in range(1, 4):
        kept.send(k)
    act = act_ref[...]
    for j in range(BLOCKS):
        if j % 4 == 0:
            weights.wait(6 + j // 4)
        put_halves(pa_ref, pb_ref, j, dot(act, weights.tile(6 * TILE + PADDED * j, PADDED)))
    kept.wait()


def feed(after, weights, blocks):
    return call(
        feed_kernel,
        (weights, *blocks),
        [shape_of(HALF, D), shape_of(HALF, D), shape_of(GROUP, D)]
        + [shape_of(GROUP, WIDE, dtype=F32)] * 2
        + [shape_of(GROUP, WIDE)],
        hbm=1,
        stay=2,
        after=after,
        flops=2 * GROUP * D * 9 * TILE,
        scratch=[pltpu.VMEM(FEED_SCRATCH, BF16), pltpu.SemaphoreType.DMA((8,))],
    )


def feed_back_kernel(w_ref, *refs):
    m_refs, (g_ref, u_ref, ea_ref, eb_ref), refs = refs[:8], refs[8:12], refs[12:]
    held, sems, kept = refs[3], refs[4], Kept(refs[:3], refs[5:])
    first, last = feed_pieces()
    weights = Weights(w_ref, held, sems, last + first)
    m_ref, dg_ref, du_ref = kept.held
    gm = rows_of(m_refs)
    m_ref[...] = gm
    kept.send(0)
    da = jnp.zeros((GROUP, WIDE), F32)
    for j in range(BLOCKS):
        if j % 4 == 0:
            weights.wait(j // 4)
        da += dot_nt(gm[:, TILE * j : TILE * (j + 1)], weights.tile(6 * TILE + PADDED * j, PADDED))
    g = g_ref[...]
    u = u_ref[...]
    sigma = jax.nn.sigmoid(g)
    dg_ref[...] = (da * u * sigma * (1.0 + g * (1.0 - sigma))).astype(BF16)
    du_ref[...] = (da * g * sigma).astype(BF16)
    kept.send(1)
    kept.send(2)
    dg = dg_ref[...]
    du = du_ref[...]
    for k in range(6):
        weights.wait(2 + k)
    for b in range(BLOCKS):
        e = jnp.zeros((GROUP, TILE), F32)
        for j in range(3):
            lanes = slice(TILE * j, TILE * (j + 1))
            e += dot_nt(dg[:, lanes], weights.block(b, TILE * j))
            e += dot_nt(du[:, lanes], weights.block(b, TILE * (3 + j)))
        put_halves(ea_ref, eb_ref, b, e)
    kept.wait()


def feed_back(after, weights, blocks, g, u):
    return call(
        feed_back_kernel,
        (weights, *blocks, g, u),
        [shape_of(HALF, D), shape_of(HALF, D), shape_of(GROUP, D)] + [shape_of(GROUP, WIDE)] * 2,
        hbm=1,
        stay=2,
        after=after,
        flops=2 * GROUP * D * 9 * TILE,
        scratch=[pltpu.VMEM(FEED_SCRATCH, BF16), pltpu.SemaphoreType.DMA((8,))],
    )


def attention_back_kernel(w_ref, *refs):
    d_refs = refs[:8]
    q_ref, k_ref, v_ref, table_ref, mask_ref, ea_ref, eb_ref, sum_ref, *refs = refs[8:]
    held, sems, kept = refs[4], refs[5], Kept(refs[:4], refs[6:])
    d_ref, dq_ref, dk_ref, dv_ref = kept.held
    order = (3, 0, 1, 2)
    weights = Weights(w_ref, held, sems, [(t // 2, TILE * (t % 2), TILE, TILE * t) for t in order])
    dattn = rows_of(d_refs)
    d_ref[...] = dattn
    kept.send(0)
    weights.wait(0)
    do = jnp.zeros((GROUP, TILE), F32)
    for j in range(BLOCKS):
        do += dot_nt(dattn[:, TILE * j : TILE * (j + 1)], weights.tile(3 * TILE + 32 * j, 32))
    do = do.astype(BF16)
    dqs, dks = [], []
    for g in range(GROUP // 128):
        rows = slice(128 * g, 128 * g + 128)
        qs = stacked(q_ref[rows, :], HEAD_DIM)
        k = k_ref[rows, :]
        p = probabilities(qs, k, mask_ref[rows, :])
        dos = stacked(do[rows], 32)
        dp = dot_nt(dos, v_ref[rows, :])
        ds = (p * (dp - jnp.sum(p * dp, axis=1, keepdims=True))).astype(BF16)
        dv_ref[rows, :] = dot_tn(p.astype(BF16), dos).astype(BF16)
        dqs.append(unstacked(dot(ds, k), HEAD_DIM))
        dks.append(dot_tn(ds, qs))
    factor = HEAD_DIM**-0.5
    dq_ref[...] = twisted(jnp.concatenate(dqs, axis=0) * factor, table_ref, -1).astype(BF16)
    dk_ref[...] = twisted(jnp.concatenate(dks, axis=0) * factor, table_ref, -1).astype(BF16)
    for k in range(1, 4):
        kept.send(k)
    parts = (dq_ref[...], dk_ref[...], dv_ref[...])
    sums = [jnp.sum(part.astype(F32), axis=0, keepdims=True) for part in parts]
    sum_ref[...] = jnp.concatenate(sums + [jnp.zeros((5, TILE), F32)], axis=0)
    for j in range(3):
        weights.wait(1 + j)
    for b in range(BLOCKS):
        e = jnp.zeros((GROUP, TILE), F32)
        for j in range(3):
            e += dot_nt(parts[j], weights.block(b, TILE * j))
        put_halves(ea_ref, eb_ref, b, e)
    kept.wait()


def attention_back(after, weights, blocks, q, k, v, table, mask):
    return call(
        attention_back_kernel,
        (weights, *blocks, q, k, v, table, mask),
        [shape_of(HALF, D), shape_of(HALF, D), shape_of(8, TILE, dtype=F32), shape_of(GROUP, D)]
        + [shape_of(GROUP, TILE)] * 3,
        hbm=1,
        stay=3,
        after=after,
        flops=2 * GROUP * D * 4 * TILE,
        scratch=[pltpu.VMEM((BLOCKS, 4 * TILE, TILE), BF16), pltpu.SemaphoreType.DMA((4,))],
    )


def send_out(copies, source, target, sem):
    copy = pltpu.make_async_copy(source, target, sem)
    copy.start()
    copies.append(copy)


def feed_grads_kernel(row, *refs):
    n, dg, du, act, gm = [ref[...] for ref in refs[:5]]
    vec_ref, out_ref, held, sems = refs[5:]
    copies = []
    for b in range(BLOCKS):
        left = n[:, TILE * b : TILE * (b + 1)]
        for half, right in enumerate((dg, du)):
            for j in range(3):
                lanes = slice(TILE * j, TILE * (j + 1))
                held[half, b, lanes, :] = dot_tn(left, right[:, lanes]).astype(BF16)
    for j in range(BLOCKS):
        half, k = divmod(j, 4)
        part = dot_tn(act, gm[:, TILE * j : TILE * (j + 1)]).astype(BF16)
        at = 3 * TILE + PADDED * k
        held[half, :, at : at + PADDED, :] = part.reshape(BLOCKS, PADDED, TILE)
    send_out(copies, held, out_ref.at[:, :, row : row + FEED, :], sems.at[0])
    send_out(copies, vec_ref, out_ref.at[:, :, row + FEED : row + FEED + VEC, :], sems.at[1])
    for copy in copies:
        copy.wait()


def feed_grads(after, n, dg, du, act, gm, vec):
    return call(
        functools.partial(feed_grads_kernel, 0),
        (n, dg, du, act, gm, vec),
        [shape_of(2, BLOCKS, SUMS, TILE)],
        after=after,
        flops=2 * GROUP * D * 9 * TILE,
        scratch=[pltpu.VMEM((2, BLOCKS, FEED, TILE), BF16), pltpu.SemaphoreType.DMA((2,))],
        to_hbm=True,
    )[0]


def attention_grads_kernel(row, *refs):
    n, dattn, o, dq, dk, dv = [ref[...] for ref in refs[:6]]
    vec_ref, out_ref, held, sems = refs[6:]
    copies = []
    for b in range(BLOCKS):
        left = n[:, TILE * b : TILE * (b + 1)]
        for j, right in enumerate((dq, dk, dv)):
            half, at = divmod(TILE * j, ATTN)
            held[half, b, at : at + TILE, :] = dot_tn(left, right).astype(BF16)
    for j in range(BLOCKS):
        part = dot_tn(o, dattn[:, TILE * j : TILE * (j + 1)]).astype(BF16)
        held[1, :, TILE + 32 * j : TILE + 32 * (j + 1), :] = part.reshape(BLOCKS, 32, TILE)
    send_out(copies, held, out_ref.at[:, :, row : row + ATTN, :], sems.at[0])
    send_out(copies, vec_ref, out_ref.at[:, :, row + ATTN : row + ATTN + VEC, :], sems.at[1])
    for copy in copies:
        copy.wait()


def attention_grads(after, sums, n, dattn, o, dq, dk, dv, vec):
    return call(
        without(functools.partial(attention_grads_kernel, FEED + VEC), 0),
        (sums, n, dattn, o, dq, dk, dv, vec),
        [shape_of(2, BLOCKS, SUMS, TILE)],
        hbm=1,
        in_place=True,
        after=after,
        flops=2 * GROUP * D * 4 * TILE,
        scratch=[pltpu.VMEM((2, BLOCKS, ATTN, TILE), BF16), pltpu.SemaphoreType.DMA((2,))],
        to_hbm=True,
    )[0]


def add_kernel(a_ref, b_ref, first_ref, *refs):
    for k, ref in enumerate((first_ref, *refs)):
        rows = slice(ROWS * k, ROWS * (k + 1))
        ref[...] = (a_ref[rows, :].astype(F32) + b_ref[rows, :].astype(F32)).astype(ref.dtype)


def added(after, a, b):
    return call(
        add_kernel,
        (a, b),
        [shape_of(ROWS, D, dtype=F32)] + [shape_of(ROWS, D)] * 3,
        flops=HALF * D,
        after=after,
    )


def total_of(refs):
    total = refs[0][...]
    for ref in refs[1:]:
        total = total + ref[...].astype(F32)
    return total


def unit_of(values):
    mean = jnp.mean(values, axis=-1, keepdims=True)
    centred = values - mean
    scale = lax.rsqrt(jnp.mean(centred * centred, axis=-1, keepdims=True) + EPSILON)
    return centred * scale, scale


def norm_kernel(base_ref, *refs):
    parts, (gain_ref, out_ref, n_ref) = refs[:4], refs[4:]
    out = (base_ref[...].astype(F32) + total_of(parts)).astype(out_ref.dtype)
    out_ref[...] = out
    unit, _ = unit_of(out.astype(F32))
    n_ref[...] = (unit * gain_ref[0:1, :] + gain_ref[1:2, :]).astype(BF16)


def normed(after, base, parts, gain, dtype):
    return call(
        norm_kernel,
        (base, *parts, gain),
        [shape_of(ROWS, D, dtype=dtype), shape_of(ROWS, D)],
        flops=16 * ROWS * D,
        after=after,
    )


def norm_back_kernel(up_ref, *refs):
    parts, (values_ref, gain_ref, grad_ref, low_ref, sum_ref) = refs[:4], refs[4:]
    e = total_of(parts)
    unit, scale = unit_of(values_ref[...].astype(F32))
    q = e * gain_ref[0:1, :]
    back = scale * (q - jnp.mean(q, axis=-1, keepdims=True) - unit * jnp.mean(q * unit, axis=-1, keepdims=True))
    grad = up_ref[...].astype(F32) + back
    grad_ref[...] = grad
    low_ref[...] = grad.astype(BF16)
    sums = [jnp.sum(e * unit, axis=0, keepdims=True), jnp.sum(e, axis=0, keepdims=True)]
    sum_ref[...] = jnp.concatenate(sums + [jnp.zeros((6, D), F32)], axis=0)


def normed_back(after, up, parts, values, gain):
    return call(
        norm_back_kernel,
        (up, *parts, values, gain),
        [shape_of(ROWS, D, dtype=F32), shape_of(ROWS, D), shape_of(8, D, dtype=F32)],
        flops=32 * ROWS * D,
        after=after,
    )


def feed_both_kernel(w_ref, *refs):
    n_refs, m_refs = refs[:8], refs[8:16]
    pa_ref, pb_ref, ea_ref, eb_ref, *refs = refs[16:]
    held, sems, kept = refs[5], refs[6], Kept(refs[:5], refs[7:])
    n_ref, m_ref, act_ref, dg_ref, du_ref = kept.held
    first, last = feed_pieces()
    weights = Weights(w_ref, held, sems, last + first)
    n = rows_of(n_refs)
    gm = rows_of(m_refs)
    n_ref[...] = n
    m_ref[...] = gm
    kept.send(0)
    kept.send(1)
    weights.wait(0)
    weights.wait(1)
    for j in range(3):
        lanes = slice(TILE * j, TILE * (j + 1))
        weights.wait(2 + 2 * j)
        g = dot(n, weights.tile(TILE * j))
        weights.wait(3 + 2 * j)
        u = dot(n, weights.tile(TILE * (3 + j)))
        da = jnp.zeros((GROUP, TILE), F32)
        for b in range(BLOCKS):
            w = weights.tile(6 * TILE + PADDED * b, PADDED)[lanes]
            da += dot_nt(gm[:, TILE * b : TILE * (b + 1)], w)
        sigma = jax.nn.sigmoid(g)
        act_ref[:, lanes] = (g * sigma * u).astype(BF16)
        dg_ref[:, lanes] = (da * u * sigma * (1.0 + g * (1.0 - sigma))).astype(BF16)
        du_ref[:, lanes] = (da * g * sigma).astype(BF16)
    for k in range(2, 5):
        kept.send(k)
    act = act_ref[...]
    dg = dg_ref[...]
    du = du_ref[...]
    for b in range(BLOCKS):
        e = jnp.zeros((GROUP, TILE), F32)
        for j in range(3):
            lanes = slice(TILE * j, TILE * (j + 1))
            e += dot_nt(dg[:, lanes], weights.block(b, TILE * j))
            e += dot_nt(du[:, lanes], weights.block(b, TILE * (3 + j)))
        put_halves(ea_ref, eb_ref, b, e)
        put_halves(pa_ref, pb_ref, b, dot(act, weights.tile(6 * TILE + PADDED * b, PADDED)))
    kept.wait()


def feed_both(after, weights, blocks, top):
    return call(
        feed_both_kernel,
        (weights, *blocks, *top),
        [shape_of(HALF, D)] * 4 + [shape_of(GROUP, D)] * 2 + [shape_of(GROUP, WIDE)] * 3,
        hbm=1,
        stay=4,
        after=after,
        flops=4 * GROUP * D * 9 * TILE,
        scratch=[pltpu.VMEM(FEED_SCRATCH, BF16), pltpu.SemaphoreType.DMA((8,))],
    )


def pieces_in_order():
    place = np.zeros((WIDE, 8 * PIECE), np.float32)
    for z in range(4):
        for c in range(2):
            for k in range(PIECE):
                place[(4 * c + z) * PADDED + k, (2 * z + c) * PIECE + k] = 1.0
    return jnp.asarray(place, BF16)


def values_in_order():
    place = np.zeros((TILE, TILE), np.float32)
    for head in range(4):
        for half in range(2):
            for k in range(32):
                place[(half * 4 + head) * 32 + k, (head * 2 + half) * 32 + k] = 1.0
    return jnp.asarray(place, BF16)


def columns_of(ref, b):
    return jnp.concatenate([ref[:, 64 * (8 * x + b) : 64 * (8 * x + b + 1)] for x in range(4)], axis=1)


def pack_kernel(qkv_ref, gate_ref, out_ref, down_ref, places_ref, values_ref, cut_ref, low_ref, high_ref):
    wide = 8 * PIECE
    rows = jnp.concatenate([gate_ref[:, wide * k : wide * (k + 1)] for k in range(16)], axis=0)
    placed = dot_nt(rows, places_ref[...]).astype(BF16)
    values = jnp.concatenate([qkv_ref[:, 2 * D + TILE * t : 2 * D + TILE * (t + 1)] for t in range(8)], axis=0)
    values = dot_nt(values, values_ref[...]).astype(BF16)
    for t in range(8):
        cut_ref[0, t, 0] = qkv_ref[:, TILE * t : TILE * (t + 1)]
        cut_ref[0, t, 1] = qkv_ref[:, D + TILE * t : D + TILE * (t + 1)]
        cut_ref[1, t, 0] = values[32 * t : 32 * (t + 1)]
        cut_ref[1, t, 4] = jnp.zeros((32, TILE), BF16)
        for half in range(2):
            row = 32 * (8 * half + t)
            for j in range(3):
                cut_ref[half, t, 2 - half + j] = placed[row : row + 32, TILE * j : TILE * (j + 1)]
    pad = jnp.zeros((PADDED - PIECE, TILE), BF16)
    for b in range(BLOCKS):
        high_ref[32 * b : 32 * (b + 1), :] = columns_of(out_ref, b)
        down = jnp.concatenate([columns_of(down_ref, b), pad], axis=0)
        row = PADDED * (b % 4)
        if b < 4:
            low_ref[row : row + PADDED, :] = down
        else:
            high_ref[TILE + row : TILE + row + PADDED, :] = down
    low_ref[DOWN:, :] = jnp.zeros((TILE, TILE), BF16)


def packed(qkv_weight, gate_up, out_weight, down_weight):
    return call(
        pack_kernel,
        (qkv_weight, gate_up, out_weight, down_weight, pieces_in_order(), values_in_order()),
        [shape_of(2, 8, 5, 32, TILE), shape_of(DOWN + TILE, TILE), shape_of(DOWN + TILE, TILE)],
        flops=2 * 512 * WIDE * 8 * PIECE,
    )


def put_columns(ref, blocks):
    for x in range(4):
        lanes = slice(64 * x, 64 * (x + 1))
        for k in range(4):
            pair = jnp.concatenate([blocks[2 * k][:, lanes], blocks[2 * k + 1][:, lanes]], axis=1)
            ref[:, 128 * (4 * x + k) : 128 * (4 * x + k + 1)] = pair.astype(F32)


def unpack_kernel(cut_ref, first_ref, second_ref, places_ref, values_ref, qkv_ref, gate_ref, out_ref, down_ref, vec_ref):
    wide = 8 * PIECE
    vec = jnp.zeros((8, TILE), F32)
    for t in range(8):
        qkv_ref[:, TILE * t : TILE * (t + 1)] = cut_ref[0, t, 0].astype(F32)
        qkv_ref[:, D + TILE * t : D + TILE * (t + 1)] = cut_ref[0, t, 1].astype(F32)
        qkv_ref[:, 2 * D + TILE * t : 2 * D + TILE * (t + 1)] = dot(cut_ref[1, t, 0], values_ref[...])
        vec += cut_ref[1, t, 4].astype(F32)[:8]
    vec_ref[...] = vec
    rows = [
        jnp.concatenate([cut_ref[half, t, 2 - half + j] for j in range(3)], axis=1) for half in range(2) for t in range(8)
    ]
    placed = dot(jnp.concatenate(rows, axis=0), places_ref[...])
    for k in range(16):
        gate_ref[:, wide * k : wide * (k + 1)] = placed[32 * k : 32 * (k + 1)]
    put_columns(out_ref, [second_ref[32 * b : 32 * (b + 1), :] for b in range(BLOCKS)])
    down = []
    for b in range(BLOCKS):
        row = PADDED * (b % 4)
        part = first_ref[row : row + PADDED, :] if b < 4 else second_ref[TILE + row : TILE + row + PADDED, :]
        down.append(part.astype(F32)[:PIECE])
    put_columns(down_ref, down)


def unpacked(cut, first, second):
    return call(
        unpack_kernel,
        (cut, first, second, pieces_in_order(), values_in_order()),
        [
            shape_of(32, 3 * D, dtype=F32),
            shape_of(32, 2 * FF, dtype=F32),
            shape_of(32, D, dtype=F32),
            shape_of(PIECE, D, dtype=F32),
            shape_of(8, TILE, dtype=F32),
        ],
        flops=2 * 512 * WIDE * 8 * PIECE,
    )


def turned(block, axis, step):
    n = math.prod(lax.axis_size(a) for a in (axis if isinstance(axis, tuple) else (axis,)))
    return lax.ppermute(block, axis, [(i, (i - step) % n) for i in range(n)])


def in_order(block, axis, n):
    ahead = jnp.stack([block] + [turned(block, axis, k) for k in range(1, n)])
    return jnp.roll(ahead, lax.axis_index(axis), axis=0)


def gathered_rows(block):
    own = [block] + [turned(block, "x", k) for k in range(1, 4)]
    return own + [turned(part, "core", 1) for part in own]


def summed_parts(after, part_a, part_b):
    first, *rest = added(after, part_a, turned(part_b, "core", 1))
    return [first] + [turned(block, "x", -k) for k, block in enumerate(rest, 1)]


def swapped(block, step):
    pairs = []
    for k in range(2):
        for y in range(2):
            for c in range(2):
                pairs.append((4 * k + 2 * y + c, 4 * ((k + step) % 2) + 2 * c + y))
    return lax.ppermute(block, ("section", "y", "core"), pairs)


def spread(block):
    return lax.all_to_all(block, ("section", "x", "core"), 0, 0, tiled=True)


def scattered(array):
    array = array.reshape(16, -1, TILE)
    return lax.optimization_barrier(lax.psum_scatter(array, SPREAD, scatter_dimension=0, tiled=False))


def to_stored(rows):
    shape = rows.shape[:-1]
    k = len(shape)
    cut = rows.reshape(*shape, 4, 8, 64)
    return jnp.swapaxes(cut, k, k + 1).reshape(*shape, D)


def from_stored(rows):
    shape = rows.shape[:-1]
    k = len(shape)
    cut = rows.reshape(*shape, 8, 4, 64)
    return jnp.swapaxes(cut, k, k + 1).reshape(*shape, D)


def value_columns(cut):
    shape = cut.shape[:-1]
    k = len(shape)
    return jnp.swapaxes(cut.reshape(*shape, 4, 2, 32), k, k + 1).reshape(*shape, TILE)


def value_columns_back(cut):
    shape = cut.shape[:-1]
    k = len(shape)
    return jnp.swapaxes(cut.reshape(*shape, 2, 4, 32), k, k + 1).reshape(*shape, TILE)


def both_layers(qkv_weight, out_weight, gate_up, down_weight):
    section = lax.axis_index("section")
    cut, low, high = packed(qkv_weight, gate_up, out_weight, down_weight)
    cut = spread(cut.reshape(16, 5, 32, TILE))
    cut = cut.reshape(2, 8, 5, 32, TILE).transpose(0, 2, 1, 3, 4).reshape(2, 5 * TILE, TILE)
    kept = swapped(jnp.where(section == 0, low, high), 0)
    sent = swapped(jnp.where(section == 0, high, low), 1)
    parts = []
    for layer in range(2):
        rows = jnp.where(section == layer, kept, sent)
        low = jnp.concatenate([cut[layer], rows[:DOWN]], axis=0)
        high = jnp.concatenate([cut[layer, :TILE], rows[:TILE], cut[layer, TILE : 4 * TILE], rows[TILE:]], axis=0)
        parts.append(jnp.where(section == 0, low, high))
    return parts


def owned(attn, feed, vecs):
    section = lax.axis_index("section")
    tiles = []
    for layer in range(2):
        low = jnp.concatenate([attn[layer], feed[layer][: 3 * TILE]], axis=0).reshape(5, 8, 32, TILE)
        vec = jnp.pad(jnp.stack(vecs[layer], axis=1), ((0, 0), (0, 30), (0, 0))).reshape(1, 8, 32, TILE)
        high = jnp.concatenate([attn[layer][:TILE], feed[layer][: 3 * TILE]], axis=0).reshape(4, 8, 32, TILE)
        tiles.append(jnp.where(section == 0, low, jnp.concatenate([high, vec], axis=0)))
    cut = spread(jnp.stack(tiles).transpose(0, 2, 1, 3, 4).reshape(16, 5, 32, TILE)).reshape(2, 8, 5, 32, TILE)
    low = [jnp.pad(feed[layer][3 * TILE :], ((0, TILE), (0, 0))) for layer in range(2)]
    high = [jnp.concatenate([attn[layer][TILE:], feed[layer][3 * TILE :]], axis=0) for layer in range(2)]
    kept = swapped(jnp.where(section == 0, low[0], high[1]), 0)
    sent = swapped(jnp.where(section == 0, low[1], high[0]), 1)
    first = jnp.where(section == 0, kept, sent)
    second = jnp.where(section == 0, sent, kept)
    return unpacked(cut, first, second)


def geometry(segments):
    groups = segments.reshape(GROUP // 128, 128)
    index = jnp.arange(128, dtype=jnp.int32)
    block = index // 32
    same = (groups[:, :, None] == groups[:, None, :]) & (block[None, :, None] == block[None, None, :])
    before = index[None, :] < index[:, None]
    places = jnp.sum(jnp.where(same & before, 1.0, 0.0), axis=-1).astype(F32).reshape(GROUP)
    inverse = 10000.0 ** (-(jnp.arange(ROT // 2).astype(F32) * 2.0 / ROT))
    theta = places[:, None] * inverse
    cosine, sine = jnp.cos(theta), jnp.sin(theta)
    rest = HEAD_DIM - ROT
    zero = jnp.zeros((GROUP, ROT // 2), F32)
    straight = jnp.concatenate([cosine, cosine, jnp.ones((GROUP, rest), F32)], axis=1)
    first = jnp.concatenate([-sine, zero, jnp.zeros((GROUP, rest), F32)], axis=1)
    second = jnp.concatenate([zero, sine, jnp.zeros((GROUP, rest), F32)], axis=1)
    table = jnp.stack([jnp.concatenate([t, t], axis=1) for t in (straight, first, second)])
    linked = same & (index[None, :] <= index[:, None])
    return table, jnp.where(linked, 1.0, 0.0).astype(F32).reshape(GROUP, 128)


def vector_rows(*parts):
    cut = jnp.concatenate(parts, axis=2).astype(BF16)
    cut = jnp.pad(cut, ((0, 0), (0, VEC - 8), (0, TILE - cut.shape[2])))
    return jnp.stack([jnp.zeros_like(cut), cut])


def by_owner(vector):
    return vector.reshape(8, 8, 32)


def on_device(
    block_input,
    segment_ids,
    cotangent,
    first_gain,
    first_shift,
    qkv_weight,
    qkv_bias,
    out_weight,
    second_gain,
    second_shift,
    gate_up,
    down_weight,
):
    section = lax.axis_index("section")
    shard = 2 * lax.axis_index("x") + lax.axis_index("core")

    weights = []
    for part in both_layers(qkv_weight[0], out_weight[0], gate_up[0], down_weight[0]):
        full = lax.all_gather(part, SPREAD, axis=0, tiled=True)
        weights.append(full.reshape(2, BLOCKS, LAYER, TILE))

    vectors = jnp.concatenate([first_gain[0], first_shift[0], second_gain[0], second_shift[0], qkv_bias[0]])
    vectors = jnp.pad(vectors, (0, 32)).reshape(1, TILE)
    vectors = in_order(vectors, "core", 2)
    vectors = in_order(vectors, "x", 4)
    vectors = in_order(vectors, "z", 4)
    vectors = in_order(vectors, RING, 4)
    vectors = vectors.reshape(2, 64, TILE).astype(F32)
    gains = [vectors[:, :, 32 * k : 32 * (k + 1)].reshape(2, D) for k in range(4)]
    bias = vectors[:, :, 128:224].reshape(2, 2, 4, 4, 2, 96).transpose(0, 3, 1, 2, 4, 5).reshape(2, 3, 8, TILE)
    bias = lax.dynamic_index_in_dim(bias, shard, 2, keepdims=False)
    bias = jnp.concatenate([bias[:, :2], value_columns(bias[:, 2:])], axis=1)
    bias = jnp.pad(bias, ((0, 0), (0, 5), (0, 0)))

    def own_rows(array):
        return lax.dynamic_slice_in_dim(array, 2 * section, 2, 0)

    rows_in = to_stored(own_rows(block_input).reshape(ROWS, D))
    top_grad = to_stored(own_rows(cotangent).reshape(ROWS, D))
    segments = gathered_rows(own_rows(segment_ids).reshape(1, ROWS))
    tables = geometry(jnp.concatenate(segments, axis=0))
    top = gathered_rows(top_grad)
    first_gains = [jnp.stack([gains[0][layer], gains[1][layer]]) for layer in range(2)]
    second_gains = [jnp.stack([gains[2][layer], gains[3][layer]]) for layer in range(2)]

    outputs = [None, None]
    kept = [{}, {}]
    base = rows_in
    unit, _ = unit_of(base.astype(F32))
    n = (unit * first_gains[0][0:1] + first_gains[0][1:2]).astype(BF16)
    for layer in range(2):
        have = kept[layer]
        part_a, part_b, have["n1"], have["q"], have["k"], have["v"], have["mixed"] = attention(
            None, weights[layer], gathered_rows(n), bias[layer], *tables
        )
        have["values1"] = base
        hidden, n = normed(None, base, summed_parts(None, part_a, part_b), second_gains[layer], F32)
        have["values2"] = hidden
        if layer == 0:
            part_a, part_b, have["n2"], have["g"], have["u"], have["act"] = feed(None, weights[0], gathered_rows(n))
            base, n = normed(None, hidden, summed_parts(None, part_a, part_b), first_gains[1], BF16)
            outputs[0] = base
    part_a, part_b, ea, eb, have["n2"], have["gm"], have["act"], have["dg"], have["du"] = feed_both(
        None, weights[1], gathered_rows(n), top
    )

    def feed_sums(have):
        sums = have["sums2"]
        vec = vector_rows(by_owner(sums[0]), by_owner(sums[1]))
        return feed_grads(None, have["n2"], have["dg"], have["du"], have["act"], have["gm"], vec)

    def attention_sums(have, buffer):
        sums = have["sums1"]
        bias_sum = have["bias_sum"]
        bias_sum = jnp.concatenate([bias_sum[:2], value_columns_back(bias_sum[2:3])], axis=0)
        bias_sum = lax.dynamic_update_slice_in_dim(jnp.zeros((3, 8, TILE), F32), bias_sum[:, None], shard, 1)
        bias_sum = bias_sum.reshape(4, 2, 4, 2, 96).transpose(1, 2, 0, 3, 4).reshape(8, 8, 96)
        vec = vector_rows(by_owner(sums[0]), by_owner(sums[1]), bias_sum)
        names = ("n1", "dattn", "mixed", "dq", "dk", "dv")
        return attention_grads(None, buffer, *(have[name] for name in names), vec)

    grads_in = [None, None]
    up = top_grad
    sums_1 = None
    for layer in (1, 0):
        have = kept[layer]
        if layer == 0:
            ea, eb, have["gm"], have["dg"], have["du"] = feed_back(
                sums_1, weights[0], gathered_rows(up), have["g"], have["u"]
            )
        grad, low, have["sums2"] = normed_back(None, up, summed_parts(None, ea, eb), have["values2"], second_gains[layer])
        buffer = feed_sums(have)
        ea, eb, have["bias_sum"], have["dattn"], have["dq"], have["dk"], have["dv"] = attention_back(
            buffer, weights[layer], gathered_rows(low), have["q"], have["k"], have["v"], *tables
        )
        parts = summed_parts(None, ea, eb)
        grads_in[layer], up, have["sums1"] = normed_back(None, grad, parts, have["values1"], first_gains[layer])
        if layer == 1:
            sums_1 = attention_sums(have, buffer)
    sums_0 = attention_sums(kept[0], buffer)
    first, *rest = summed_parts(sums_0, part_a, part_b)
    total = kept[1]["values2"] + first
    for block in rest:
        total = total + block.astype(F32)
    outputs[1] = total.astype(BF16)

    sum_1 = scattered(sums_1)
    sum_0 = scattered(sums_0)
    feed_0, attn_0 = sum_0[: FEED + VEC], sum_0[FEED + VEC :]
    feed_1, attn_1 = sum_1[: FEED + VEC], sum_1[FEED + VEC :]
    attn = [attn_0[:ATTN], attn_1[:ATTN]]
    feeds = [feed_0[:FEED], feed_1[:FEED]]
    vecs = [(attn_0[ATTN : ATTN + 8], feed_0[FEED : FEED + 8]), (attn_1[ATTN : ATTN + 8], feed_1[FEED : FEED + 8])]
    qkv_grad, gate_up_grad, out_grad, down_grad, small = owned(attn, feeds, vecs)

    def layer_rows(first, second):
        mine = jnp.where(section == 0, first, second)
        other = turned(jnp.where(section == 0, second, first).astype(BF16), "section", 1).astype(first.dtype)
        rows = jnp.where(section == 0, jnp.concatenate([mine, other]), jnp.concatenate([other, mine]))
        return from_stored(rows).reshape(1, 4, 32, D)

    activations = layer_rows(outputs[0], outputs[1])
    input_grads = layer_rows(grads_in[0], upstream_of(grads_in[1]))
    return (
        activations,
        input_grads,
        small[0][None, 0:32],
        small[0][None, 32:64],
        qkv_grad[None],
        small[0][None, 64:160],
        out_grad[None],
        small[1][None, 0:32],
        small[1][None, 32:64],
        gate_up_grad[None],
        down_grad[None],
    )


def upstream_of(grad_rows):
    return grad_rows.astype(BF16).astype(F32)


def solution(mesh):
    grid = Mesh(mesh.devices.reshape(2, 4, 2, 4, 2), GRID)
    return jax.shard_map(
        on_device,
        mesh=grid,
        in_specs=(
            P(None, DP, None),
            P(None, DP),
            P(None, DP, None),
            P("section", DP),
            P("section", DP),
            P("section", DP, None),
            P("section", DP),
            P("section", DP, None),
            P("section", DP),
            P("section", DP),
            P("section", DP, None),
            P("section", DP, None),
        ),
        out_specs=(
            P("section", None, DP, None),
            P("section", None, DP, None),
            P("section", DP),
            P("section", DP),
            P("section", DP, None),
            P("section", DP),
            P("section", DP, None),
            P("section", DP),
            P("section", DP),
            P("section", DP, None),
            P("section", DP, None),
        ),
        check_vma=False,
    )
```

time: 971 us -> 748 us (0.77)
  waiting for transfers between devices: 544 us -> 308 us
  local copies, waits for them, and re-layouts: 54.2 us -> 120 us
  other arithmetic: 64.1 us -> 18.6 us
  Pallas kernels: 141 us -> 119 us
  starting transfers between devices: 142 us -> 156 us
    unnamed x8 -> x6, waiting for transfers between devices: 244 us -> 78.7 us
    unnamed x108 -> x241, local copies, waits for them, and re-layouts: 11.3 us -> 78.7 us
    ppermute x82 -> x107, waiting for transfers between devices: 206 us -> 174 us  [turned(): return lax.ppermute(block, axis, [(i, (i - step) % n) for i in range(n)])]
    all_gather x2, waiting for transfers between devices: 62.5 us -> 34.6 us  [on_device(): full = lax.all_gather(part, SPREAD, axis=0, tiled=True)]
    ppermute x82 -> x107, starting transfers between devices: 105 us -> 132 us  [turned(): return lax.ppermute(block, axis, [(i, (i - step) % n) for i in range(n)])]
    pallas_call x12 -> x28, Pallas kernels: 141 us -> 119 us  [call(): pl.pallas_call(kernel, in_specs=in_specs, out_specs=[in_hbm() if to_hbm o...]
    concatenate x18 -> x6, other arithmetic: 18.7 us -> 0.18 us  [the longest x2 0.09 us: owned(): jnp.concatenate([attn[layer], feed[layer][:3 * TILE]], axis=0)]
    all_to_all x5 -> x2, waiting for transfers between devices: 18.3 us -> 0.01 us  [spread(): return lax.all_to_all(block, ('section', 'x', 'core'), 0, 0, tiled=True)]
  transfers between devices with their start and end apart: 96 -> 117, of which waited for: 65 -> 58; matrix products, arithmetic and copies ran while one was open for 7% -> 8% of each run, Pallas kernels for 7% -> 10%
where the time goes in v2:
time: 748 us; the launch traced here: 737 us
  waiting for transfers between devices  308 us (41%)
  starting transfers between devices  156 us (21%)
  local copies, waits for them, and re-layouts  120 us (16%)
  Pallas kernels  119 us (16%)
  other arithmetic  18.6 us (2%)
  between operations  15.7 us (2%)
    ppermute x107, waiting for transfers between devices, turned(): return lax.ppermute(block, axis, [(i, (i - step) % n) for i in range(n)])  174 us
    ppermute x107, starting transfers between devices, turned(): return lax.ppermute(block, axis, [(i, (i - step) % n) for i in range(n)])  132 us
    pallas_call x28, Pallas kernels, call(): pl.pallas_call(kernel, in_specs=in_specs, out_specs=[in_hbm() if to_hbm o...  119 us
    unnamed x6, waiting for transfers between devices  78.7 us
    unnamed x241, local copies, waits for them, and re-layouts  78.7 us
    all_gather x2, waiting for transfers between devices, on_device(): full = lax.all_gather(part, SPREAD, axis=0, tiled=True)  34.6 us
    ppermute x4, waiting for transfers between devices, swapped(): return lax.ppermute(block, ('section', 'y', 'core'), pairs)  20.4 us
    all_to_all x2, starting transfers between devices, spread(): return lax.all_to_all(block, ('section', 'x', 'core'), 0, 0, tiled=True)  15 us
  transfers between devices with their start and end apart: 117, of which 58 were waited for; matrix products, arithmetic and copies ran while one was open for 8% of the time, Pallas kernels for 10%

profile of v2, /device:TPU:1, one launch (start us, length us, event | category | flops | bytes accessed | tf_op | source)
XLA Modules:
  0.0 736.7 jit_solution(14245506312523966047)
XLA Ops:
  15.3 8.4 %all-to-all-start = ((bf16[16,5,32,256]{3,2,1,0:T(8,128)(2,1)}), bf16[16,5,32,256]{3,2,1,0:T(8,128)(2,1)S(1)}, u32[]{:S(2)}, u32[]{:S(2)}) async-start(bf16[16,5,32,256]{3,2,1,0:T(8,128)(2,1)} %bitcast.5), calls=%async_computation | async-start | bytes 2621440 | tf_op jit(solution)/shard_map/all_to_all | solution.py:715
  29.3 17.4 %collective-permute-done = bf16[640,256]{1,0:T(8,128)(2,1)S(1)} collective-permute-done((bf16[640,256]{1,0:T(8,128)(2,1)S(1)}, bf16[640,256]{1,0:T(8,128)(2,1)S(1)}, u32[]{:S(2)}, u32[]{:S(2)}) %collective-permute-start) | collective-permute-done | bytes 327712 | tf_op jit(solution)/shard_map/ppermute | solution.py:711
  111.8 34.6 %all-gather.3.cloned.1.call-done = bf16[26624,256]{1,0:T(8,128)(2,1)} async-done(((bf16[1664,256]{1,0:T(8,128)(2,1)}), bf16[26624,256]{1,0:T(8,128)(2,1)}) %all-gather.3.cloned.1.call-update) | async-done | bytes 13631504 | tf_op jit(solution)/shard_map/all_gather | solution.py:832
  146.4 8.4 %shard_map.240 = (bf16[256,2048]{1,0:T(8,128)(2,1)S(1)}, bf16[256,2048]{1,0:T(8,128)(2,1)S(1)}, bf16[512,2048]{1,0:T(8,128)(2,1)S(1)}, bf16[512,256]{1,0:T(8,128...) custom-call(bf16[2,8,1664,256]{3,2,1,0:T(8,128)(2,1)} %bitcast.178, ...), custom_call_target="tpu_custom_call" | custom-call | flops 2147483648 | bytes 16777216 | tf_op jit(solution)/shard_map/pallas_call | solution.py:87
  169.0 6.5 collective-permute-done.28.refs_2_
  180.9 8.6 %collective-permute-done.30.refs_1_ = bf16[64,2048]{1,0:T(8,128)(2,1)S(1)} collective-permute-done((bf16[64,2048]{1,0:T(8,128)(2,1)S(1)}, bf16[64,2048]{1,0:T(8,128)(2,1)S(1)}, u32[]{:S(2)}, u32[]{:S(2)}) %collective-permute-start.30) | collective-permute-done | bytes 262176 | tf_op jit(solution)/shard_map/ppermute | solution.py:687
  195.8 11.1 %shard_map.243 = (bf16[256,2048]{1,0:T(8,128)(2,1)S(1)}, bf16[256,2048]{1,0:T(8,128)(2,1)S(1)}, bf16[512,2048]{1,0:T(8,128)(2,1)S(1)}, f32[512,768]{1,0:T(8,128)...) custom-call(bf16[2,8,1664,256]{3,2,1,0:T(8,128)(2,1)} %bitcast.179, ...), custom_call_target="tpu_custom_call" | custom-call | flops 4831838208 | bytes 16777216 | tf_op jit(solution)/shard_map/pallas_call | solution.py:87
  223.9 4.3 collective-permute-done.39.refs_2_
  238.7 6.4 collective-permute-start.45
  254.7 10.5 %shard_map.246 = (bf16[256,2048]{1,0:T(8,128)(2,1)S(1)}, bf16[256,2048]{1,0:T(8,128)(2,1)}, bf16[512,2048]{1,0:T(8,128)(2,1)S(1)}, bf16[512,256]{1,0:T(8,128)(2,...) custom-call(bf16[2,8,1664,256]{3,2,1,0:T(8,128)(2,1)} %bitcast.182, ...), custom_call_target="tpu_custom_call" | custom-call | flops 2147483648 | bytes 16777216 | tf_op jit(solution)/shard_map/pallas_call | solution.py:87
  307.3 8.8 %collective-permute-done.52.refs_1_ = bf16[64,2048]{1,0:T(8,128)(2,1)S(1)} collective-permute-done((bf16[64,2048]{1,0:T(8,128)(2,1)S(1)}, bf16[64,2048]{1,0:T(8,128)(2,1)S(1)}, u32[]{:S(2)}, u32[]{:S(2)}) %collective-permute-start.52) | collective-permute-done | bytes 262176 | tf_op jit(solution)/shard_map/ppermute | solution.py:687
  322.7 17.5 %shard_map.249 = (bf16[256,2048]{1,0:T(8,128)(2,1)S(1)}, bf16[256,2048]{1,0:T(8,128)(2,1)S(1)}, bf16[256,2048]{1,0:T(8,128)(2,1)S(1)}, bf16[256,2048]{1,0:T(8,12...) custom-call(bf16[2,8,1664,256]{3,2,1,0:T(8,128)(2,1)} %bitcast.183, ...), custom_call_target="tpu_custom_call" | custom-call | flops 9663676416 | bytes 16777216 | tf_op jit(solution)/shard_map/pallas_call | solution.py:87
  347.7 11.7 %collective-permute-done.68.refs_1_ = bf16[64,2048]{1,0:T(8,128)(2,1)S(1)} collective-permute-done((bf16[64,2048]{1,0:T(8,128)(2,1)S(1)}, bf16[64,2048]{1,0:T(8,128)(2,1)S(1)}, u32[]{:S(2)}, u32[]{:S(2)}) %collective-permute-start.68) | collective-permute-done | bytes 262176 | tf_op jit(solution)/shard_map/ppermute | solution.py:687
  367.0 4.5 collective-permute-done.71.refs_2_
  371.5 5.5 collective-permute-start.75
  387.2 8.8 %shard_map.252.refs_14_.refs_0_ = bf16[2,8,1696,256]{3,2,1,0:T(8,128)(2,1)} custom-call(bf16[512,2048]{1,0:T(8,128)(2,1)S(1)} %copy-done.11, bf16[512,768]{1,0:T(8,128)(2,1)S(1)} %copy-done.34, bf16[512,768]{1,0:T(8,128)(2,1)S(1)} %copy-done.36, bf16[512,768]{1,0:T(8,128)(2,1)S(1)} %copy-done.32, bf16[512,2048]{1,0:T(8,128)(2,1)S(1)} %copy-done.12, ...), custom_call_target="tpu_custom_call" | custom-call | flops 4831838208 | bytes 16777216 | tf_op jit(solution)/shard_map/pallas_call | solution.py:87
  396.0 8.6 %shard_map.253 = (bf16[256,2048]{1,0:T(8,128)(2,1)S(1)}, bf16[256,2048]{1,0:T(8,128)(2,1)S(1)}, f32[8,256]{1,0:T(8,128)S(1)}, bf16[512,2048]{1,0:T(8,128)(2,1)S(...) custom-call(bf16[2,8,1664,256]{3,2,1,0:T(8,128)(2,1)} %bitcast.184, ...), custom_call_target="tpu_custom_call" | custom-call | flops 2147483648 | bytes 16777216 | tf_op jit(solution)/shard_map/pallas_call | solution.py:87
  413.9 11.3 %collective-permute-done.79.refs_1_ = bf16[64,2048]{1,0:T(8,128)(2,1)S(1)} collective-permute-done((bf16[64,2048]{1,0:T(8,128)(2,1)}, bf16[64,2048]{1,0:T(8,128)(2,1)S(1)}, u32[]{:S(2)}, u32[]{:S(2)}) %collective-permute-start.79) | collective-permute-done | bytes 262176 | tf_op jit(solution)/shard_map/ppermute | solution.py:687
  440.3 4.4 shard_map.256.refs_11_
  448.6 4.3 collective-permute-done.82.refs_2_
  452.9 6.1 collective-permute-start.86
  466.4 8.8 %shard_map.257 = (bf16[256,2048]{1,0:T(8,128)(2,1)S(1)}, bf16[256,2048]{1,0:T(8,128)(2,1)S(1)}, bf16[512,2048]{1,0:T(8,128)(2,1)S(1)}, bf16[512,768]{1,0:T(8,128)(2,1)S(1)}, bf16[512,768]{1,0:T(8,128)(2,1)S(1)}) custom-call(bf16[2,8,1664,256]{3,2,1,0:T(8,128)(2,1)} %bitcast.180, bf16[64,2048]{1,0:T(8,128)(2,1)S(1)} %get-tuple-element.169.refs_1_.up_ref, ...), custom_call_target="tpu_custom_call" | custom-call | flops 4831838208 | bytes 16777216 | tf_op jit(solution)/shard_map/pallas_call | solution.py:87
  481.2 6.7 collective-permute-done.90.refs_1_
  500.3 8.9 %collective-permute-done.93.refs_2_ = bf16[64,2048]{1,0:T(8,128)(2,1)S(1)} collective-permute-done((bf16[64,2048]{1,0:T(8,128)(2,1)}, bf16[64,2048]{1,0:T(8,128)(2,1)S(1)}, u32[]{:S(2)}, u32[]{:S(2)}) %collective-permute-start.93) | collective-permute-done | bytes 262176 | tf_op jit(solution)/shard_map/ppermute | solution.py:687
  520.8 8.8 %shard_map.260.refs_14_.refs_0_ = bf16[2,8,1696,256]{3,2,1,0:T(8,128)(2,1)} custom-call(bf16[512,2048]{1,0:T(8,128)(2,1)S(1)} %copy-done.7, bf16[512,768]{1,0:T(8,128)(2,1)S(1)} %copy-done.38, bf16[512,768]{1,0:T(8,128)(2,1)S(1)} %copy-done.40, bf16[512,768]{1,0:T(8,128)(2,1)S(1)} %copy-done.30, bf16[512,2048]{1,0:T(8,128)(2,1)S(1)} %copy-done.16, ...), custom_call_target="tpu_custom_call" | custom-call | flops 4831838208 | bytes 16777216 | tf_op jit(solution)/shard_map/pallas_call | solution.py:87
  529.7 9.6 %shard_map.261 = (bf16[256,2048]{1,0:T(8,128)(2,1)S(1)}, bf16[256,2048]{1,0:T(8,128)(2,1)}, f32[8,256]{1,0:T(8,128)S(1)}, bf16[512,2048]{1,0:T(8,128)(2,1)S(1)},...) custom-call(bf16[2,8,1664,256]{3,2,1,0:T(8,128)(2,1)} %bitcast.181, ...), custom_call_target="tpu_custom_call" | custom-call | flops 2147483648 | bytes 16777216 | tf_op jit(solution)/shard_map/pallas_call | solution.py:87
  552.9 11.5 %collective-permute-done.101.refs_1_ = bf16[64,2048]{1,0:T(8,128)(2,1)S(1)} collective-permute-done((bf16[64,2048]{1,0:T(8,128)(2,1)}, bf16[64,2048]{1,0:T(8,128)(2,1)S(1)}, u32[]{:S(2)}, u32[]{:S(2)}) %collective-permute-start.101) | collective-permute-done | bytes 262176 | tf_op jit(solution)/shard_map/ppermute | solution.py:687
  574.5 4.4 shard_map.264.refs_2_
  592.0 6.2 collective-permute-done.105
  603.0 78.6 %reduce-scatter.7.cloned.1.call-done = bf16[1,1696,256]{2,1,0:T(8,128)(2,1)} async-done(((bf16[16,1696,256]{2,1,0:T(8,128)(2,1)}), bf16[1,1696,256]{2,1,0:T(8,128)(2,1)}) %reduce-scatter.7.cloned.1.call-update) | async-done | bytes 868368
  687.5 6.5 all-to-all-start.1
  712.8 4.9 collective-permute-done.107
  (643 shorter events, 358.1 us)
Async XLA Ops:
  15.3 33.4 %all-to-all-start = ((bf16[16,5,32,256]{3,2,1,0:T(8,128)(2,1)}), bf16[16,5,32,256]{3,2,1,0:T(8,128)(2,1)S(1)}, u32[]{:S(2)}, u32[]{:S(2)}) async-start(bf16[16,5,32,256]{3,2,1,0:T(8,128)(2,1)} %bitcast.5), calls=%async_computation | async-start | bytes 2621440 | tf_op jit(solution)/shard_map/all_to_all | solution.py:715
  23.8 122.7 %all-gather.3.cloned.1.call-start = ((), (), s32[]{:S(2)}) async-start(), calls=%async_computation.4 | async-start | bytes 14483456 | tf_op jit(solution)/shard_map/all_gather | solution.py:832
  23.9 22.8 %collective-permute-start = (bf16[640,256]{1,0:T(8,128)(2,1)S(1)}, bf16[640,256]{1,0:T(8,128)(2,1)S(1)}, u32[]{:S(2)}, u32[]{:S(2)}) collective-permute-start(bf16[640,256]{1,0:T(8,128)(2,1)S(1)} %get-tuple-element.258), channel_id=1, source_target_pairs={{0,0},{1,8},{8,1},{9,9},{64,64},{65,72},{72,65},{73,73},{2,2},{3,1... | collective-permute-start | bytes 983048 | tf_op jit(solution)/shard_map/ppermute | solution.py:711
  26.2 22.5 %collective-permute-start.1 = (bf16[640,256]{1,0:T(8,128)(2,1)S(1)}, bf16[640,256]{1,0:T(8,128)(2,1)S(1)}, u32[]{:S(2)}, u32[]{:S(2)}) collective-permute-start(bf16[640,256]{1,0:T(8,128)(2,1)S(1)} %get-tuple-element.257), channel_id=1, source_target_pairs={{0,64},{1,72},{8,65},{9,73},{64,0},{65,8},{72,1},{73,9},{2,66},{3,... | collective-permute-start | bytes 983048 | tf_op jit(solution)/shard_map/ppermute | solution.py:711
  50.2 199.3 %all-gather.5.cloned.1.call-start = ((), (), s32[]{:S(2)}) async-start(), calls=%async_computation.5 | async-start | bytes 14483456 | tf_op jit(solution)/shard_map/all_gather | solution.py:832
  51.6 547.6 %reduce-scatter.9.cloned.1.call-start = ((), (), s32[]{:S(2)}) async-start(), calls=%async_computation.7 | async-start | bytes 14761984
  51.7 24.7 %collective-permute-start.19 = (s32[1,64]{1,0:T(1,128)S(1)}, s32[1,64]{1,0:T(1,128)S(1)}, u32[]{:S(2)}, u32[]{:S(2)}) collective-permute-start(s32[1,64]{1,0:T(1,128)S(1)} %reshape.354), channel_id=1, source_target_pairs={{0,48},{16,0},{32,16},{48,32},{1,49},{17,1},{33,17},{49,33},{2,50}... | collective-permute-start | bytes 776 | tf_op jit(solution)/shard_map/ppermute | solution.py:687
  54.1 25.5 %collective-permute-start.20 = (s32[1,64]{1,0:T(1,128)S(1)}, s32[1,64]{1,0:T(1,128)S(1)}, u32[]{:S(2)}, u32[]{:S(2)}) collective-permute-start(s32[1,64]{1,0:T(1,128)S(1)} %reshape.354), channel_id=1, source_target_pairs={{0,32},{16,48},{32,0},{48,16},{1,33},{17,49},{33,1},{49,17},{2,34}... | collective-permute-start | bytes 776 | tf_op jit(solution)/shard_map/ppermute | solution.py:687
  54.7 25.0 %collective-permute-start.21 = (s32[1,64]{1,0:T(1,128)S(1)}, s32[1,64]{1,0:T(1,128)S(1)}, u32[]{:S(2)}, u32[]{:S(2)}) collective-permute-start(s32[1,64]{1,0:T(1,128)S(1)} %reshape.354), channel_id=1, source_target_pairs={{0,16},{16,32},{32,48},{48,0},{1,17},{17,33},{33,49},{49,1},{2,18}... | collective-permute-start | bytes 776 | tf_op jit(solution)/shard_map/ppermute | solution.py:687
  55.3 24.8 %collective-permute-start.22 = (s32[1,64]{1,0:T(1,128)S(1)}, s32[1,64]{1,0:T(1,128)S(1)}, u32[]{:S(2)}, u32[]{:S(2)}) collective-permute-start(s32[1,64]{1,0:T(1,128)S(1)} %reshape.354), channel_id=1, source_target_pairs={{0,1},{1,0},{2,3},{3,2},{4,5},{5,4},{6,7},{7,6},{8,9},{9,8},{10,11... | collective-permute-start | bytes 776 | tf_op jit(solution)/shard_map/ppermute | solution.py:687
  179.5 15.2 %collective-permute-start.33 = (bf16[64,2048]{1,0:T(8,128)(2,1)S(1)}, bf16[64,2048]{1,0:T(8,128)(2,1)S(1)}, u32[]{:S(2)}, u32[]{:S(2)}) collective-permute-start(bf16[64,2048]{1,0:T(8,128)(2,1)S(1)} %get-tuple-element.126.refs_0_), channel_id=1, source_target_pairs={{0,1},{1,0},{2,3},{3,2},{4,5},{5,4},{6,7},{7,6},{8,9},{9,8},{10,11... | collective-permute-start | bytes 786440 | tf_op jit(solution)/shard_map/ppermute | solution.py:687
  233.2 16.3 %collective-permute-start.44 = (bf16[64,2048]{1,0:T(8,128)(2,1)}, bf16[64,2048]{1,0:T(8,128)(2,1)S(1)}, u32[]{:S(2)}, u32[]{:S(2)}) collective-permute-start(bf16[64,2048]{1,0:T(8,128)(2,1)} %get-tuple-element.134.refs_0_), channel_id=1, source_target_pairs={{0,1},{1,0},{2,3},{3,2},{4,5},{5,4},{6,7},{7,6},{8,9},{9,8},{10,11... | collective-permute-start | bytes 786440 | tf_op jit(solution)/shard_map/ppermute | solution.py:687
  282.8 15.4 %collective-permute-start.51 = (bf16[64,2048]{1,0:T(8,128)(2,1)}, bf16[64,2048]{1,0:T(8,128)(2,1)}, u32[]{:S(2)}, u32[]{:S(2)}) collective-permute-start(bf16[64,2048]{1,0:T(8,128)(2,1)} %get-tuple-element.140), channel_id=1, source_target_pairs={{0,48},{16,0},{32,16},{48,32},{1,49},{17,1},{33,17},{49,33},{2,50}... | collective-permute-start | bytes 786440 | tf_op jit(solution)/shard_map/ppermute | solution.py:687
  283.7 21.7 %collective-permute-start.61 = (bf16[64,2048]{1,0:T(8,128)(2,1)S(1)}, bf16[64,2048]{1,0:T(8,128)(2,1)}, u32[]{:S(2)}, u32[]{:S(2)}) collective-permute-start(bf16[64,2048]{1,0:T(8,128)(2,1)S(1)} %reshape.356.refs_8_.up_ref), channel_id=1, source_target_pairs={{0,16},{16,32},{32,48},{48,0},{1,17},{17,33},{33,49},{49,1},{2,18}... | collective-permute-start | bytes 786440 | tf_op jit(solution)/shard_map/ppermute | solution.py:687
  284.3 21.2 %collective-permute-start.62 = (bf16[64,2048]{1,0:T(8,128)(2,1)S(1)}, bf16[64,2048]{1,0:T(8,128)(2,1)}, u32[]{:S(2)}, u32[]{:S(2)}) collective-permute-start(bf16[64,2048]{1,0:T(8,128)(2,1)S(1)} %reshape.356.refs_8_.up_ref), channel_id=1, source_target_pairs={{0,1},{1,0},{2,3},{3,2},{4,5},{5,4},{6,7},{7,6},{8,9},{9,8},{10,11... | collective-permute-start | bytes 786440 | tf_op jit(solution)/shard_map/ppermute | solution.py:687
  306.2 15.3 %collective-permute-start.65 = (bf16[64,2048]{1,0:T(8,128)(2,1)}, bf16[64,2048]{1,0:T(8,128)(2,1)S(1)}, u32[]{:S(2)}, u32[]{:S(2)}) collective-permute-start(bf16[64,2048]{1,0:T(8,128)(2,1)} %collective-permute-done.61.refs_11_), channel_id=1, source_target_pairs={{0,1},{1,0},{2,3},{3,2},{4,5},{5,4},{6,7},{7,6},{8,9},{9,8},{10,11... | collective-permute-start | bytes 786440 | tf_op jit(solution)/shard_map/ppermute | solution.py:687
  364.6 15.4 %collective-permute-start.73 = (bf16[64,2048]{1,0:T(8,128)(2,1)}, bf16[64,2048]{1,0:T(8,128)(2,1)}, u32[]{:S(2)}, u32[]{:S(2)}) collective-permute-start(bf16[64,2048]{1,0:T(8,128)(2,1)} %get-tuple-element.153.refs_1_), channel_id=1, source_target_pairs={{0,16},{16,32},{32,48},{48,0},{1,17},{17,33},{33,49},{49,1},{2,18}... | collective-permute-start | bytes 786440 | tf_op jit(solution)/shard_map/ppermute | solution.py:687
  365.3 30.6 %collective-permute-start.74 = (bf16[64,2048]{1,0:T(8,128)(2,1)}, bf16[64,2048]{1,0:T(8,128)(2,1)}, u32[]{:S(2)}, u32[]{:S(2)}) collective-permute-start(bf16[64,2048]{1,0:T(8,128)(2,1)} %get-tuple-element.153.refs_1_), channel_id=1, source_target_pairs={{0,1},{1,0},{2,3},{3,2},{4,5},{5,4},{6,7},{7,6},{8,9},{9,8},{10,11... | collective-permute-start | bytes 786440 | tf_op jit(solution)/shard_map/ppermute | solution.py:687
  371.5 24.5 %collective-permute-start.75 = (bf16[64,2048]{1,0:T(8,128)(2,1)}, bf16[64,2048]{1,0:T(8,128)(2,1)S(1)}, u32[]{:S(2)}, u32[]{:S(2)}) collective-permute-start(bf16[64,2048]{1,0:T(8,128)(2,1)} %collective-permute-done.71.refs_2_), channel_id=1, source_target_pairs={{0,1},{1,0},{2,3},{3,2},{4,5},{5,4},{6,7},{7,6},{8,9},{9,8},{10,11... | collective-permute-start | bytes 786440 | tf_op jit(solution)/shard_map/ppermute | solution.py:687
  377.1 18.9 %collective-permute-start.76 = (bf16[64,2048]{1,0:T(8,128)(2,1)}, bf16[64,2048]{1,0:T(8,128)(2,1)S(1)}, u32[]{:S(2)}, u32[]{:S(2)}) collective-permute-start(bf16[64,2048]{1,0:T(8,128)(2,1)} %collective-permute-done.72.refs_3_), channel_id=1, source_target_pairs={{0,1},{1,0},{2,3},{3,2},{4,5},{5,4},{6,7},{7,6},{8,9},{9,8},{10,11... | collective-permute-start | bytes 786440 | tf_op jit(solution)/shard_map/ppermute | solution.py:687
  380.0 16.0 %collective-permute-start.77 = (bf16[64,2048]{1,0:T(8,128)(2,1)}, bf16[64,2048]{1,0:T(8,128)(2,1)S(1)}, u32[]{:S(2)}, u32[]{:S(2)}) collective-permute-start(bf16[64,2048]{1,0:T(8,128)(2,1)} %collective-permute-done.73.refs_4_), channel_id=1, source_target_pairs={{0,1},{1,0},{2,3},{3,2},{4,5},{5,4},{6,7},{7,6},{8,9},{9,8},{10,11... | collective-permute-start | bytes 786440 | tf_op jit(solution)/shard_map/ppermute | solution.py:687
  410.5 15.5 %collective-permute-start.80 = (bf16[64,2048]{1,0:T(8,128)(2,1)}, bf16[64,2048]{1,0:T(8,128)(2,1)S(1)}, u32[]{:S(2)}, u32[]{:S(2)}) collective-permute-start(bf16[64,2048]{1,0:T(8,128)(2,1)} %get-tuple-element.167), channel_id=1, source_target_pairs={{0,32},{16,48},{32,0},{48,16},{1,33},{17,49},{33,1},{49,17},{2,34}... | collective-permute-start | bytes 786440 | tf_op jit(solution)/shard_map/ppermute | solution.py:687
  444.7 236.9 %reduce-scatter.7.cloned.1.call-start = ((), (), s32[]{:S(2)}) async-start(), calls=%async_computation.6 | async-start | bytes 14761984
  498.9 30.7 %collective-permute-start.96 = (bf16[64,2048]{1,0:T(8,128)(2,1)}, bf16[64,2048]{1,0:T(8,128)(2,1)}, u32[]{:S(2)}, u32[]{:S(2)}) collective-permute-start(bf16[64,2048]{1,0:T(8,128)(2,1)} %get-tuple-element.192.refs_1_), channel_id=1, source_target_pairs={{0,1},{1,0},{2,3},{3,2},{4,5},{5,4},{6,7},{7,6},{8,9},{9,8},{10,11... | collective-permute-start | bytes 786440 | tf_op jit(solution)/shard_map/ppermute | solution.py:687
  509.3 20.4 %collective-permute-start.97 = (bf16[64,2048]{1,0:T(8,128)(2,1)S(1)}, bf16[64,2048]{1,0:T(8,128)(2,1)S(1)}, u32[]{:S(2)}, u32[]{:S(2)}) collective-permute-start(bf16[64,2048]{1,0:T(8,128)(2,1)S(1)} %collective-permute-done.93.refs_2_), channel_id=1, source_target_pairs={{0,1},{1,0},{2,3},{3,2},{4,5},{5,4},{6,7},{7,6},{8,9},{9,8},{10,11... | collective-permute-start | bytes 786440 | tf_op jit(solution)/shard_map/ppermute | solution.py:687
  510.8 18.9 %collective-permute-start.98 = (bf16[64,2048]{1,0:T(8,128)(2,1)}, bf16[64,2048]{1,0:T(8,128)(2,1)S(1)}, u32[]{:S(2)}, u32[]{:S(2)}) collective-permute-start(bf16[64,2048]{1,0:T(8,128)(2,1)} %collective-permute-done.94.refs_3_), channel_id=1, source_target_pairs={{0,1},{1,0},{2,3},{3,2},{4,5},{5,4},{6,7},{7,6},{8,9},{9,8},{10,11... | collective-permute-start | bytes 786440 | tf_op jit(solution)/shard_map/ppermute | solution.py:687
  513.4 16.3 %collective-permute-start.99 = (bf16[64,2048]{1,0:T(8,128)(2,1)}, bf16[64,2048]{1,0:T(8,128)(2,1)S(1)}, u32[]{:S(2)}, u32[]{:S(2)}) collective-permute-start(bf16[64,2048]{1,0:T(8,128)(2,1)} %collective-permute-done.95.refs_4_), channel_id=1, source_target_pairs={{0,1},{1,0},{2,3},{3,2},{4,5},{5,4},{6,7},{7,6},{8,9},{9,8},{10,11... | collective-permute-start | bytes 786440 | tf_op jit(solution)/shard_map/ppermute | solution.py:687
  587.1 119.2 %collective-permute-start.108 = (bf16[64,2048]{1,0:T(8,128)(2,1)}, bf16[64,2048]{1,0:T(8,128)(2,1)}, u32[]{:S(2)}, u32[]{:S(2)}) collective-permute-start(bf16[64,2048]{1,0:T(8,128)(2,1)} %fusion.4), channel_id=1, source_target_pairs={{0,64},{64,0},{1,65},{65,1},{2,66},{66,2},{3,67},{67,3},{4,68},{68... | collective-permute-start | bytes 786440 | tf_op jit(solution)/shard_map/ppermute | solution.py:687
  687.5 38.3 %all-to-all-start.1 = ((bf16[16,5,32,256]{3,2,1,0:T(8,128)(2,1)}), bf16[16,5,32,256]{3,2,1,0:T(8,128)(2,1)S(1)}, u32[]{:S(2)}, u32[]{:S(2)}) async-start(bf16[16,5,32,256]{3,2,1,0:T(8,128)(2,1)} %bitcast.189), calls=%async_computation.1 | async-start | bytes 2621440 | tf_op jit(solution)/shard_map/all_to_all | solution.py:715
  695.7 22.0 %collective-permute-start.107 = (bf16[64,2048]{1,0:T(8,128)(2,1)}, bf16[64,2048]{1,0:T(8,128)(2,1)}, u32[]{:S(2)}, u32[]{:S(2)}) collective-permute-start(bf16[64,2048]{1,0:T(8,128)(2,1)} %broadcast_select_fusion.6), channel_id=1, source_target_pairs={{0,64},{64,0},{1,65},{65,1},{2,66},{66,2},{3,67},{67,3},{4,68},{68... | collective-permute-start | bytes 786440 | tf_op jit(solution)/shard_map/ppermute | solution.py:687
  700.7 22.9 %collective-permute-start.109 = (bf16[640,256]{1,0:T(8,128)(2,1)}, bf16[640,256]{1,0:T(8,128)(2,1)}, u32[]{:S(2)}, u32[]{:S(2)}) collective-permute-start(bf16[640,256]{1,0:T(8,128)(2,1)} %get-tuple-element.260), channel_id=1, source_target_pairs={{0,0},{1,8},{8,1},{9,9},{64,64},{65,72},{72,65},{73,73},{2,2},{3,1... | collective-permute-start | bytes 983048 | tf_op jit(solution)/shard_map/ppermute | solution.py:711
  703.5 21.2 %collective-permute-start.110 = (bf16[640,256]{1,0:T(8,128)(2,1)}, bf16[640,256]{1,0:T(8,128)(2,1)}, u32[]{:S(2)}, u32[]{:S(2)}) collective-permute-start(bf16[640,256]{1,0:T(8,128)(2,1)} %get-tuple-element.259), channel_id=1, source_target_pairs={{0,64},{1,72},{8,65},{9,73},{64,0},{65,8},{72,1},{73,9},{2,66},{3,... | collective-permute-start | bytes 983048 | tf_op jit(solution)/shard_map/ppermute | solution.py:711
  (195 other events, 1210.5 us)
Sparse Core Ops, SparseCore 0:
  50.3 96.0 all-gather.2
  149.2 94.6 all-gather.4
  444.8 97.3 reduce-scatter.8
  579.1 102.4 reduce-scatter.6

commit v3 on v2

--- a/solution.py
+++ b/solution.py
@@ -80,15 +80,16 @@
     moved = sum(math.prod(o.shape) * o.dtype.itemsize for o in outs)
     moved += sum(math.prod(a.shape) * a.dtype.itemsize for a in args)
     in_specs = [in_hbm() if k < hbm else in_vmem() for k in range(len(args))]
-    if after is not None:
+    args = [pltpu.with_memory_space_constraint(a, pltpu.HBM) if k < hbm else a for k, a in enumerate(args)]
+    for array in after or ():
         kernel = without(kernel, len(args))
-        args = (*args, after)
-        in_specs.append(in_hbm())
+        args = (*args, array)
+        in_specs.append(pl.BlockSpec(memory_space=pl.ANY))
     return pl.pallas_call(
         kernel,
         in_specs=in_specs,
         out_specs=[in_hbm() if to_hbm or k >= stay else in_vmem() for k in range(len(outs))],
-        out_shape=outs,
+        out_shape=[pltpu.HBM(o.shape, o.dtype) if to_hbm or k >= stay else o for k, o in enumerate(outs)],
         scratch_shapes=scratch,
         input_output_aliases={0: 0} if in_place else {},
         compiler_params=pltpu.CompilerParams(vmem_limit_bytes=VMEM),
@@ -113,6 +114,23 @@
     def wait(self):
         for copy in self.copies:
             copy.wait()
+
+
+class Loads:
+    def __init__(self, sources, held, sems):
+        self.held = held
+        self.copies = [pltpu.make_async_copy(a, b, sems.at[k]) for k, (a, b) in enumerate(zip(sources, held))]
+        for copy in self.copies:
+            copy.start()
+
+    def wait(self, *which):
+        for k in which:
+            self.copies[k].wait()
+        return [self.held[k] for k in which]
+
+
+def loads_of(*arrays):
+    return [pltpu.VMEM(a.shape, a.dtype) for a in arrays] + [pltpu.SemaphoreType.DMA((len(arrays),))]
 
 
 class Weights:
@@ -177,14 +195,15 @@
     b_ref[:, TILE * j : TILE * (j + 1)] = part[HALF:]
 
 
-def attention_kernel(w_ref, *refs):
-    n_refs, (bias_ref, table_ref, mask_ref, pa_ref, pb_ref), refs = refs[:8], refs[8:13], refs[13:]
-    targets, held, sems, kept = refs[:5], refs[5], refs[6], Kept(refs[:5], refs[7:])
+def attention_kernel(w_ref, table_ref, mask_ref, *refs):
+    n_refs, (bias_ref, pa_ref, pb_ref), refs = refs[:8], refs[8:11], refs[11:]
+    held, sems, loads, kept = refs[5], refs[6], Loads((table_ref, mask_ref), refs[7:9], refs[9]), Kept(refs[:5], refs[10:])
     weights = Weights(w_ref, held, sems, [(t // 2, TILE * (t % 2), TILE, TILE * t) for t in range(4)])
     n_ref, q_ref, k_ref, v_ref, o_ref = kept.held
     n = rows_of(n_refs)
     n_ref[...] = n
     kept.send(0)
+    table_ref, mask_ref = loads.wait(0, 1)
     for j, ref in enumerate((q_ref, k_ref, v_ref)):
         weights.wait(j)
         u = dot(n, weights.tile(TILE * j)) + bias_ref[j : j + 1, :]
@@ -205,13 +224,13 @@
 def attention(after, weights, blocks, bias, table, mask):
     return call(
         attention_kernel,
-        (weights, *blocks, bias, table, mask),
+        (weights, table, mask, *blocks, bias),
         [shape_of(HALF, D), shape_of(HALF, D), shape_of(GROUP, D)] + [shape_of(GROUP, TILE)] * 4,
-        hbm=1,
+        hbm=3,
         stay=2,
         after=after,
         flops=2 * GROUP * D * 4 * TILE,
-        scratch=[pltpu.VMEM((BLOCKS, 4 * TILE, TILE), BF16), pltpu.SemaphoreType.DMA((4,))],
+        scratch=[pltpu.VMEM((BLOCKS, 4 * TILE, TILE), BF16), pltpu.SemaphoreType.DMA((4,))] + loads_of(table, mask),
     )
 
 
@@ -270,9 +289,9 @@
     )
 
 
-def feed_back_kernel(w_ref, *refs):
-    m_refs, (g_ref, u_ref, ea_ref, eb_ref), refs = refs[:8], refs[8:12], refs[12:]
-    held, sems, kept = refs[3], refs[4], Kept(refs[:3], refs[5:])
+def feed_back_kernel(w_ref, g_ref, u_ref, *refs):
+    m_refs, (ea_ref, eb_ref), refs = refs[:8], refs[8:10], refs[10:]
+    held, sems, loads, kept = refs[3], refs[4], Loads((g_ref, u_ref), refs[5:7], refs[7]), Kept(refs[:3], refs[8:])
     first, last = feed_pieces()
     weights = Weights(w_ref, held, sems, last + first)
     m_ref, dg_ref, du_ref = kept.held
@@ -284,8 +303,7 @@
         if j % 4 == 0:
             weights.wait(j // 4)
         da += dot_nt(gm[:, TILE * j : TILE * (j + 1)], weights.tile(6 * TILE + PADDED * j, PADDED))
-    g = g_ref[...]
-    u = u_ref[...]
+    g, u = [ref[...] for ref in loads.wait(0, 1)]
     sigma = jax.nn.sigmoid(g)
     dg_ref[...] = (da * u * sigma * (1.0 + g * (1.0 - sigma))).astype(BF16)
     du_ref[...] = (da * g * sigma).astype(BF16)
@@ -308,20 +326,19 @@
 def feed_back(after, weights, blocks, g, u):
     return call(
         feed_back_kernel,
-        (weights, *blocks, g, u),
+        (weights, g, u, *blocks),
         [shape_of(HALF, D), shape_of(HALF, D), shape_of(GROUP, D)] + [shape_of(GROUP, WIDE)] * 2,
-        hbm=1,
+        hbm=3,
         stay=2,
         after=after,
         flops=2 * GROUP * D * 9 * TILE,
-        scratch=[pltpu.VMEM(FEED_SCRATCH, BF16), pltpu.SemaphoreType.DMA((8,))],
+        scratch=[pltpu.VMEM(FEED_SCRATCH, BF16), pltpu.SemaphoreType.DMA((8,))] + loads_of(g, u),
     )
 
 
 def attention_back_kernel(w_ref, *refs):
-    d_refs = refs[:8]
-    q_ref, k_ref, v_ref, table_ref, mask_ref, ea_ref, eb_ref, sum_ref, *refs = refs[8:]
-    held, sems, kept = refs[4], refs[5], Kept(refs[:4], refs[6:])
+    sources, d_refs, (ea_ref, eb_ref, sum_ref), refs = refs[:5], refs[5:13], refs[13:16], refs[16:]
+    held, sems, loads, kept = refs[4], refs[5], Loads(sources, refs[6:11], refs[11]), Kept(refs[:4], refs[12:])
     d_ref, dq_ref, dk_ref, dv_ref = kept.held
     order = (3, 0, 1, 2)
     weights = Weights(w_ref, held, sems, [(t // 2, TILE * (t % 2), TILE, TILE * t) for t in order])
@@ -333,6 +350,7 @@
     for j in range(BLOCKS):
         do += dot_nt(dattn[:, TILE * j : TILE * (j + 1)], weights.tile(3 * TILE + 32 * j, 32))
     do = do.astype(BF16)
+    q_ref, k_ref, v_ref, table_ref, mask_ref = loads.wait(*range(5))
     dqs, dks = [], []
     for g in range(GROUP // 128):
         rows = slice(128 * g, 128 * g + 128)
@@ -366,14 +384,14 @@
 def attention_back(after, weights, blocks, q, k, v, table, mask):
     return call(
         attention_back_kernel,
-        (weights, *blocks, q, k, v, table, mask),
+        (weights, q, k, v, table, mask, *blocks),
         [shape_of(HALF, D), shape_of(HALF, D), shape_of(8, TILE, dtype=F32), shape_of(GROUP, D)]
         + [shape_of(GROUP, TILE)] * 3,
-        hbm=1,
+        hbm=6,
         stay=3,
         after=after,
         flops=2 * GROUP * D * 4 * TILE,
-        scratch=[pltpu.VMEM((BLOCKS, 4 * TILE, TILE), BF16), pltpu.SemaphoreType.DMA((4,))],
+        scratch=[pltpu.VMEM((BLOCKS, 4 * TILE, TILE), BF16), pltpu.SemaphoreType.DMA((4,))] + loads_of(q, k, v, table, mask),
     )
 
 
@@ -384,15 +402,17 @@
 
 
 def feed_grads_kernel(row, *refs):
-    n, dg, du, act, gm = [ref[...] for ref in refs[:5]]
-    vec_ref, out_ref, held, sems = refs[5:]
+    sources, (vec_ref, out_ref, held, sems), refs = refs[:5], refs[5:9], refs[9:]
+    loads = Loads(sources, refs[:5], refs[5])
     copies = []
+    n, dg, du = [ref[...] for ref in loads.wait(0, 1, 2)]
     for b in range(BLOCKS):
         left = n[:, TILE * b : TILE * (b + 1)]
         for half, right in enumerate((dg, du)):
             for j in range(3):
                 lanes = slice(TILE * j, TILE * (j + 1))
                 held[half, b, lanes, :] = dot_tn(left, right[:, lanes]).astype(BF16)
+    act, gm = [ref[...] for ref in loads.wait(3, 4)]
     for j in range(BLOCKS):
         half, k = divmod(j, 4)
         part = dot_tn(act, gm[:, TILE * j : TILE * (j + 1)]).astype(BF16)
@@ -409,22 +429,25 @@
         functools.partial(feed_grads_kernel, 0),
         (n, dg, du, act, gm, vec),
         [shape_of(2, BLOCKS, SUMS, TILE)],
+        hbm=5,
         after=after,
         flops=2 * GROUP * D * 9 * TILE,
-        scratch=[pltpu.VMEM((2, BLOCKS, FEED, TILE), BF16), pltpu.SemaphoreType.DMA((2,))],
+        scratch=[pltpu.VMEM((2, BLOCKS, FEED, TILE), BF16), pltpu.SemaphoreType.DMA((2,))] + loads_of(n, dg, du, act, gm),
         to_hbm=True,
     )[0]
 
 
 def attention_grads_kernel(row, *refs):
-    n, dattn, o, dq, dk, dv = [ref[...] for ref in refs[:6]]
-    vec_ref, out_ref, held, sems = refs[6:]
+    sources, (vec_ref, out_ref, held, sems), refs = refs[:6], refs[6:10], refs[10:]
+    loads = Loads(sources, refs[:6], refs[6])
     copies = []
+    n, dq, dk, dv = [ref[...] for ref in loads.wait(0, 3, 4, 5)]
     for b in range(BLOCKS):
         left = n[:, TILE * b : TILE * (b + 1)]
         for j, right in enumerate((dq, dk, dv)):
             half, at = divmod(TILE * j, ATTN)
             held[half, b, at : at + TILE, :] = dot_tn(left, right).astype(BF16)
+    dattn, o = [ref[...] for ref in loads.wait(1, 2)]
     for j in range(BLOCKS):
         part = dot_tn(o, dattn[:, TILE * j : TILE * (j + 1)]).astype(BF16)
         held[1, :, TILE + 32 * j : TILE + 32 * (j + 1), :] = part.reshape(BLOCKS, 32, TILE)
@@ -439,11 +462,11 @@
         without(functools.partial(attention_grads_kernel, FEED + VEC), 0),
         (sums, n, dattn, o, dq, dk, dv, vec),
         [shape_of(2, BLOCKS, SUMS, TILE)],
-        hbm=1,
+        hbm=7,
         in_place=True,
         after=after,
         flops=2 * GROUP * D * 4 * TILE,
-        scratch=[pltpu.VMEM((2, BLOCKS, ATTN, TILE), BF16), pltpu.SemaphoreType.DMA((2,))],
+        scratch=[pltpu.VMEM((2, BLOCKS, ATTN, TILE), BF16), pltpu.SemaphoreType.DMA((2,))] + loads_of(n, dattn, o, dq, dk, dv),
         to_hbm=True,
     )[0]
 
@@ -478,29 +501,29 @@
     return centred * scale, scale
 
 
-def norm_kernel(base_ref, *refs):
+def norm_kernel(row, base_ref, *refs):
     parts, (gain_ref, out_ref, n_ref) = refs[:4], refs[4:]
     out = (base_ref[...].astype(F32) + total_of(parts)).astype(out_ref.dtype)
     out_ref[...] = out
     unit, _ = unit_of(out.astype(F32))
-    n_ref[...] = (unit * gain_ref[0:1, :] + gain_ref[1:2, :]).astype(BF16)
-
-
-def normed(after, base, parts, gain, dtype):
-    return call(
-        norm_kernel,
-        (base, *parts, gain),
+    n_ref[...] = (unit * gain_ref[row : row + 1, :] + gain_ref[row + 1 : row + 2, :]).astype(BF16)
+
+
+def normed(after, base, parts, gains, row, dtype):
+    return call(
+        functools.partial(norm_kernel, row),
+        (base, *parts, gains),
         [shape_of(ROWS, D, dtype=dtype), shape_of(ROWS, D)],
         flops=16 * ROWS * D,
         after=after,
     )
 
 
-def norm_back_kernel(up_ref, *refs):
+def norm_back_kernel(row, up_ref, *refs):
     parts, (values_ref, gain_ref, grad_ref, low_ref, sum_ref) = refs[:4], refs[4:]
     e = total_of(parts)
     unit, scale = unit_of(values_ref[...].astype(F32))
-    q = e * gain_ref[0:1, :]
+    q = e * gain_ref[row : row + 1, :]
     back = scale * (q - jnp.mean(q, axis=-1, keepdims=True) - unit * jnp.mean(q * unit, axis=-1, keepdims=True))
     grad = up_ref[...].astype(F32) + back
     grad_ref[...] = grad
@@ -509,10 +532,10 @@
     sum_ref[...] = jnp.concatenate(sums + [jnp.zeros((6, D), F32)], axis=0)
 
 
-def normed_back(after, up, parts, values, gain):
-    return call(
-        norm_back_kernel,
-        (up, *parts, values, gain),
+def normed_back(after, up, parts, values, gains, row):
+    return call(
+        functools.partial(norm_back_kernel, row),
+        (up, *parts, values, gains),
         [shape_of(ROWS, D, dtype=F32), shape_of(ROWS, D), shape_of(8, D, dtype=F32)],
         flops=32 * ROWS * D,
         after=after,
@@ -520,17 +543,18 @@
 
 
 def feed_both_kernel(w_ref, *refs):
-    n_refs, m_refs = refs[:8], refs[8:16]
+    m_refs, n_refs = refs[:8], refs[8:16]
     pa_ref, pb_ref, ea_ref, eb_ref, *refs = refs[16:]
-    held, sems, kept = refs[5], refs[6], Kept(refs[:5], refs[7:])
+    held, sems, kept = refs[5], refs[6], Kept(refs[:5], (*refs[8:13], refs[13]))
     n_ref, m_ref, act_ref, dg_ref, du_ref = kept.held
+    loads = Loads(m_refs, [m_ref.at[ROWS * k : ROWS * (k + 1), :] for k in range(8)], refs[7])
     first, last = feed_pieces()
     weights = Weights(w_ref, held, sems, last + first)
     n = rows_of(n_refs)
-    gm = rows_of(m_refs)
     n_ref[...] = n
-    m_ref[...] = gm
     kept.send(0)
+    loads.wait(*range(8))
+    gm = m_ref[...]
     kept.send(1)
     weights.wait(0)
     weights.wait(1)
@@ -567,13 +591,13 @@
 def feed_both(after, weights, blocks, top):
     return call(
         feed_both_kernel,
-        (weights, *blocks, *top),
+        (weights, *top, *blocks),
         [shape_of(HALF, D)] * 4 + [shape_of(GROUP, D)] * 2 + [shape_of(GROUP, WIDE)] * 3,
-        hbm=1,
+        hbm=9,
         stay=4,
         after=after,
         flops=4 * GROUP * D * 9 * TILE,
-        scratch=[pltpu.VMEM(FEED_SCRATCH, BF16), pltpu.SemaphoreType.DMA((8,))],
+        scratch=[pltpu.VMEM(FEED_SCRATCH, BF16), pltpu.SemaphoreType.DMA((8,)), pltpu.SemaphoreType.DMA((8,))],
     )
 
 
@@ -599,10 +623,38 @@
     return jnp.concatenate([ref[:, 64 * (8 * x + b) : 64 * (8 * x + b + 1)] for x in range(4)], axis=1)
 
 
-def pack_kernel(qkv_ref, gate_ref, out_ref, down_ref, places_ref, values_ref, cut_ref, low_ref, high_ref):
+def pack_rows_kernel(out_in, down_in, low_ref, high_ref, out_ref, down_ref, sems):
+    Loads((out_in, down_in), (out_ref, down_ref), sems).wait(0, 1)
+    pad = jnp.zeros((PADDED - PIECE, TILE), BF16)
+    for b in range(BLOCKS):
+        high_ref[32 * b : 32 * (b + 1), :] = columns_of(out_ref, b)
+        down = jnp.concatenate([columns_of(down_ref, b), pad], axis=0)
+        row = PADDED * (b % 4)
+        if b < 4:
+            low_ref[row : row + PADDED, :] = down
+        else:
+            high_ref[TILE + row : TILE + row + PADDED, :] = down
+    low_ref[DOWN:, :] = jnp.zeros((TILE, TILE), BF16)
+
+
+def packed_rows(out_weight, down_weight):
+    return call(
+        pack_rows_kernel,
+        (out_weight, down_weight),
+        [shape_of(DOWN + TILE, TILE), shape_of(DOWN + TILE, TILE)],
+        hbm=2,
+        scratch=loads_of(out_weight, down_weight),
+        flops=1024,
+    )
+
+
+def pack_kernel(qkv_in, gate_in, places_in, values_in, cut_ref, *refs):
+    loads = Loads((gate_in, places_in, qkv_in, values_in), refs[:4], refs[4])
     wide = 8 * PIECE
+    gate_ref, places_ref = loads.wait(0, 1)
     rows = jnp.concatenate([gate_ref[:, wide * k : wide * (k + 1)] for k in range(16)], axis=0)
     placed = dot_nt(rows, places_ref[...]).astype(BF16)
+    qkv_ref, values_ref = loads.wait(2, 3)
     values = jnp.concatenate([qkv_ref[:, 2 * D + TILE * t : 2 * D + TILE * (t + 1)] for t in range(8)], axis=0)
     values = dot_nt(values, values_ref[...]).astype(BF16)
     for t in range(8):
@@ -614,25 +666,19 @@
             row = 32 * (8 * half + t)
             for j in range(3):
                 cut_ref[half, t, 2 - half + j] = placed[row : row + 32, TILE * j : TILE * (j + 1)]
-    pad = jnp.zeros((PADDED - PIECE, TILE), BF16)
-    for b in range(BLOCKS):
-        high_ref[32 * b : 32 * (b + 1), :] = columns_of(out_ref, b)
-        down = jnp.concatenate([columns_of(down_ref, b), pad], axis=0)
-        row = PADDED * (b % 4)
-        if b < 4:
-            low_ref[row : row + PADDED, :] = down
-        else:
-            high_ref[TILE + row : TILE + row + PADDED, :] = down
-    low_ref[DOWN:, :] = jnp.zeros((TILE, TILE), BF16)
-
-
-def packed(qkv_weight, gate_up, out_weight, down_weight):
+
+
+def packed(after, qkv_weight, gate_up):
+    places, values = pieces_in_order(), values_in_order()
     return call(
         pack_kernel,
-        (qkv_weight, gate_up, out_weight, down_weight, pieces_in_order(), values_in_order()),
-        [shape_of(2, 8, 5, 32, TILE), shape_of(DOWN + TILE, TILE), shape_of(DOWN + TILE, TILE)],
+        (qkv_weight, gate_up, places, values),
+        [shape_of(2, 8, 5, 32, TILE)],
+        hbm=4,
+        after=after,
+        scratch=loads_of(gate_up, places, qkv_weight, values),
         flops=2 * 512 * WIDE * 8 * PIECE,
-    )
+    )[0]
 
 
 def put_columns(ref, blocks):
@@ -643,7 +689,55 @@
             ref[:, 128 * (4 * x + k) : 128 * (4 * x + k + 1)] = pair.astype(F32)
 
 
-def unpack_kernel(cut_ref, first_ref, second_ref, places_ref, values_ref, qkv_ref, gate_ref, out_ref, down_ref, vec_ref):
+def in_smem():
+    return pl.BlockSpec(memory_space=pltpu.SMEM)
+
+
+def to_owners_kernel(section_ref, sum_0, sum_1, cut_ref, kept_ref, sent_ref):
+    lower = section_ref[0, 0] == 0
+    rows = []
+    for layer, ref in enumerate((sum_0, sum_1)):
+        feed = [ref[TILE * j : TILE * (j + 1), :] for j in range(3)]
+        down = ref[3 * TILE : FEED, :]
+        attn = [ref[FEED + VEC + TILE * j : FEED + VEC + TILE * (j + 1), :] for j in range(2)]
+        vecs = [ref[row : row + VEC, :].astype(F32) for row in (FEED + VEC + ATTN, FEED)]
+        pad = jnp.zeros((30, TILE), F32)
+        vec = [jnp.concatenate([v[o : o + 1] for v in vecs] + [pad], axis=0).astype(BF16) for o in range(8)]
+        low = (attn[0], attn[1], feed[0], feed[1], feed[2])
+        high = (attn[0], feed[0], feed[1], feed[2], jnp.concatenate(vec, axis=0))
+        for t in range(5):
+            tile = jnp.where(lower, low[t], high[t])
+            for o in range(8):
+                cut_ref[layer, o, t] = tile[32 * o : 32 * (o + 1)]
+        rows.append((jnp.concatenate([down, attn[1]], axis=0), jnp.concatenate([attn[1], down], axis=0)))
+    kept_ref[...] = jnp.where(lower, rows[0][0], rows[1][1])
+    sent_ref[...] = jnp.where(lower, rows[1][0], rows[0][1])
+
+
+def to_owners(after, section, sum_0, sum_1):
+    kernel = to_owners_kernel
+    for _ in after:
+        kernel = without(kernel, 3)
+    return pl.pallas_call(
+        kernel,
+        in_specs=[in_smem(), in_vmem(), in_vmem()] + [pl.BlockSpec(memory_space=pl.ANY)] * len(after),
+        out_specs=[in_vmem()] * 3,
+        out_shape=[shape_of(2, 8, 5, 32, TILE), shape_of(DOWN + TILE, TILE), shape_of(DOWN + TILE, TILE)],
+        compiler_params=pltpu.CompilerParams(vmem_limit_bytes=VMEM),
+    )(section, sum_0, sum_1, *after)
+
+
+def unpack_kernel(section_ref, kept_ref, sent_ref, places_ref, values_ref, cut_ref, qkv_ref, gate_ref, out_ref, down_ref, vec_ref):
+    lower = section_ref[0, 0] == 0
+    first = jnp.where(lower, kept_ref[:DOWN, :], sent_ref[:DOWN, :])
+    second = jnp.where(lower, sent_ref[...], kept_ref[...])
+    put_columns(out_ref, [second[32 * b : 32 * (b + 1)] for b in range(BLOCKS)])
+    down = []
+    for b in range(BLOCKS):
+        row = PADDED * (b % 4)
+        part = first[row : row + PADDED] if b < 4 else second[TILE + row : TILE + row + PADDED]
+        down.append(part.astype(F32)[:PIECE])
+    put_columns(down_ref, down)
     wide = 8 * PIECE
     vec = jnp.zeros((8, TILE), F32)
     for t in range(8):
@@ -658,28 +752,22 @@
     placed = dot(jnp.concatenate(rows, axis=0), places_ref[...])
     for k in range(16):
         gate_ref[:, wide * k : wide * (k + 1)] = placed[32 * k : 32 * (k + 1)]
-    put_columns(out_ref, [second_ref[32 * b : 32 * (b + 1), :] for b in range(BLOCKS)])
-    down = []
-    for b in range(BLOCKS):
-        row = PADDED * (b % 4)
-        part = first_ref[row : row + PADDED, :] if b < 4 else second_ref[TILE + row : TILE + row + PADDED, :]
-        down.append(part.astype(F32)[:PIECE])
-    put_columns(down_ref, down)
-
-
-def unpacked(cut, first, second):
-    return call(
+
+
+def unpacked(section, kept, sent, cut):
+    return pl.pallas_call(
         unpack_kernel,
-        (cut, first, second, pieces_in_order(), values_in_order()),
-        [
+        in_specs=[in_smem()] + [in_vmem()] * 5,
+        out_specs=[in_vmem()] * 5,
+        out_shape=[
             shape_of(32, 3 * D, dtype=F32),
             shape_of(32, 2 * FF, dtype=F32),
             shape_of(32, D, dtype=F32),
             shape_of(PIECE, D, dtype=F32),
             shape_of(8, TILE, dtype=F32),
         ],
-        flops=2 * 512 * WIDE * 8 * PIECE,
-    )
+        compiler_params=pltpu.CompilerParams(vmem_limit_bytes=VMEM),
+    )(section, kept, sent, pieces_in_order(), values_in_order(), cut)
 
 
 def turned(block, axis, step):
@@ -748,8 +836,8 @@
 
 def both_layers(qkv_weight, out_weight, gate_up, down_weight):
     section = lax.axis_index("section")
-    cut, low, high = packed(qkv_weight, gate_up, out_weight, down_weight)
-    cut = spread(cut.reshape(16, 5, 32, TILE))
+    low, high = packed_rows(out_weight, down_weight)
+    cut = spread(packed((low,), qkv_weight, gate_up).reshape(16, 5, 32, TILE))
     cut = cut.reshape(2, 8, 5, 32, TILE).transpose(0, 2, 1, 3, 4).reshape(2, 5 * TILE, TILE)
     kept = swapped(jnp.where(section == 0, low, high), 0)
     sent = swapped(jnp.where(section == 0, high, low), 1)
@@ -762,22 +850,12 @@
     return parts
 
 
-def owned(attn, feed, vecs):
-    section = lax.axis_index("section")
-    tiles = []
-    for layer in range(2):
-        low = jnp.concatenate([attn[layer], feed[layer][: 3 * TILE]], axis=0).reshape(5, 8, 32, TILE)
-        vec = jnp.pad(jnp.stack(vecs[layer], axis=1), ((0, 0), (0, 30), (0, 0))).reshape(1, 8, 32, TILE)
-        high = jnp.concatenate([attn[layer][:TILE], feed[layer][: 3 * TILE]], axis=0).reshape(4, 8, 32, TILE)
-        tiles.append(jnp.where(section == 0, low, jnp.concatenate([high, vec], axis=0)))
-    cut = spread(jnp.stack(tiles).transpose(0, 2, 1, 3, 4).reshape(16, 5, 32, TILE)).reshape(2, 8, 5, 32, TILE)
-    low = [jnp.pad(feed[layer][3 * TILE :], ((0, TILE), (0, 0))) for layer in range(2)]
-    high = [jnp.concatenate([attn[layer][TILE:], feed[layer][3 * TILE :]], axis=0) for layer in range(2)]
-    kept = swapped(jnp.where(section == 0, low[0], high[1]), 0)
-    sent = swapped(jnp.where(section == 0, low[1], high[0]), 1)
-    first = jnp.where(section == 0, kept, sent)
-    second = jnp.where(section == 0, sent, kept)
-    return unpacked(cut, first, second)
+def owned(after, sum_0, sum_1):
+    section = lax.axis_index("section").reshape(1, 1)
+    cut, kept, sent = to_owners(after, section, sum_0, sum_1)
+    kept, sent = swapped(kept, 0), swapped(sent, 1)
+    cut = spread(cut.reshape(16, 5, 32, TILE)).reshape(2, 8, 5, 32, TILE)
+    return unpacked(section, kept, sent, cut)
 
 
 def geometry(segments):
@@ -839,7 +917,7 @@
     vectors = in_order(vectors, "z", 4)
     vectors = in_order(vectors, RING, 4)
     vectors = vectors.reshape(2, 64, TILE).astype(F32)
-    gains = [vectors[:, :, 32 * k : 32 * (k + 1)].reshape(2, D) for k in range(4)]
+    gains = vectors[:, :, :128].reshape(2, 64, 4, 32).transpose(0, 2, 1, 3).reshape(8, D)
     bias = vectors[:, :, 128:224].reshape(2, 2, 4, 4, 2, 96).transpose(0, 3, 1, 2, 4, 5).reshape(2, 3, 8, TILE)
     bias = lax.dynamic_index_in_dim(bias, shard, 2, keepdims=False)
     bias = jnp.concatenate([bias[:, :2], value_columns(bias[:, 2:])], axis=1)
@@ -853,25 +931,22 @@
     segments = gathered_rows(own_rows(segment_ids).reshape(1, ROWS))
     tables = geometry(jnp.concatenate(segments, axis=0))
     top = gathered_rows(top_grad)
-    first_gains = [jnp.stack([gains[0][layer], gains[1][layer]]) for layer in range(2)]
-    second_gains = [jnp.stack([gains[2][layer], gains[3][layer]]) for layer in range(2)]
-
     outputs = [None, None]
     kept = [{}, {}]
     base = rows_in
     unit, _ = unit_of(base.astype(F32))
-    n = (unit * first_gains[0][0:1] + first_gains[0][1:2]).astype(BF16)
+    n = (unit * gains[0:1] + gains[1:2]).astype(BF16)
     for layer in range(2):
         have = kept[layer]
         part_a, part_b, have["n1"], have["q"], have["k"], have["v"], have["mixed"] = attention(
-            None, weights[layer], gathered_rows(n), bias[layer], *tables
+            top if layer == 0 else None, weights[layer], gathered_rows(n), bias[layer], *tables
         )
         have["values1"] = base
-        hidden, n = normed(None, base, summed_parts(None, part_a, part_b), second_gains[layer], F32)
+        hidden, n = normed(None, base, summed_parts(None, part_a, part_b), gains, 4 * layer + 2, F32)
         have["values2"] = hidden
         if layer == 0:
             part_a, part_b, have["n2"], have["g"], have["u"], have["act"] = feed(None, weights[0], gathered_rows(n))
-            base, n = normed(None, hidden, summed_parts(None, part_a, part_b), first_gains[1], BF16)
+            base, n = normed(None, hidden, summed_parts(None, part_a, part_b), gains, 4, BF16)
             outputs[0] = base
     part_a, part_b, ea, eb, have["n2"], have["gm"], have["act"], have["dg"], have["du"] = feed_both(
         None, weights[1], gathered_rows(n), top
@@ -899,19 +974,19 @@
         have = kept[layer]
         if layer == 0:
             ea, eb, have["gm"], have["dg"], have["du"] = feed_back(
-                sums_1, weights[0], gathered_rows(up), have["g"], have["u"]
+                (sums_1,), weights[0], gathered_rows(up), have["g"], have["u"]
             )
-        grad, low, have["sums2"] = normed_back(None, up, summed_parts(None, ea, eb), have["values2"], second_gains[layer])
+        grad, low, have["sums2"] = normed_back(None, up, summed_parts(None, ea, eb), have["values2"], gains, 4 * layer + 2)
         buffer = feed_sums(have)
         ea, eb, have["bias_sum"], have["dattn"], have["dq"], have["dk"], have["dv"] = attention_back(
-            buffer, weights[layer], gathered_rows(low), have["q"], have["k"], have["v"], *tables
+            (buffer,), weights[layer], gathered_rows(low), have["q"], have["k"], have["v"], *tables
         )
         parts = summed_parts(None, ea, eb)
-        grads_in[layer], up, have["sums1"] = normed_back(None, grad, parts, have["values1"], first_gains[layer])
+        grads_in[layer], up, have["sums1"] = normed_back(None, grad, parts, have["values1"], gains, 4 * layer)
         if layer == 1:
             sums_1 = attention_sums(have, buffer)
     sums_0 = attention_sums(kept[0], buffer)
-    first, *rest = summed_parts(sums_0, part_a, part_b)
+    first, *rest = summed_parts((sums_0,), part_a, part_b)
     total = kept[1]["values2"] + first
     for block in rest:
         total = total + block.astype(F32)
@@ -919,13 +994,6 @@
 
     sum_1 = scattered(sums_1)
     sum_0 = scattered(sums_0)
-    feed_0, attn_0 = sum_0[: FEED + VEC], sum_0[FEED + VEC :]
-    feed_1, attn_1 = sum_1[: FEED + VEC], sum_1[FEED + VEC :]
-    attn = [attn_0[:ATTN], attn_1[:ATTN]]
-    feeds = [feed_0[:FEED], feed_1[:FEED]]
-    vecs = [(attn_0[ATTN : ATTN + 8], feed_0[FEED : FEED + 8]), (attn_1[ATTN : ATTN + 8], feed_1[FEED : FEED + 8])]
-    qkv_grad, gate_up_grad, out_grad, down_grad, small = owned(attn, feeds, vecs)
-
     def layer_rows(first, second):
         mine = jnp.where(section == 0, first, second)
         other = turned(jnp.where(section == 0, second, first).astype(BF16), "section", 1).astype(first.dtype)
@@ -934,6 +1002,7 @@
 
     activations = layer_rows(outputs[0], outputs[1])
     input_grads = layer_rows(grads_in[0], upstream_of(grads_in[1]))
+    qkv_grad, gate_up_grad, out_grad, down_grad, small = owned((activations, input_grads), sum_0, sum_1)
     return (
         activations,
         input_grads,

time: 748 us -> 692 us (0.925)
  local copies, waits for them, and re-layouts: 120 us -> 47.8 us
  Pallas kernels: 119 us -> 131 us
  waiting for transfers between devices: 308 us -> 319 us
    unnamed x241 -> x138, local copies, waits for them, and re-layouts: 78.7 us -> 28.6 us
    ppermute x107, waiting for transfers between devices: 174 us -> 197 us  [turned(): return lax.ppermute(block, axis, [(i, (i - step) % n) for i in range(n)])]
    all_gather x2, waiting for transfers between devices: 34.6 us -> 12.9 us  [on_device(): full = lax.all_gather(part, SPREAD, axis=0, tiled=True)]
    ppermute x4, waiting for transfers between devices: 20.4 us -> 38.7 us  [swapped(): return lax.ppermute(block, ('section', 'y', 'core'), pairs)]
    slice x17 -> x2, local copies, waits for them, and re-layouts: 14.8 us -> 0.02 us  [the longest x1 0.01 us: on_device(): n = (unit * gains[0:1] + gains[1:2]).astype(BF16)]
    pallas_call x28, Pallas kernels: 119 us -> 128 us  [call(): pl.pallas_call(kernel, in_specs=in_specs, out_specs=[in_hbm() if to_hbm o...]
    unnamed x6, waiting for transfers between devices: 78.7 us -> 70.2 us
  transfers between devices with their start and end apart: 117 -> 117, of which waited for: 58 -> 58; matrix products, arithmetic and copies ran while one was open for 8% -> 4% of each run, Pallas kernels for 10% -> 11%
where the time goes in v3:
time: 692 us; the launch traced here: 682 us
  waiting for transfers between devices  319 us (46%)
  starting transfers between devices  156 us (23%)
  Pallas kernels  131 us (19%)
  local copies, waits for them, and re-layouts  47.8 us (7%)
  between operations  15.3 us (2%)
  other arithmetic  13.4 us (2%)
    ppermute x107, waiting for transfers between devices, turned(): return lax.ppermute(block, axis, [(i, (i - step) % n) for i in range(n)])  197 us
    ppermute x107, starting transfers between devices, turned(): return lax.ppermute(block, axis, [(i, (i - step) % n) for i in range(n)])  130 us
    pallas_call x28, Pallas kernels, call(): pl.pallas_call(kernel, in_specs=in_specs, out_specs=[in_hbm() if to_hbm o...  128 us
    unnamed x6, waiting for transfers between devices  70.2 us
    ppermute x4, waiting for transfers between devices, swapped(): return lax.ppermute(block, ('section', 'y', 'core'), pairs)  38.7 us
    unnamed x138, local copies, waits for them, and re-layouts  28.6 us
    all_to_all x2, starting transfers between devices, spread(): return lax.all_to_all(block, ('section', 'x', 'core'), 0, 0, tiled=True)  15.2 us
  transfers between devices with their start and end apart: 117, of which 58 were waited for; matrix products, arithmetic and copies ran while one was open for 4% of the time, Pallas kernels for 11%

profile of v3, /device:TPU:1, one launch (start us, length us, event | category | flops | bytes accessed | tf_op | source)
XLA Modules:
  0.0 682.3 jit_solution(6239658181853866445)
XLA Ops:
  12.2 8.5 %all-to-all-start = ((bf16[16,5,32,256]{3,2,1,0:T(8,128)(2,1)}), bf16[16,5,32,256]{3,2,1,0:T(8,128)(2,1)S(1)}, u32[]{:S(2)}, u32[]{:S(2)}) async-start(bf16[16,5,32,256]{3,2,1,0:T(8,128)(2,1)} %bitcast.5), calls=%async_computation | async-start | bytes 2621440 | tf_op jit(solution)/shard_map/all_to_all | solution.py:803
  26.2 17.4 %collective-permute-done = bf16[640,256]{1,0:T(8,128)(2,1)S(1)} collective-permute-done((bf16[640,256]{1,0:T(8,128)(2,1)S(1)}, bf16[640,256]{1,0:T(8,128)(2,1)S(1)}, u32[]{:S(2)}, u32[]{:S(2)}) %collective-permute-start) | collective-permute-done | bytes 327712 | tf_op jit(solution)/shard_map/ppermute | solution.py:799
  107.9 5.1 collective-permute-start.22
  130.5 12.9 %all-gather.3.cloned.1.call-done = bf16[26624,256]{1,0:T(8,128)(2,1)} async-done(((bf16[1664,256]{1,0:T(8,128)(2,1)}), bf16[26624,256]{1,0:T(8,128)(2,1)}) %all-gather.3.cloned.1.call-update) | async-done | bytes 13631504 | tf_op jit(solution)/shard_map/all_gather | solution.py:910
  146.3 10.4 %shard_map.241 = (bf16[256,2048]{1,0:T(8,128)(2,1)S(1)}, bf16[256,2048]{1,0:T(8,128)(2,1)S(1)}, bf16[512,2048]{1,0:T(8,128)(2,1)}, bf16[512,256]{1,0:T(8,128)(2,...) custom-call(bf16[2,8,1664,256]{3,2,1,0:T(8,128)(2,1)} %bitcast.156, ...), custom_call_target="tpu_custom_call" | custom-call | flops 2147483648 | bytes 16777216 | tf_op jit(solution)/shard_map/pallas_call | solution.py:88
  168.9 6.4 collective-permute-done.35.refs_2_
  181.1 8.1 %collective-permute-done.37.refs_1_ = bf16[64,2048]{1,0:T(8,128)(2,1)S(1)} collective-permute-done((bf16[64,2048]{1,0:T(8,128)(2,1)S(1)}, bf16[64,2048]{1,0:T(8,128)(2,1)S(1)}, u32[]{:S(2)}, u32[]{:S(2)}) %collective-permute-start.37) | collective-permute-done | bytes 262176 | tf_op jit(solution)/shard_map/ppermute | solution.py:775
  195.7 11.0 %shard_map.244 = (bf16[256,2048]{1,0:T(8,128)(2,1)S(1)}, bf16[256,2048]{1,0:T(8,128)(2,1)S(1)}, bf16[512,2048]{1,0:T(8,128)(2,1)}, f32[512,768]{1,0:T(8,128)}, f...) custom-call(bf16[2,8,1664,256]{3,2,1,0:T(8,128)(2,1)} %bitcast.157, bf16[64,2048]{1,0:T(8,128)(2,1)S(1)} %get-tuple-element.127.refs_0_, ...), custom_call_target="tpu_custom_call" | custom-call | flops 4831838208 | bytes 16777216 | tf_op jit(solution)/shard_map/pallas_call | solution.py:88
  212.4 11.9 %collective-permute-done.45.refs_1_ = bf16[64,2048]{1,0:T(8,128)(2,1)S(1)} collective-permute-done((bf16[64,2048]{1,0:T(8,128)(2,1)S(1)}, bf16[64,2048]{1,0:T(8,128)(2,1)S(1)}, u32[]{:S(2)}, u32[]{:S(2)}) %collective-permute-start.45) | collective-permute-done | bytes 262176 | tf_op jit(solution)/shard_map/ppermute | solution.py:775
  234.2 5.6 collective-permute-start.52
  244.8 9.5 %shard_map.247 = (bf16[256,2048]{1,0:T(8,128)(2,1)S(1)}, bf16[256,2048]{1,0:T(8,128)(2,1)S(1)}, bf16[512,2048]{1,0:T(8,128)(2,1)}, bf16[512,256]{1,0:T(8,128)(2,...) custom-call(bf16[2,8,1664,256]{3,2,1,0:T(8,128)(2,1)} %bitcast.160, ...), custom_call_target="tpu_custom_call" | custom-call | flops 2147483648 | bytes 16777216 | tf_op jit(solution)/shard_map/pallas_call | solution.py:88
  260.0 6.9 %collective-permute-done.56.refs_1_ = bf16[64,2048]{1,0:T(8,128)(2,1)S(1)} collective-permute-done((bf16[64,2048]{1,0:T(8,128)(2,1)S(1)}, bf16[64,2048]{1,0:T(8,128)(2,1)S(1)}, u32[]{:S(2)}, u32[]{:S(2)}) %collective-permute-start.56) | collective-permute-done | bytes 262176 | tf_op jit(solution)/shard_map/ppermute | solution.py:775
  281.8 5.5 collective-permute-start.63
  292.1 17.7 %shard_map.250 = (bf16[256,2048]{1,0:T(8,128)(2,1)S(1)}, bf16[256,2048]{1,0:T(8,128)(2,1)S(1)}, bf16[256,2048]{1,0:T(8,128)(2,1)S(1)}, bf16[256,2048]{1,0:T(8,12...) custom-call(bf16[2,8,1664,256]{3,2,1,0:T(8,128)(2,1)} %bitcast.161, ...), custom_call_target="tpu_custom_call" | custom-call | flops 9663676416 | bytes 16777216 | tf_op jit(solution)/shard_map/pallas_call | solution.py:88
  316.4 6.9 %collective-permute-done.68.refs_1_ = bf16[64,2048]{1,0:T(8,128)(2,1)S(1)} collective-permute-done((bf16[64,2048]{1,0:T(8,128)(2,1)S(1)}, bf16[64,2048]{1,0:T(8,128)(2,1)S(1)}, u32[]{:S(2)}, u32[]{:S(2)}) %collective-permute-start.68) | collective-permute-done | bytes 262176 | tf_op jit(solution)/shard_map/ppermute | solution.py:775
  339.2 5.5 collective-permute-start.75
  348.2 10.9 %shard_map.253.refs_14_.refs_0_ = bf16[2,8,1696,256]{3,2,1,0:T(8,128)(2,1)} custom-call(bf16[512,2048]{1,0:T(8,128)(2,1)} %get-tuple-element.160.refs_0_, bf16[512,768]{1,0:T(8,128)(2,1)} %get-tuple-element.161.refs_1_, bf16[512,768]{1,0:T(8,128)(2,1)} %get-tuple-element.162.refs_2_, bf16[512,768]{1,0:T(8,128)(2,1)} %get-tuple-element.163.refs_3_, ...), custom_call_target="tpu_custom_call" | custom-call | flops 4831838208 | bytes 16777216 | tf_op jit(solution)/shard_map/pallas_call | solution.py:88
  359.2 9.4 %shard_map.254 = (bf16[256,2048]{1,0:T(8,128)(2,1)S(1)}, bf16[256,2048]{1,0:T(8,128)(2,1)S(1)}, f32[8,256]{1,0:T(8,128)S(1)}, bf16[512,2048]{1,0:T(8,128)(2,1)},...) custom-call(bf16[2,8,1664,256]{3,2,1,0:T(8,128)(2,1)} %bitcast.162, ...), custom_call_target="tpu_custom_call" | custom-call | flops 2147483648 | bytes 16777216 | tf_op jit(solution)/shard_map/pallas_call | solution.py:88
  376.5 11.5 %collective-permute-done.79.refs_1_ = bf16[64,2048]{1,0:T(8,128)(2,1)S(1)} collective-permute-done((bf16[64,2048]{1,0:T(8,128)(2,1)}, bf16[64,2048]{1,0:T(8,128)(2,1)S(1)}, u32[]{:S(2)}, u32[]{:S(2)}) %collective-permute-start.79) | collective-permute-done | bytes 262176 | tf_op jit(solution)/shard_map/ppermute | solution.py:775
  396.1 7.2 %shard_map.257.refs_11_ = bf16[2,8,1696,256]{3,2,1,0:T(8,128)(2,1)} custom-call(bf16[2,8,1696,256]{3,2,1,0:T(8,128)(2,1)} %shard_map.253.refs_14_.refs_0_, bf16[512,2048]{1,0:T(8,128)(2,1)} %get-tuple-element.173.refs_1_, bf16[512,2048]{1,0:T(8,128)(2,1)} %get-tuple-element.174.refs_2_, ...), custom_call_target="tpu_custom_call", output_to_operand_aliasing={{}: (0, {})} | custom-call | flops 2147483648 | bytes 16777216 | tf_op jit(solution)/shard_map/pallas_call | solution.py:88
  421.6 10.5 %shard_map.258 = (bf16[256,2048]{1,0:T(8,128)(2,1)S(1)}, bf16[256,2048]{1,0:T(8,128)(2,1)S(1)}, bf16[512,2048]{1,0:T(8,128)(2,1)}, bf16[512,768]{1,0:T(8,128)(2,1)}, bf16[512,768]{1,0:T(8,128)(2,1)}) custom-call(bf16[2,8,1664,256]{3,2,1,0:T(8,128)(2,1)} %bitcast.158, f32[512,768]{1,0:T(8,128)} %get-tuple-element.147.refs_1_, ...), custom_call_target="tpu_custom_call" | custom-call | flops 4831838208 | bytes 16777216 | tf_op jit(solution)/shard_map/pallas_call | solution.py:88
  437.8 6.8 collective-permute-done.90.refs_1_
  461.8 5.4 collective-permute-start.97
  471.0 11.1 %shard_map.261.refs_14_.refs_0_ = bf16[2,8,1696,256]{3,2,1,0:T(8,128)(2,1)} custom-call(bf16[512,2048]{1,0:T(8,128)(2,1)} %get-tuple-element.146.refs_0_, bf16[512,768]{1,0:T(8,128)(2,1)} %get-tuple-element.181.refs_1_, bf16[512,768]{1,0:T(8,128)(2,1)} %get-tuple-element.182.refs_2_, bf16[512,768]{1,0:T(8,128)(2,1)} %get-tuple-element.183.refs_3_, ...), custom_call_target="tpu_custom_call" | custom-call | flops 4831838208 | bytes 16777216 | tf_op jit(solution)/shard_map/pallas_call | solution.py:88
  484.1 9.8 %shard_map.262 = (bf16[256,2048]{1,0:T(8,128)(2,1)S(1)}, bf16[256,2048]{1,0:T(8,128)(2,1)S(1)}, f32[8,256]{1,0:T(8,128)S(1)}, bf16[512,2048]{1,0:T(8,128)(2,1)},...) custom-call(bf16[2,8,1664,256]{3,2,1,0:T(8,128)(2,1)} %bitcast.159, ...), custom_call_target="tpu_custom_call" | custom-call | flops 2147483648 | bytes 16777216 | tf_op jit(solution)/shard_map/pallas_call | solution.py:88
  501.7 11.5 %collective-permute-done.101.refs_1_ = bf16[64,2048]{1,0:T(8,128)(2,1)S(1)} collective-permute-done((bf16[64,2048]{1,0:T(8,128)(2,1)}, bf16[64,2048]{1,0:T(8,128)(2,1)S(1)}, u32[]{:S(2)}, u32[]{:S(2)}) %collective-permute-start.101) | collective-permute-done | bytes 262176 | tf_op jit(solution)/shard_map/ppermute | solution.py:775
  520.3 7.1 %shard_map.265.refs_2_ = bf16[2,8,1696,256]{3,2,1,0:T(8,128)(2,1)} custom-call(bf16[2,8,1696,256]{3,2,1,0:T(8,128)(2,1)} %shard_map.261.refs_14_.refs_0_, bf16[512,2048]{1,0:T(8,128)(2,1)} %get-tuple-element.192.refs_1_, bf16[512,2048]{1,0:T(8,128)(2,1)} %get-tuple-element.197.refs_2_, ...), custom_call_target="tpu_custom_call", output_to_operand_aliasing={{}: (0, {})} | custom-call | flops 2147483648 | bytes 16777216 | tf_op jit(solution)/shard_map/pallas_call | solution.py:88
  540.1 6.0 collective-permute-done.105
  552.6 9.8 %collective-permute-done.107 = bf16[64,2048]{1,0:T(8,128)(2,1)} collective-permute-done((bf16[64,2048]{1,0:T(8,128)(2,1)}, bf16[64,2048]{1,0:T(8,128)(2,1)}, u32[]{:S(2)}, u32[]{:S(2)}) %collective-permute-start.107) | collective-permute-done | bytes 262176 | tf_op jit(solution)/shard_map/ppermute | solution.py:775
  565.3 70.1 %reduce-scatter.7.cloned.1.call-done = bf16[1,1696,256]{2,1,0:T(8,128)(2,1)} async-done(((bf16[16,1696,256]{2,1,0:T(8,128)(2,1)}), bf16[1,1696,256]{2,1,0:T(8,128)(2,1)}) %reduce-scatter.7.cloned.1.call-update) | async-done | bytes 868368
  640.3 6.8 all-to-all-start.1
  652.6 17.6 %collective-permute-done.109.kept_ref = bf16[640,256]{1,0:T(8,128)(2,1)S(1)} collective-permute-done((bf16[640,256]{1,0:T(8,128)(2,1)}, bf16[640,256]{1,0:T(8,128)(2,1)S(1)}, u32[]{:S(2)}, u32[]{:S(2)}) %collective-permute-start.109) | collective-permute-done | bytes 327712 | tf_op jit(solution)/shard_map/ppermute | solution.py:799
  (509 shorter events, 306.1 us)
Async XLA Ops:
  12.2 33.5 %all-to-all-start = ((bf16[16,5,32,256]{3,2,1,0:T(8,128)(2,1)}), bf16[16,5,32,256]{3,2,1,0:T(8,128)(2,1)S(1)}, u32[]{:S(2)}, u32[]{:S(2)}) async-start(bf16[16,5,32,256]{3,2,1,0:T(8,128)(2,1)} %bitcast.5), calls=%async_computation | async-start | bytes 2621440 | tf_op jit(solution)/shard_map/all_to_all | solution.py:803
  20.7 122.8 %all-gather.3.cloned.1.call-start = ((), (), s32[]{:S(2)}) async-start(), calls=%async_computation.4 | async-start | bytes 14483456 | tf_op jit(solution)/shard_map/all_gather | solution.py:910
  20.8 22.8 %collective-permute-start = (bf16[640,256]{1,0:T(8,128)(2,1)S(1)}, bf16[640,256]{1,0:T(8,128)(2,1)S(1)}, u32[]{:S(2)}, u32[]{:S(2)}) collective-permute-start(bf16[640,256]{1,0:T(8,128)(2,1)S(1)} %get-tuple-element.252), channel_id=1, source_target_pairs={{0,0},{1,8},{8,1},{9,9},{64,64},{65,72},{72,65},{73,73},{2,2},{3,1... | collective-permute-start | bytes 983048 | tf_op jit(solution)/shard_map/ppermute | solution.py:799
  23.1 22.5 %collective-permute-start.1 = (bf16[640,256]{1,0:T(8,128)(2,1)S(1)}, bf16[640,256]{1,0:T(8,128)(2,1)S(1)}, u32[]{:S(2)}, u32[]{:S(2)}) collective-permute-start(bf16[640,256]{1,0:T(8,128)(2,1)S(1)} %get-tuple-element.251), channel_id=1, source_target_pairs={{0,64},{1,72},{8,65},{9,73},{64,0},{65,8},{72,1},{73,9},{2,66},{3,... | collective-permute-start | bytes 983048 | tf_op jit(solution)/shard_map/ppermute | solution.py:799
  47.1 196.5 %all-gather.5.cloned.1.call-start = ((), (), s32[]{:S(2)}) async-start(), calls=%async_computation.5 | async-start | bytes 14483456 | tf_op jit(solution)/shard_map/all_gather | solution.py:910
  48.4 516.8 %reduce-scatter.9.cloned.1.call-start = ((), (), s32[]{:S(2)}) async-start(), calls=%async_computation.7 | async-start | bytes 14761984
  48.6 25.9 %collective-permute-start.2 = (s32[1,64]{1,0:T(1,128)S(1)}, s32[1,64]{1,0:T(1,128)S(1)}, u32[]{:S(2)}, u32[]{:S(2)}) collective-permute-start(s32[1,64]{1,0:T(1,128)S(1)} %reshape.258), channel_id=1, source_target_pairs={{0,48},{16,0},{32,16},{48,32},{1,49},{17,1},{33,17},{49,33},{2,50}... | collective-permute-start | bytes 776 | tf_op jit(solution)/shard_map/ppermute | solution.py:775
  51.0 26.6 %collective-permute-start.3 = (s32[1,64]{1,0:T(1,128)S(1)}, s32[1,64]{1,0:T(1,128)S(1)}, u32[]{:S(2)}, u32[]{:S(2)}) collective-permute-start(s32[1,64]{1,0:T(1,128)S(1)} %reshape.258), channel_id=1, source_target_pairs={{0,32},{16,48},{32,0},{48,16},{1,33},{17,49},{33,1},{49,17},{2,34}... | collective-permute-start | bytes 776 | tf_op jit(solution)/shard_map/ppermute | solution.py:775
  51.6 26.2 %collective-permute-start.4 = (s32[1,64]{1,0:T(1,128)S(1)}, s32[1,64]{1,0:T(1,128)S(1)}, u32[]{:S(2)}, u32[]{:S(2)}) collective-permute-start(s32[1,64]{1,0:T(1,128)S(1)} %reshape.258), channel_id=1, source_target_pairs={{0,16},{16,32},{32,48},{48,0},{1,17},{17,33},{33,49},{49,1},{2,18}... | collective-permute-start | bytes 776 | tf_op jit(solution)/shard_map/ppermute | solution.py:775
  52.2 25.9 %collective-permute-start.5 = (s32[1,64]{1,0:T(1,128)S(1)}, s32[1,64]{1,0:T(1,128)S(1)}, u32[]{:S(2)}, u32[]{:S(2)}) collective-permute-start(s32[1,64]{1,0:T(1,128)S(1)} %reshape.258), channel_id=1, source_target_pairs={{0,1},{1,0},{2,3},{3,2},{4,5},{5,4},{6,7},{7,6},{8,9},{9,8},{10,11... | collective-permute-start | bytes 776 | tf_op jit(solution)/shard_map/ppermute | solution.py:775
  78.1 27.9 %collective-permute-start.26 = (bf16[64,2048]{1,0:T(8,128)(2,1)S(1)}, bf16[64,2048]{1,0:T(8,128)(2,1)S(1)}, u32[]{:S(2)}, u32[]{:S(2)}) collective-permute-start(bf16[64,2048]{1,0:T(8,128)(2,1)S(1)} %reshape.266.refs_12_.refs_0_.up_ref), channel_id=1, source_target_pairs={{0,48},{16,0},{32,16},{48,32},{1,49},{17,1},{33,17},{49,33},{2,50}... | collective-permute-start | bytes 786440 | tf_op jit(solution)/shard_map/ppermute | solution.py:775
  79.9 28.0 %collective-permute-start.27 = (bf16[64,2048]{1,0:T(8,128)(2,1)S(1)}, bf16[64,2048]{1,0:T(8,128)(2,1)S(1)}, u32[]{:S(2)}, u32[]{:S(2)}) collective-permute-start(bf16[64,2048]{1,0:T(8,128)(2,1)S(1)} %reshape.266.refs_12_.refs_0_.up_ref), channel_id=1, source_target_pairs={{0,32},{16,48},{32,0},{48,16},{1,33},{17,49},{33,1},{49,17},{2,34}... | collective-permute-start | bytes 786440 | tf_op jit(solution)/shard_map/ppermute | solution.py:775
  79.9 28.0 %collective-permute-start.28 = (bf16[64,2048]{1,0:T(8,128)(2,1)S(1)}, bf16[64,2048]{1,0:T(8,128)(2,1)S(1)}, u32[]{:S(2)}, u32[]{:S(2)}) collective-permute-start(bf16[64,2048]{1,0:T(8,128)(2,1)S(1)} %reshape.266.refs_12_.refs_0_.up_ref), channel_id=1, source_target_pairs={{0,16},{16,32},{32,48},{48,0},{1,17},{17,33},{33,49},{49,1},{2,18}... | collective-permute-start | bytes 786440 | tf_op jit(solution)/shard_map/ppermute | solution.py:775
  80.8 32.3 %collective-permute-start.29 = (bf16[64,2048]{1,0:T(8,128)(2,1)S(1)}, bf16[64,2048]{1,0:T(8,128)(2,1)S(1)}, u32[]{:S(2)}, u32[]{:S(2)}) collective-permute-start(bf16[64,2048]{1,0:T(8,128)(2,1)S(1)} %reshape.266.refs_12_.refs_0_.up_ref), channel_id=1, source_target_pairs={{0,1},{1,0},{2,3},{3,2},{4,5},{5,4},{6,7},{7,6},{8,9},{9,8},{10,11... | collective-permute-start | bytes 786440 | tf_op jit(solution)/shard_map/ppermute | solution.py:775
  104.5 21.5 %collective-permute-start.19 = (bf16[64,2048]{1,0:T(8,128)(2,1)S(1)}, bf16[64,2048]{1,0:T(8,128)(2,1)S(1)}, u32[]{:S(2)}, u32[]{:S(2)}) collective-permute-start(bf16[64,2048]{1,0:T(8,128)(2,1)S(1)} %add_convert_fusion.1.refs_3_), channel_id=1, source_target_pairs={{0,48},{16,0},{32,16},{48,32},{1,49},{17,1},{33,17},{49,33},{2,50}... | collective-permute-start | bytes 786440 | tf_op jit(solution)/shard_map/ppermute | solution.py:775
  106.0 20.4 %collective-permute-start.20 = (bf16[64,2048]{1,0:T(8,128)(2,1)S(1)}, bf16[64,2048]{1,0:T(8,128)(2,1)S(1)}, u32[]{:S(2)}, u32[]{:S(2)}) collective-permute-start(bf16[64,2048]{1,0:T(8,128)(2,1)S(1)} %add_convert_fusion.1.refs_3_), channel_id=1, source_target_pairs={{0,32},{16,48},{32,0},{48,16},{1,33},{17,49},{33,1},{49,17},{2,34}... | collective-permute-start | bytes 786440 | tf_op jit(solution)/shard_map/ppermute | solution.py:775
  107.9 18.7 %collective-permute-start.21 = (bf16[64,2048]{1,0:T(8,128)(2,1)S(1)}, bf16[64,2048]{1,0:T(8,128)(2,1)S(1)}, u32[]{:S(2)}, u32[]{:S(2)}) collective-permute-start(bf16[64,2048]{1,0:T(8,128)(2,1)S(1)} %add_convert_fusion.1.refs_3_), channel_id=1, source_target_pairs={{0,16},{16,32},{32,48},{48,0},{1,17},{17,33},{33,49},{49,1},{2,18}... | collective-permute-start | bytes 786440 | tf_op jit(solution)/shard_map/ppermute | solution.py:775
  107.9 19.1 %collective-permute-start.22 = (bf16[64,2048]{1,0:T(8,128)(2,1)S(1)}, bf16[64,2048]{1,0:T(8,128)(2,1)}, u32[]{:S(2)}, u32[]{:S(2)}) collective-permute-start(bf16[64,2048]{1,0:T(8,128)(2,1)S(1)} %add_convert_fusion.1.refs_3_), channel_id=1, source_target_pairs={{0,1},{1,0},{2,3},{3,2},{4,5},{5,4},{6,7},{7,6},{8,9},{9,8},{10,11... | collective-permute-start | bytes 786440 | tf_op jit(solution)/shard_map/ppermute | solution.py:775
  178.7 15.1 %collective-permute-start.39 = (bf16[64,2048]{1,0:T(8,128)(2,1)S(1)}, bf16[64,2048]{1,0:T(8,128)(2,1)S(1)}, u32[]{:S(2)}, u32[]{:S(2)}) collective-permute-start(bf16[64,2048]{1,0:T(8,128)(2,1)S(1)} %get-tuple-element.127.refs_0_), channel_id=1, source_target_pairs={{0,16},{16,32},{32,48},{48,0},{1,17},{17,33},{33,49},{49,1},{2,18}... | collective-permute-start | bytes 786440 | tf_op jit(solution)/shard_map/ppermute | solution.py:775
  179.2 15.3 %collective-permute-start.40 = (bf16[64,2048]{1,0:T(8,128)(2,1)S(1)}, bf16[64,2048]{1,0:T(8,128)(2,1)S(1)}, u32[]{:S(2)}, u32[]{:S(2)}) collective-permute-start(bf16[64,2048]{1,0:T(8,128)(2,1)S(1)} %get-tuple-element.127.refs_0_), channel_id=1, source_target_pairs={{0,1},{1,0},{2,3},{3,2},{4,5},{5,4},{6,7},{7,6},{8,9},{9,8},{10,11... | collective-permute-start | bytes 786440 | tf_op jit(solution)/shard_map/ppermute | solution.py:775
  228.4 15.3 %collective-permute-start.51 = (bf16[64,2048]{1,0:T(8,128)(2,1)S(1)}, bf16[64,2048]{1,0:T(8,128)(2,1)S(1)}, u32[]{:S(2)}, u32[]{:S(2)}) collective-permute-start(bf16[64,2048]{1,0:T(8,128)(2,1)S(1)} %get-tuple-element.135.refs_0_), channel_id=1, source_target_pairs={{0,1},{1,0},{2,3},{3,2},{4,5},{5,4},{6,7},{7,6},{8,9},{9,8},{10,11... | collective-permute-start | bytes 786440 | tf_op jit(solution)/shard_map/ppermute | solution.py:775
  275.9 15.0 %collective-permute-start.62 = (bf16[64,2048]{1,0:T(8,128)(2,1)S(1)}, bf16[64,2048]{1,0:T(8,128)(2,1)S(1)}, u32[]{:S(2)}, u32[]{:S(2)}) collective-permute-start(bf16[64,2048]{1,0:T(8,128)(2,1)S(1)} %get-tuple-element.143.refs_8_), channel_id=1, source_target_pairs={{0,1},{1,0},{2,3},{3,2},{4,5},{5,4},{6,7},{7,6},{8,9},{9,8},{10,11... | collective-permute-start | bytes 786440 | tf_op jit(solution)/shard_map/ppermute | solution.py:775
  333.2 26.0 %collective-permute-start.74 = (bf16[64,2048]{1,0:T(8,128)(2,1)S(1)}, bf16[64,2048]{1,0:T(8,128)(2,1)}, u32[]{:S(2)}, u32[]{:S(2)}) collective-permute-start(bf16[64,2048]{1,0:T(8,128)(2,1)S(1)} %get-tuple-element.159.refs_6_), channel_id=1, source_target_pairs={{0,1},{1,0},{2,3},{3,2},{4,5},{5,4},{6,7},{7,6},{8,9},{9,8},{10,11... | collective-permute-start | bytes 786440 | tf_op jit(solution)/shard_map/ppermute | solution.py:775
  339.2 20.0 %collective-permute-start.75 = (bf16[64,2048]{1,0:T(8,128)(2,1)S(1)}, bf16[64,2048]{1,0:T(8,128)(2,1)S(1)}, u32[]{:S(2)}, u32[]{:S(2)}) collective-permute-start(bf16[64,2048]{1,0:T(8,128)(2,1)S(1)} %collective-permute-done.71.refs_7_), channel_id=1, source_target_pairs={{0,1},{1,0},{2,3},{3,2},{4,5},{5,4},{6,7},{7,6},{8,9},{9,8},{10,11... | collective-permute-start | bytes 786440 | tf_op jit(solution)/shard_map/ppermute | solution.py:775
  373.2 15.5 %collective-permute-start.80 = (bf16[64,2048]{1,0:T(8,128)(2,1)}, bf16[64,2048]{1,0:T(8,128)(2,1)S(1)}, u32[]{:S(2)}, u32[]{:S(2)}) collective-permute-start(bf16[64,2048]{1,0:T(8,128)(2,1)} %get-tuple-element.170), channel_id=1, source_target_pairs={{0,32},{16,48},{32,0},{48,16},{1,33},{17,49},{33,1},{49,17},{2,34}... | collective-permute-start | bytes 786440 | tf_op jit(solution)/shard_map/ppermute | solution.py:775
  403.3 232.1 %reduce-scatter.7.cloned.1.call-start = ((), (), s32[]{:S(2)}) async-start(), calls=%async_computation.6 | async-start | bytes 14761984
  455.4 26.8 %collective-permute-start.96 = (bf16[64,2048]{1,0:T(8,128)(2,1)}, bf16[64,2048]{1,0:T(8,128)(2,1)}, u32[]{:S(2)}, u32[]{:S(2)}) collective-permute-start(bf16[64,2048]{1,0:T(8,128)(2,1)} %get-tuple-element.196.refs_6_), channel_id=1, source_target_pairs={{0,1},{1,0},{2,3},{3,2},{4,5},{5,4},{6,7},{7,6},{8,9},{9,8},{10,11... | collective-permute-start | bytes 786440 | tf_op jit(solution)/shard_map/ppermute | solution.py:775
  461.8 20.4 %collective-permute-start.97 = (bf16[64,2048]{1,0:T(8,128)(2,1)S(1)}, bf16[64,2048]{1,0:T(8,128)(2,1)S(1)}, u32[]{:S(2)}, u32[]{:S(2)}) collective-permute-start(bf16[64,2048]{1,0:T(8,128)(2,1)S(1)} %collective-permute-done.93.refs_7_), channel_id=1, source_target_pairs={{0,1},{1,0},{2,3},{3,2},{4,5},{5,4},{6,7},{7,6},{8,9},{9,8},{10,11... | collective-permute-start | bytes 786440 | tf_op jit(solution)/shard_map/ppermute | solution.py:775
  547.1 15.3 %collective-permute-start.107 = (bf16[64,2048]{1,0:T(8,128)(2,1)}, bf16[64,2048]{1,0:T(8,128)(2,1)}, u32[]{:S(2)}, u32[]{:S(2)}) collective-permute-start(bf16[64,2048]{1,0:T(8,128)(2,1)} %broadcast_select_fusion.4), channel_id=1, source_target_pairs={{0,64},{64,0},{1,65},{65,1},{2,66},{66,2},{3,67},{67,3},{4,68},{68... | collective-permute-start | bytes 786440 | tf_op jit(solution)/shard_map/ppermute | solution.py:775
  640.3 31.7 %all-to-all-start.1 = ((bf16[16,5,32,256]{3,2,1,0:T(8,128)(2,1)}), bf16[16,5,32,256]{3,2,1,0:T(8,128)(2,1)S(1)}, u32[]{:S(2)}, u32[]{:S(2)}) async-start(bf16[16,5,32,256]{3,2,1,0:T(8,128)(2,1)} %bitcast.151), calls=%async_computation.1 | async-start | bytes 2621440 | tf_op jit(solution)/shard_map/all_to_all | solution.py:803
  647.1 23.0 %collective-permute-start.109 = (bf16[640,256]{1,0:T(8,128)(2,1)}, bf16[640,256]{1,0:T(8,128)(2,1)S(1)}, u32[]{:S(2)}, u32[]{:S(2)}) collective-permute-start(bf16[640,256]{1,0:T(8,128)(2,1)} %get-tuple-element.217), channel_id=1, source_target_pairs={{0,0},{1,8},{8,1},{9,9},{64,64},{65,72},{72,65},{73,73},{2,2},{3,1... | collective-permute-start | bytes 983048 | tf_op jit(solution)/shard_map/ppermute | solution.py:799
  649.5 22.5 %collective-permute-start.110 = (bf16[640,256]{1,0:T(8,128)(2,1)}, bf16[640,256]{1,0:T(8,128)(2,1)S(1)}, u32[]{:S(2)}, u32[]{:S(2)}) collective-permute-start(bf16[640,256]{1,0:T(8,128)(2,1)} %copy-done.47), channel_id=1, source_target_pairs={{0,64},{1,72},{8,65},{9,73},{64,0},{65,8},{72,1},{73,9},{2,66},{3,... | collective-permute-start | bytes 983048 | tf_op jit(solution)/shard_map/ppermute | solution.py:799
  (144 other events, 1504.6 us)
Sparse Core Ops, SparseCore 0:
  47.2 96.1 all-gather.2
  146.2 95.0 all-gather.4
  403.4 97.3 reduce-scatter.8
  527.6 107.7 reduce-scatter.6

commit v4 on v3

--- a/solution.py
+++ b/solution.py
@@ -30,7 +30,7 @@
 FEED = 3 * TILE + DOWN
 LAYER = ATTN + FEED
 SUMS = LAYER + 2 * VEC
-VMEM = 40 * 1024 * 1024
+VMEM = 34 * 1024 * 1024
 F32 = jnp.float32
 BF16 = jnp.bfloat16
 
@@ -83,8 +83,8 @@
     args = [pltpu.with_memory_space_constraint(a, pltpu.HBM) if k < hbm else a for k, a in enumerate(args)]
     for array in after or ():
         kernel = without(kernel, len(args))
-        args = (*args, array)
-        in_specs.append(pl.BlockSpec(memory_space=pl.ANY))
+        args = (*args, pltpu.with_memory_space_constraint(array, pltpu.HBM))
+        in_specs.append(in_hbm())
     return pl.pallas_call(
         kernel,
         in_specs=in_specs,
@@ -720,11 +720,11 @@
         kernel = without(kernel, 3)
     return pl.pallas_call(
         kernel,
-        in_specs=[in_smem(), in_vmem(), in_vmem()] + [pl.BlockSpec(memory_space=pl.ANY)] * len(after),
+        in_specs=[in_smem(), in_vmem(), in_vmem()] + [in_hbm()] * len(after),
         out_specs=[in_vmem()] * 3,
         out_shape=[shape_of(2, 8, 5, 32, TILE), shape_of(DOWN + TILE, TILE), shape_of(DOWN + TILE, TILE)],
         compiler_params=pltpu.CompilerParams(vmem_limit_bytes=VMEM),
-    )(section, sum_0, sum_1, *after)
+    )(section, sum_0, sum_1, *(pltpu.with_memory_space_constraint(a, pltpu.HBM) for a in after))
 
 
 def unpack_kernel(section_ref, kept_ref, sent_ref, places_ref, values_ref, cut_ref, qkv_ref, gate_ref, out_ref, down_ref, vec_ref):
@@ -785,6 +785,13 @@
     return own + [turned(part, "core", 1) for part in own]
 
 
+def gathered_beside(block, work):
+    own = [turned(block, "x", k) for k in range(1, 4)]
+    *own, work = lax.optimization_barrier((*own, work))
+    own = [block, *own]
+    return own + [turned(part, "core", 1) for part in own], work
+
+
 def summed_parts(after, part_a, part_b):
     first, *rest = added(after, part_a, turned(part_b, "core", 1))
     return [first] + [turned(block, "x", -k) for k, block in enumerate(rest, 1)]
@@ -837,7 +844,7 @@
 def both_layers(qkv_weight, out_weight, gate_up, down_weight):
     section = lax.axis_index("section")
     low, high = packed_rows(out_weight, down_weight)
-    cut = spread(packed((low,), qkv_weight, gate_up).reshape(16, 5, 32, TILE))
+    cut = spread(packed(None, qkv_weight, gate_up).reshape(16, 5, 32, TILE))
     cut = cut.reshape(2, 8, 5, 32, TILE).transpose(0, 2, 1, 3, 4).reshape(2, 5 * TILE, TILE)
     kept = swapped(jnp.where(section == 0, low, high), 0)
     sent = swapped(jnp.where(section == 0, high, low), 1)
@@ -973,13 +980,12 @@
     for layer in (1, 0):
         have = kept[layer]
         if layer == 0:
-            ea, eb, have["gm"], have["dg"], have["du"] = feed_back(
-                (sums_1,), weights[0], gathered_rows(up), have["g"], have["u"]
-            )
+            blocks, sums_1 = gathered_beside(up, sums_1)
+            ea, eb, have["gm"], have["dg"], have["du"] = feed_back((sums_1,), weights[0], blocks, have["g"], have["u"])
         grad, low, have["sums2"] = normed_back(None, up, summed_parts(None, ea, eb), have["values2"], gains, 4 * layer + 2)
-        buffer = feed_sums(have)
+        blocks, buffer = gathered_beside(low, feed_sums(have))
         ea, eb, have["bias_sum"], have["dattn"], have["dq"], have["dk"], have["dv"] = attention_back(
-            (buffer,), weights[layer], gathered_rows(low), have["q"], have["k"], have["v"], *tables
+            (buffer,), weights[layer], blocks, have["q"], have["k"], have["v"], *tables
         )
         parts = summed_parts(None, ea, eb)
         grads_in[layer], up, have["sums1"] = normed_back(None, grad, parts, have["values1"], gains, 4 * layer)

time: 692 us -> 668 us (0.965)
  starting transfers between devices: 156 us -> 144 us
  local copies, waits for them, and re-layouts: 47.8 us -> 40.4 us
    ppermute x107, starting transfers between devices: 130 us -> 118 us  [turned(): return lax.ppermute(block, axis, [(i, (i - step) % n) for i in range(n)])]
    ppermute x107, waiting for transfers between devices: 197 us -> 187 us  [turned(): return lax.ppermute(block, axis, [(i, (i - step) % n) for i in range(n)])]
    all_gather x2, waiting for transfers between devices: 12.9 us -> 22.4 us  [on_device(): full = lax.all_gather(part, SPREAD, axis=0, tiled=True)]
    unnamed x138 -> x108, local copies, waits for them, and re-layouts: 28.6 us -> 25.1 us
  transfers between devices with their start and end apart: 117 -> 117, of which waited for: 58 -> 64; matrix products, arithmetic and copies ran while one was open for 4% -> 4% of each run, Pallas kernels for 11% -> 13%
where the time goes in v4:
time: 668 us; the launch traced here: 659 us
  waiting for transfers between devices  316 us (47%)
  starting transfers between devices  144 us (22%)
  Pallas kernels  133 us (20%)
  local copies, waits for them, and re-layouts  40.4 us (6%)
  between operations  15.2 us (2%)
  other arithmetic  10.2 us (2%)
    ppermute x107, waiting for transfers between devices, turned(): return lax.ppermute(block, axis, [(i, (i - step) % n) for i in range(n)])  187 us
    pallas_call x28, Pallas kernels, call(): pl.pallas_call(kernel, in_specs=in_specs, out_specs=[in_hbm() if to_hbm o...  130 us
    ppermute x107, starting transfers between devices, turned(): return lax.ppermute(block, axis, [(i, (i - step) % n) for i in range(n)])  118 us
    unnamed x6, waiting for transfers between devices  68.7 us
    ppermute x4, waiting for transfers between devices, swapped(): return lax.ppermute(block, ('section', 'y', 'core'), pairs)  37.5 us
    unnamed x108, local copies, waits for them, and re-layouts  25.1 us
    all_gather x2, waiting for transfers between devices, on_device(): full = lax.all_gather(part, SPREAD, axis=0, tiled=True)  22.4 us
    all_to_all x2, starting transfers between devices, spread(): return lax.all_to_all(block, ('section', 'x', 'core'), 0, 0, tiled=True)  15.2 us
  transfers between devices with their start and end apart: 117, of which 64 were waited for; matrix products, arithmetic and copies ran while one was open for 4% of the time, Pallas kernels for 13%

profile of v4, /device:TPU:1, one launch (start us, length us, event | category | flops | bytes accessed | tf_op | source)
XLA Modules:
  0.0 659.1 jit_solution(12390411595863757558)
XLA Ops:
  10.9 8.5 %all-to-all-start = ((bf16[16,5,32,256]{3,2,1,0:T(8,128)(2,1)}), bf16[16,5,32,256]{3,2,1,0:T(8,128)(2,1)S(1)}, u32[]{:S(2)}, u32[]{:S(2)}) async-start(bf16[16,5,32,256]{3,2,1,0:T(8,128)(2,1)} %bitcast.3), calls=%async_computation | async-start | bytes 2621440 | tf_op jit(solution)/shard_map/all_to_all | solution.py:810
  26.2 16.1 %collective-permute-done = bf16[640,256]{1,0:T(8,128)(2,1)S(1)} collective-permute-done((bf16[640,256]{1,0:T(8,128)(2,1)S(1)}, bf16[640,256]{1,0:T(8,128)(2,1)S(1)}, u32[]{:S(2)}, u32[]{:S(2)}) %collective-permute-start) | collective-permute-done | bytes 327712 | tf_op jit(solution)/shard_map/ppermute | solution.py:806
  79.9 4.3 collective-permute-done.14
  105.2 5.2 collective-permute-start.22
  121.3 20.9 %all-gather.3.cloned.1.call-done = bf16[26624,256]{1,0:T(8,128)(2,1)} async-done(((bf16[1664,256]{1,0:T(8,128)(2,1)}), bf16[26624,256]{1,0:T(8,128)(2,1)}) %all-gather.3.cloned.1.call-update) | async-done | bytes 13631504 | tf_op jit(solution)/shard_map/all_gather | solution.py:917
  142.2 9.5 %shard_map.241 = (bf16[256,2048]{1,0:T(8,128)(2,1)S(1)}, bf16[256,2048]{1,0:T(8,128)(2,1)S(1)}, bf16[512,2048]{1,0:T(8,128)(2,1)}, bf16[512,256]{1,0:T(8,128)(2,...) custom-call(bf16[2,8,1664,256]{3,2,1,0:T(8,128)(2,1)} %bitcast.156, ...), custom_call_target="tpu_custom_call" | custom-call | flops 2147483648 | bytes 16777216 | tf_op jit(solution)/shard_map/pallas_call | solution.py:88
  163.9 6.4 collective-permute-done.35.refs_2_
  176.1 8.3 %collective-permute-done.37.refs_1_ = bf16[64,2048]{1,0:T(8,128)(2,1)S(1)} collective-permute-done((bf16[64,2048]{1,0:T(8,128)(2,1)S(1)}, bf16[64,2048]{1,0:T(8,128)(2,1)S(1)}, u32[]{:S(2)}, u32[]{:S(2)}) %collective-permute-start.37) | collective-permute-done | bytes 262176 | tf_op jit(solution)/shard_map/ppermute | solution.py:775
  190.6 11.0 %shard_map.244 = (bf16[256,2048]{1,0:T(8,128)(2,1)S(1)}, bf16[256,2048]{1,0:T(8,128)(2,1)S(1)}, bf16[512,2048]{1,0:T(8,128)(2,1)}, f32[512,768]{1,0:T(8,128)}, f...) custom-call(bf16[2,8,1664,256]{3,2,1,0:T(8,128)(2,1)} %bitcast.157, bf16[64,2048]{1,0:T(8,128)(2,1)S(1)} %get-tuple-element.139.refs_0_, ...), custom_call_target="tpu_custom_call" | custom-call | flops 4831838208 | bytes 16777216 | tf_op jit(solution)/shard_map/pallas_call | solution.py:88
  207.4 11.8 %collective-permute-done.45.refs_1_ = bf16[64,2048]{1,0:T(8,128)(2,1)S(1)} collective-permute-done((bf16[64,2048]{1,0:T(8,128)(2,1)S(1)}, bf16[64,2048]{1,0:T(8,128)(2,1)S(1)}, u32[]{:S(2)}, u32[]{:S(2)}) %collective-permute-start.45) | collective-permute-done | bytes 262176 | tf_op jit(solution)/shard_map/ppermute | solution.py:775
  224.6 4.8 collective-permute-done.48.refs_1_
  229.4 5.4 collective-permute-start.52
  239.9 9.5 %shard_map.247 = (bf16[256,2048]{1,0:T(8,128)(2,1)S(1)}, bf16[256,2048]{1,0:T(8,128)(2,1)S(1)}, bf16[512,2048]{1,0:T(8,128)(2,1)}, bf16[512,256]{1,0:T(8,128)(2,...) custom-call(bf16[2,8,1664,256]{3,2,1,0:T(8,128)(2,1)} %bitcast.160, ...), custom_call_target="tpu_custom_call" | custom-call | flops 2147483648 | bytes 16777216 | tf_op jit(solution)/shard_map/pallas_call | solution.py:88
  261.5 6.5 collective-permute-done.57.refs_2_
  273.8 8.1 %collective-permute-done.59.refs_9_ = bf16[64,2048]{1,0:T(8,128)(2,1)S(1)} collective-permute-done((bf16[64,2048]{1,0:T(8,128)(2,1)S(1)}, bf16[64,2048]{1,0:T(8,128)(2,1)S(1)}, u32[]{:S(2)}, u32[]{:S(2)}) %collective-permute-start.59) | collective-permute-done | bytes 262176 | tf_op jit(solution)/shard_map/ppermute | solution.py:775
  288.5 17.6 %shard_map.250 = (bf16[256,2048]{1,0:T(8,128)(2,1)S(1)}, bf16[256,2048]{1,0:T(8,128)(2,1)S(1)}, bf16[256,2048]{1,0:T(8,128)(2,1)S(1)}, bf16[256,2048]{1,0:T(8,12...) custom-call(bf16[2,8,1664,256]{3,2,1,0:T(8,128)(2,1)} %bitcast.161, ...), custom_call_target="tpu_custom_call" | custom-call | flops 9663676416 | bytes 16777216 | tf_op jit(solution)/shard_map/pallas_call | solution.py:88
  312.8 11.7 %collective-permute-done.68.refs_1_ = bf16[64,2048]{1,0:T(8,128)(2,1)S(1)} collective-permute-done((bf16[64,2048]{1,0:T(8,128)(2,1)S(1)}, bf16[64,2048]{1,0:T(8,128)(2,1)S(1)}, u32[]{:S(2)}, u32[]{:S(2)}) %collective-permute-start.68) | collective-permute-done | bytes 262176 | tf_op jit(solution)/shard_map/ppermute | solution.py:775
  331.4 10.9 %shard_map.253.refs_14_.refs_0_ = bf16[2,8,1696,256]{3,2,1,0:T(8,128)(2,1)} custom-call(bf16[512,2048]{1,0:T(8,128)(2,1)} %get-tuple-element.169.refs_0_, bf16[512,768]{1,0:T(8,128)(2,1)} %get-tuple-element.170.refs_1_, bf16[512,768]{1,0:T(8,128)(2,1)} %get-tuple-element.171.refs_2_, bf16[512,768]{1,0:T(8,128)(2,1)} %get-tuple-element.172.refs_3_, ...), custom_call_target="tpu_custom_call" | custom-call | flops 4831838208 | bytes 16777216 | tf_op jit(solution)/shard_map/pallas_call | solution.py:88
  346.8 9.4 %shard_map.254 = (bf16[256,2048]{1,0:T(8,128)(2,1)S(1)}, bf16[256,2048]{1,0:T(8,128)(2,1)S(1)}, f32[8,256]{1,0:T(8,128)S(1)}, bf16[512,2048]{1,0:T(8,128)(2,1)},...) custom-call(bf16[2,8,1664,256]{3,2,1,0:T(8,128)(2,1)} %bitcast.162, ...), custom_call_target="tpu_custom_call" | custom-call | flops 2147483648 | bytes 16777216 | tf_op jit(solution)/shard_map/pallas_call | solution.py:88
  364.3 6.2 collective-permute-done.79.refs_1_
  386.3 7.1 %shard_map.257.refs_11_ = bf16[2,8,1696,256]{3,2,1,0:T(8,128)(2,1)} custom-call(bf16[2,8,1696,256]{3,2,1,0:T(8,128)(2,1)} %shard_map.253.refs_14_.refs_0_, bf16[512,2048]{1,0:T(8,128)(2,1)} %get-tuple-element.188.refs_1_, bf16[512,2048]{1,0:T(8,128)(2,1)} %get-tuple-element.189.refs_2_, ...), custom_call_target="tpu_custom_call", output_to_operand_aliasing={{}: (0, {})} | custom-call | flops 2147483648 | bytes 16777216 | tf_op jit(solution)/shard_map/pallas_call | solution.py:88
  403.6 13.0 %shard_map.258 = (bf16[256,2048]{1,0:T(8,128)(2,1)S(1)}, bf16[256,2048]{1,0:T(8,128)(2,1)S(1)}, bf16[512,2048]{1,0:T(8,128)(2,1)}, bf16[512,768]{1,0:T(8,128)(2,1)}, bf16[512,768]{1,0:T(8,128)(2,1)}) custom-call(bf16[2,8,1664,256]{3,2,1,0:T(8,128)(2,1)} %bitcast.158, f32[512,768]{1,0:T(8,128)} %get-tuple-element.186.refs_1_, ...), custom_call_target="tpu_custom_call" | custom-call | flops 4831838208 | bytes 16777216 | tf_op jit(solution)/shard_map/pallas_call | solution.py:88
  422.8 11.8 %collective-permute-done.90.refs_1_ = bf16[64,2048]{1,0:T(8,128)(2,1)S(1)} collective-permute-done((bf16[64,2048]{1,0:T(8,128)(2,1)S(1)}, bf16[64,2048]{1,0:T(8,128)(2,1)S(1)}, u32[]{:S(2)}, u32[]{:S(2)}) %collective-permute-start.90) | collective-permute-done | bytes 262176 | tf_op jit(solution)/shard_map/ppermute | solution.py:775
  441.9 11.4 %shard_map.261.refs_14_.refs_0_ = bf16[2,8,1696,256]{3,2,1,0:T(8,128)(2,1)} custom-call(bf16[512,2048]{1,0:T(8,128)(2,1)} %get-tuple-element.207.refs_0_, bf16[512,768]{1,0:T(8,128)(2,1)} %get-tuple-element.208.refs_1_, bf16[512,768]{1,0:T(8,128)(2,1)} %get-tuple-element.209.refs_2_, bf16[512,768]{1,0:T(8,128)(2,1)} %get-tuple-element.210.refs_3_, ...), custom_call_target="tpu_custom_call" | custom-call | flops 4831838208 | bytes 16777216 | tf_op jit(solution)/shard_map/pallas_call | solution.py:88
  461.0 9.8 %shard_map.262 = (bf16[256,2048]{1,0:T(8,128)(2,1)S(1)}, bf16[256,2048]{1,0:T(8,128)(2,1)S(1)}, f32[8,256]{1,0:T(8,128)S(1)}, bf16[512,2048]{1,0:T(8,128)(2,1)},...) custom-call(bf16[2,8,1664,256]{3,2,1,0:T(8,128)(2,1)} %bitcast.159, ...), custom_call_target="tpu_custom_call" | custom-call | flops 2147483648 | bytes 16777216 | tf_op jit(solution)/shard_map/pallas_call | solution.py:88
  478.7 11.3 %collective-permute-done.101.refs_1_ = bf16[64,2048]{1,0:T(8,128)(2,1)S(1)} collective-permute-done((bf16[64,2048]{1,0:T(8,128)(2,1)}, bf16[64,2048]{1,0:T(8,128)(2,1)S(1)}, u32[]{:S(2)}, u32[]{:S(2)}) %collective-permute-start.101) | collective-permute-done | bytes 262176 | tf_op jit(solution)/shard_map/ppermute | solution.py:775
  497.1 7.2 %shard_map.265.refs_2_ = bf16[2,8,1696,256]{3,2,1,0:T(8,128)(2,1)} custom-call(bf16[2,8,1696,256]{3,2,1,0:T(8,128)(2,1)} %shard_map.261.refs_14_.refs_0_, bf16[512,2048]{1,0:T(8,128)(2,1)} %get-tuple-element.214.refs_1_, bf16[512,2048]{1,0:T(8,128)(2,1)} %get-tuple-element.221.refs_2_, ...), custom_call_target="tpu_custom_call", output_to_operand_aliasing={{}: (0, {})} | custom-call | flops 2147483648 | bytes 16777216 | tf_op jit(solution)/shard_map/pallas_call | solution.py:88
  517.1 6.3 collective-permute-done.105
  531.5 8.4 %collective-permute-done.107 = bf16[64,2048]{1,0:T(8,128)(2,1)} collective-permute-done((bf16[64,2048]{1,0:T(8,128)(2,1)}, bf16[64,2048]{1,0:T(8,128)(2,1)}, u32[]{:S(2)}, u32[]{:S(2)}) %collective-permute-start.107) | collective-permute-done | bytes 262176 | tf_op jit(solution)/shard_map/ppermute | solution.py:775
  543.5 68.6 %reduce-scatter.7.cloned.1.call-done = bf16[1,1696,256]{2,1,0:T(8,128)(2,1)} async-done(((bf16[16,1696,256]{2,1,0:T(8,128)(2,1)}), bf16[1,1696,256]{2,1,0:T(8,128)(2,1)}) %reduce-scatter.7.cloned.1.call-update) | async-done | bytes 868368
  617.1 6.8 %all-to-all-start.1 = ((bf16[16,5,32,256]{3,2,1,0:T(8,128)(2,1)}), bf16[16,5,32,256]{3,2,1,0:T(8,128)(2,1)S(1)}, u32[]{:S(2)}, u32[]{:S(2)}) async-start(bf16[16,5,32,256]{3,2,1,0:T(8,128)(2,1)} %bitcast.151), calls=%async_computation.1 | async-start | bytes 2621440 | tf_op jit(solution)/shard_map/all_to_all | solution.py:810
  629.3 17.5 %collective-permute-done.109.kept_ref = bf16[640,256]{1,0:T(8,128)(2,1)S(1)} collective-permute-done((bf16[640,256]{1,0:T(8,128)(2,1)}, bf16[640,256]{1,0:T(8,128)(2,1)S(1)}, u32[]{:S(2)}, u32[]{:S(2)}) %collective-permute-start.109) | collective-permute-done | bytes 327712 | tf_op jit(solution)/shard_map/ppermute | solution.py:806
  (478 shorter events, 272.6 us)
Async XLA Ops:
  10.9 33.5 %all-to-all-start = ((bf16[16,5,32,256]{3,2,1,0:T(8,128)(2,1)}), bf16[16,5,32,256]{3,2,1,0:T(8,128)(2,1)S(1)}, u32[]{:S(2)}, u32[]{:S(2)}) async-start(bf16[16,5,32,256]{3,2,1,0:T(8,128)(2,1)} %bitcast.3), calls=%async_computation | async-start | bytes 2621440 | tf_op jit(solution)/shard_map/all_to_all | solution.py:810
  19.4 122.8 %all-gather.3.cloned.1.call-start = ((), (), s32[]{:S(2)}) async-start(), calls=%async_computation.4 | async-start | bytes 14483456 | tf_op jit(solution)/shard_map/all_gather | solution.py:917
  20.8 21.5 %collective-permute-start = (bf16[640,256]{1,0:T(8,128)(2,1)S(1)}, bf16[640,256]{1,0:T(8,128)(2,1)S(1)}, u32[]{:S(2)}, u32[]{:S(2)}) collective-permute-start(bf16[640,256]{1,0:T(8,128)(2,1)S(1)} %get-tuple-element.276), channel_id=1, source_target_pairs={{0,0},{1,8},{8,1},{9,9},{64,64},{65,72},{72,65},{73,73},{2,2},{3,1... | collective-permute-start | bytes 983048 | tf_op jit(solution)/shard_map/ppermute | solution.py:806
  23.1 21.2 %collective-permute-start.1 = (bf16[640,256]{1,0:T(8,128)(2,1)S(1)}, bf16[640,256]{1,0:T(8,128)(2,1)S(1)}, u32[]{:S(2)}, u32[]{:S(2)}) collective-permute-start(bf16[640,256]{1,0:T(8,128)(2,1)S(1)} %get-tuple-element.275), channel_id=1, source_target_pairs={{0,64},{1,72},{8,65},{9,73},{64,0},{65,8},{72,1},{73,9},{2,66},{3,... | collective-permute-start | bytes 983048 | tf_op jit(solution)/shard_map/ppermute | solution.py:806
  45.8 194.1 %all-gather.5.cloned.1.call-start = ((), (), s32[]{:S(2)}) async-start(), calls=%async_computation.5 | async-start | bytes 14483456 | tf_op jit(solution)/shard_map/all_gather | solution.py:917
  47.2 496.3 %reduce-scatter.9.cloned.1.call-start = ((), (), s32[]{:S(2)}) async-start(), calls=%async_computation.7 | async-start | bytes 14761984
  47.3 25.3 %collective-permute-start.2 = (s32[1,64]{1,0:T(1,128)S(1)}, s32[1,64]{1,0:T(1,128)S(1)}, u32[]{:S(2)}, u32[]{:S(2)}) collective-permute-start(s32[1,64]{1,0:T(1,128)S(1)} %reshape.258), channel_id=1, source_target_pairs={{0,48},{16,0},{32,16},{48,32},{1,49},{17,1},{33,17},{49,33},{2,50}... | collective-permute-start | bytes 776 | tf_op jit(solution)/shard_map/ppermute | solution.py:775
  49.7 26.0 %collective-permute-start.3 = (s32[1,64]{1,0:T(1,128)S(1)}, s32[1,64]{1,0:T(1,128)S(1)}, u32[]{:S(2)}, u32[]{:S(2)}) collective-permute-start(s32[1,64]{1,0:T(1,128)S(1)} %reshape.258), channel_id=1, source_target_pairs={{0,32},{16,48},{32,0},{48,16},{1,33},{17,49},{33,1},{49,17},{2,34}... | collective-permute-start | bytes 776 | tf_op jit(solution)/shard_map/ppermute | solution.py:775
  50.3 25.6 %collective-permute-start.4 = (s32[1,64]{1,0:T(1,128)S(1)}, s32[1,64]{1,0:T(1,128)S(1)}, u32[]{:S(2)}, u32[]{:S(2)}) collective-permute-start(s32[1,64]{1,0:T(1,128)S(1)} %reshape.258), channel_id=1, source_target_pairs={{0,16},{16,32},{32,48},{48,0},{1,17},{17,33},{33,49},{49,1},{2,18}... | collective-permute-start | bytes 776 | tf_op jit(solution)/shard_map/ppermute | solution.py:775
  50.9 25.3 %collective-permute-start.5 = (s32[1,64]{1,0:T(1,128)S(1)}, s32[1,64]{1,0:T(1,128)S(1)}, u32[]{:S(2)}, u32[]{:S(2)}) collective-permute-start(s32[1,64]{1,0:T(1,128)S(1)} %reshape.258), channel_id=1, source_target_pairs={{0,1},{1,0},{2,3},{3,2},{4,5},{5,4},{6,7},{7,6},{8,9},{9,8},{10,11... | collective-permute-start | bytes 776 | tf_op jit(solution)/shard_map/ppermute | solution.py:775
  76.3 27.1 %collective-permute-start.26 = (bf16[64,2048]{1,0:T(8,128)(2,1)S(1)}, bf16[64,2048]{1,0:T(8,128)(2,1)}, u32[]{:S(2)}, u32[]{:S(2)}) collective-permute-start(bf16[64,2048]{1,0:T(8,128)(2,1)S(1)} %reshape.266.refs_12_.refs_0_.up_ref), channel_id=1, source_target_pairs={{0,48},{16,0},{32,16},{48,32},{1,49},{17,1},{33,17},{49,33},{2,50}... | collective-permute-start | bytes 786440 | tf_op jit(solution)/shard_map/ppermute | solution.py:775
  78.0 27.2 %collective-permute-start.27 = (bf16[64,2048]{1,0:T(8,128)(2,1)S(1)}, bf16[64,2048]{1,0:T(8,128)(2,1)}, u32[]{:S(2)}, u32[]{:S(2)}) collective-permute-start(bf16[64,2048]{1,0:T(8,128)(2,1)S(1)} %reshape.266.refs_12_.refs_0_.up_ref), channel_id=1, source_target_pairs={{0,32},{16,48},{32,0},{48,16},{1,33},{17,49},{33,1},{49,17},{2,34}... | collective-permute-start | bytes 786440 | tf_op jit(solution)/shard_map/ppermute | solution.py:775
  78.0 27.2 %collective-permute-start.28 = (bf16[64,2048]{1,0:T(8,128)(2,1)S(1)}, bf16[64,2048]{1,0:T(8,128)(2,1)}, u32[]{:S(2)}, u32[]{:S(2)}) collective-permute-start(bf16[64,2048]{1,0:T(8,128)(2,1)S(1)} %reshape.266.refs_12_.refs_0_.up_ref), channel_id=1, source_target_pairs={{0,16},{16,32},{32,48},{48,0},{1,17},{17,33},{33,49},{49,1},{2,18}... | collective-permute-start | bytes 786440 | tf_op jit(solution)/shard_map/ppermute | solution.py:775
  78.9 31.5 %collective-permute-start.29 = (bf16[64,2048]{1,0:T(8,128)(2,1)S(1)}, bf16[64,2048]{1,0:T(8,128)(2,1)S(1)}, u32[]{:S(2)}, u32[]{:S(2)}) collective-permute-start(bf16[64,2048]{1,0:T(8,128)(2,1)S(1)} %reshape.266.refs_12_.refs_0_.up_ref), channel_id=1, source_target_pairs={{0,1},{1,0},{2,3},{3,2},{4,5},{5,4},{6,7},{7,6},{8,9},{9,8},{10,11... | collective-permute-start | bytes 786440 | tf_op jit(solution)/shard_map/ppermute | solution.py:775
  173.8 15.0 %collective-permute-start.39 = (bf16[64,2048]{1,0:T(8,128)(2,1)S(1)}, bf16[64,2048]{1,0:T(8,128)(2,1)S(1)}, u32[]{:S(2)}, u32[]{:S(2)}) collective-permute-start(bf16[64,2048]{1,0:T(8,128)(2,1)S(1)} %get-tuple-element.139.refs_0_), channel_id=1, source_target_pairs={{0,16},{16,32},{32,48},{48,0},{1,17},{17,33},{33,49},{49,1},{2,18}... | collective-permute-start | bytes 786440 | tf_op jit(solution)/shard_map/ppermute | solution.py:775
  174.3 15.2 %collective-permute-start.40 = (bf16[64,2048]{1,0:T(8,128)(2,1)S(1)}, bf16[64,2048]{1,0:T(8,128)(2,1)S(1)}, u32[]{:S(2)}, u32[]{:S(2)}) collective-permute-start(bf16[64,2048]{1,0:T(8,128)(2,1)S(1)} %get-tuple-element.139.refs_0_), channel_id=1, source_target_pairs={{0,1},{1,0},{2,3},{3,2},{4,5},{5,4},{6,7},{7,6},{8,9},{9,8},{10,11... | collective-permute-start | bytes 786440 | tf_op jit(solution)/shard_map/ppermute | solution.py:775
  223.4 16.5 %collective-permute-start.51 = (bf16[64,2048]{1,0:T(8,128)(2,1)S(1)}, bf16[64,2048]{1,0:T(8,128)(2,1)S(1)}, u32[]{:S(2)}, u32[]{:S(2)}) collective-permute-start(bf16[64,2048]{1,0:T(8,128)(2,1)S(1)} %get-tuple-element.147.refs_0_), channel_id=1, source_target_pairs={{0,1},{1,0},{2,3},{3,2},{4,5},{5,4},{6,7},{7,6},{8,9},{9,8},{10,11... | collective-permute-start | bytes 786440 | tf_op jit(solution)/shard_map/ppermute | solution.py:775
  271.4 14.9 %collective-permute-start.61 = (bf16[64,2048]{1,0:T(8,128)(2,1)S(1)}, bf16[64,2048]{1,0:T(8,128)(2,1)S(1)}, u32[]{:S(2)}, u32[]{:S(2)}) collective-permute-start(bf16[64,2048]{1,0:T(8,128)(2,1)S(1)} %get-tuple-element.155.refs_8_), channel_id=1, source_target_pairs={{0,16},{16,32},{32,48},{48,0},{1,17},{17,33},{33,49},{49,1},{2,18}... | collective-permute-start | bytes 786440 | tf_op jit(solution)/shard_map/ppermute | solution.py:775
  271.9 15.4 %collective-permute-start.62 = (bf16[64,2048]{1,0:T(8,128)(2,1)S(1)}, bf16[64,2048]{1,0:T(8,128)(2,1)S(1)}, u32[]{:S(2)}, u32[]{:S(2)}) collective-permute-start(bf16[64,2048]{1,0:T(8,128)(2,1)S(1)} %get-tuple-element.155.refs_8_), channel_id=1, source_target_pairs={{0,1},{1,0},{2,3},{3,2},{4,5},{5,4},{6,7},{7,6},{8,9},{9,8},{10,11... | collective-permute-start | bytes 786440 | tf_op jit(solution)/shard_map/ppermute | solution.py:775
  326.3 16.1 %collective-permute-start.71 = (bf16[64,2048]{1,0:T(8,128)(2,1)S(1)}, bf16[64,2048]{1,0:T(8,128)(2,1)S(1)}, u32[]{:S(2)}, u32[]{:S(2)}) collective-permute-start(bf16[64,2048]{1,0:T(8,128)(2,1)S(1)} %get-tuple-element.168.refs_6_), channel_id=1, source_target_pairs={{0,48},{16,0},{32,16},{48,32},{1,49},{17,1},{33,17},{49,33},{2,50}... | collective-permute-start | bytes 786440 | tf_op jit(solution)/shard_map/ppermute | solution.py:775
  329.6 15.6 %collective-permute-start.74 = (bf16[64,2048]{1,0:T(8,128)(2,1)S(1)}, bf16[64,2048]{1,0:T(8,128)(2,1)}, u32[]{:S(2)}, u32[]{:S(2)}) collective-permute-start(bf16[64,2048]{1,0:T(8,128)(2,1)S(1)} %get-tuple-element.168.refs_6_), channel_id=1, source_target_pairs={{0,1},{1,0},{2,3},{3,2},{4,5},{5,4},{6,7},{7,6},{8,9},{9,8},{10,11... | collective-permute-start | bytes 786440 | tf_op jit(solution)/shard_map/ppermute | solution.py:775
  400.2 211.9 %reduce-scatter.7.cloned.1.call-start = ((), (), s32[]{:S(2)}) async-start(), calls=%async_computation.6 | async-start | bytes 14761984
  419.6 14.9 %collective-permute-start.90 = (bf16[64,2048]{1,0:T(8,128)(2,1)S(1)}, bf16[64,2048]{1,0:T(8,128)(2,1)S(1)}, u32[]{:S(2)}, u32[]{:S(2)}) collective-permute-start(bf16[64,2048]{1,0:T(8,128)(2,1)S(1)} %get-tuple-element.203), channel_id=1, source_target_pairs={{0,16},{16,32},{32,48},{48,0},{1,17},{17,33},{33,49},{49,1},{2,18}... | collective-permute-start | bytes 786440 | tf_op jit(solution)/shard_map/ppermute | solution.py:775
  437.0 16.3 %collective-permute-start.93 = (bf16[64,2048]{1,0:T(8,128)(2,1)}, bf16[64,2048]{1,0:T(8,128)(2,1)S(1)}, u32[]{:S(2)}, u32[]{:S(2)}) collective-permute-start(bf16[64,2048]{1,0:T(8,128)(2,1)} %get-tuple-element.206.refs_6_), channel_id=1, source_target_pairs={{0,48},{16,0},{32,16},{48,32},{1,49},{17,1},{33,17},{49,33},{2,50}... | collective-permute-start | bytes 786440 | tf_op jit(solution)/shard_map/ppermute | solution.py:775
  439.7 15.2 %collective-permute-start.95 = (bf16[64,2048]{1,0:T(8,128)(2,1)}, bf16[64,2048]{1,0:T(8,128)(2,1)}, u32[]{:S(2)}, u32[]{:S(2)}) collective-permute-start(bf16[64,2048]{1,0:T(8,128)(2,1)} %get-tuple-element.206.refs_6_), channel_id=1, source_target_pairs={{0,16},{16,32},{32,48},{48,0},{1,17},{17,33},{33,49},{49,1},{2,18}... | collective-permute-start | bytes 786440 | tf_op jit(solution)/shard_map/ppermute | solution.py:775
  440.2 17.5 %collective-permute-start.96 = (bf16[64,2048]{1,0:T(8,128)(2,1)}, bf16[64,2048]{1,0:T(8,128)(2,1)}, u32[]{:S(2)}, u32[]{:S(2)}) collective-permute-start(bf16[64,2048]{1,0:T(8,128)(2,1)} %get-tuple-element.206.refs_6_), channel_id=1, source_target_pairs={{0,1},{1,0},{2,3},{3,2},{4,5},{5,4},{6,7},{7,6},{8,9},{9,8},{10,11... | collective-permute-start | bytes 786440 | tf_op jit(solution)/shard_map/ppermute | solution.py:775
  508.5 14.9 %collective-permute-start.105 = (bf16[64,2048]{1,0:T(8,128)(2,1)S(1)}, bf16[64,2048]{1,0:T(8,128)(2,1)S(1)}, u32[]{:S(2)}, u32[]{:S(2)}) collective-permute-start(bf16[64,2048]{1,0:T(8,128)(2,1)S(1)} %get-tuple-element.237), channel_id=1, source_target_pairs={{0,32},{16,48},{32,0},{48,16},{1,33},{17,49},{33,1},{49,17},{2,34}... | collective-permute-start | bytes 786440 | tf_op jit(solution)/shard_map/ppermute | solution.py:775
  512.5 15.5 %collective-permute-start.108 = (bf16[64,2048]{1,0:T(8,128)(2,1)}, bf16[64,2048]{1,0:T(8,128)(2,1)S(1)}, u32[]{:S(2)}, u32[]{:S(2)}) collective-permute-start(bf16[64,2048]{1,0:T(8,128)(2,1)} %fusion.4), channel_id=1, source_target_pairs={{0,64},{64,0},{1,65},{65,1},{2,66},{66,2},{3,67},{67,3},{4,68},{68... | collective-permute-start | bytes 786440 | tf_op jit(solution)/shard_map/ppermute | solution.py:775
  524.3 15.6 %collective-permute-start.107 = (bf16[64,2048]{1,0:T(8,128)(2,1)}, bf16[64,2048]{1,0:T(8,128)(2,1)}, u32[]{:S(2)}, u32[]{:S(2)}) collective-permute-start(bf16[64,2048]{1,0:T(8,128)(2,1)} %broadcast_select_fusion.4), channel_id=1, source_target_pairs={{0,64},{64,0},{1,65},{65,1},{2,66},{66,2},{3,67},{67,3},{4,68},{68... | collective-permute-start | bytes 786440 | tf_op jit(solution)/shard_map/ppermute | solution.py:775
  617.1 31.6 %all-to-all-start.1 = ((bf16[16,5,32,256]{3,2,1,0:T(8,128)(2,1)}), bf16[16,5,32,256]{3,2,1,0:T(8,128)(2,1)S(1)}, u32[]{:S(2)}, u32[]{:S(2)}) async-start(bf16[16,5,32,256]{3,2,1,0:T(8,128)(2,1)} %bitcast.151), calls=%async_computation.1 | async-start | bytes 2621440 | tf_op jit(solution)/shard_map/all_to_all | solution.py:810
  623.8 23.0 %collective-permute-start.109 = (bf16[640,256]{1,0:T(8,128)(2,1)}, bf16[640,256]{1,0:T(8,128)(2,1)S(1)}, u32[]{:S(2)}, u32[]{:S(2)}) collective-permute-start(bf16[640,256]{1,0:T(8,128)(2,1)} %get-tuple-element.241), channel_id=1, source_target_pairs={{0,0},{1,8},{8,1},{9,9},{64,64},{65,72},{72,65},{73,73},{2,2},{3,1... | collective-permute-start | bytes 983048 | tf_op jit(solution)/shard_map/ppermute | solution.py:806
  626.2 22.5 %collective-permute-start.110 = (bf16[640,256]{1,0:T(8,128)(2,1)}, bf16[640,256]{1,0:T(8,128)(2,1)S(1)}, u32[]{:S(2)}, u32[]{:S(2)}) collective-permute-start(bf16[640,256]{1,0:T(8,128)(2,1)} %copy-done.32), channel_id=1, source_target_pairs={{0,64},{1,72},{8,65},{9,73},{64,0},{65,8},{72,1},{73,9},{2,66},{3,... | collective-permute-start | bytes 983048 | tf_op jit(solution)/shard_map/ppermute | solution.py:806
  (128 other events, 974.3 us)
Sparse Core Ops, SparseCore 0:
  46.0 96.1 all-gather.2
  145.0 94.9 all-gather.4
  400.3 96.5 reduce-scatter.8
  504.4 107.6 reduce-scatter.6
